TPU v7x, 32 devices: a whole 2x2x4 slice. The times are simulated.
32 devices in a mesh: dp: 16 (over z, y, x), fsdp: 2 (over core).
Axes of the slice: x: 2, y: 2, z: 4, core: 2. Of those that a mesh axis runs over, the one named last changes fastest.
Arguments:
- points: float32 [3, 524288], P(None, ('dp', 'fsdp')), may hold values from -6 to 6
- point_count: int32 [16384], P(('dp', 'fsdp')), may hold values from 1 to 32, as said below
- centre_slot: int32 [16384], P(('dp', 'fsdp')), may hold values from 0 to 31, as said below
- cloud_length: int32 [256], P(('dp', 'fsdp')), may hold values from 32 to 64
- cotangent: float32 [16384, 384], P(('dp', 'fsdp')), may hold values from -6 to 6
- point_master: float32 [493824], P(('dp', 'fsdp')), may hold values from -2 to 2
- block_master: float32 [1773312], P(('dp', 'fsdp')), may hold values from -2 to 2
- point_first: float32 [493824], P(('dp', 'fsdp')), may hold values from -362.03867 to 362.03867
- block_first: float32 [1773312], P(('dp', 'fsdp')), may hold values from -64 to 64
- point_second: float32 [493824], P(('dp', 'fsdp')), may hold values from 104.8576 to 524288
- block_second: float32 [1773312], P(('dp', 'fsdp')), may hold values from 3.2768 to 16384
Outputs:
- tokens_out: float32 [16384, 384], P(('dp', 'fsdp'))
- point_grad: float32 [3, 524288], P(None, ('dp', 'fsdp'))
- point_master_new: float32 [493824], P(('dp', 'fsdp'))
- block_master_new: float32 [1773312], P(('dp', 'fsdp'))
- point_first_new: float32 [493824], P(('dp', 'fsdp'))
- block_first_new: float32 [1773312], P(('dp', 'fsdp'))
- point_second_new: float32 [493824], P(('dp', 'fsdp'))
- block_second_new: float32 [1773312], P(('dp', 'fsdp'))
- point_copy: bfloat16 [493824], P(('dp', 'fsdp'))
- block_copy: bfloat16 [1773312], P(('dp', 'fsdp'))
- block_small_grad: float32 [3840], P(('dp', 'fsdp'))
Inputs may be any that keep to these rules, and one draw needn't show every extreme that they name: Patch t holds its points in slots 0 to point_count[t] - 1; its other slots are padding. `centre_slot`: the centre slot of a patch is one of its points, below its point_count.
All inputs are finite; a program needn't handle non-finite values.
Results may differ from a plain program's by a relative error of at most 0.025.
Values may be sent and summed in bfloat16 or wider, within the bound.
A program may use at most 256 MiB of HBM per device.

v0:
```python
import math

import jax
import jax.numpy as jnp
from jax import lax
from jax.sharding import PartitionSpec as P

C1 = 128
C2 = 256
C3 = 512
D = 384
HEADS = 6
HEAD_DIM = 64
FF = 1536
GROUP = 32
PATCHES = 64
STEP = 10


EPS_NORM = 1e-05
BETA_ONE = 0.9
BETA_TWO = 0.95
ADAM_EPS = 1e-08
DECAY_RATE = 0.05
NEG_FILL = -1e30
HIGH = lax.Precision.HIGHEST


def point_layout():
    return [
        [
            ("w1", (3, C1), 3.0 ** (-0.5), 0.1),
            ("bn1_gain", (C1,), 0.0, 0.2),
            ("bn1_shift", (C1,), -1.0, 0.2),
            ("b2", (C2,), -1.0, 0.2),
            ("bn3_gain", (C3,), 0.0, 0.3),
            ("bn3_shift", (C3,), -1.0, 0.3),
            ("b4", (D,), -1.0, 1.5),
        ],
        [("w2", (C1, C2), C1 ** (-0.5), 0.1)],
        [("w3", (2 * C2, C3), (2 * C2) ** (-0.5), 0.15)],
        [("w4", (C3, D), C3 ** (-0.5), 0.5)],
    ]


def block_layout():
    return [
        [
            ("ln1_gain", (D,), 0.0, 0.5),
            ("ln1_shift", (D,), -1.0, 0.5),
            ("bo", (D,), -1.0, 1.2),
            ("ln2_gain", (D,), 0.0, 0.7),
            ("ln2_shift", (D,), -1.0, 0.7),
            ("bf1", (FF,), -1.0, 0.3),
            ("bf2", (D,), -1.0, 1.0),
        ],
        [("wqkv", (D, 3 * D), D ** (-0.5), 0.3)],
        [("wo", (D, D), 3.0 * D ** (-0.5), 0.4)],
        [("wf1", (D, FF), D ** (-0.5), 0.3)],
        [("wf2", (FF, D), FF ** (-0.5), 0.65)],
    ]


def rate_for(spread):
    return 2.0 * spread if spread > 0.0 else 0.5 if spread == 0.0 else 0.6


def decay_for(spread):
    return DECAY_RATE if spread > 0.0 else 0.0


def segment_lengths(layout, devices):
    lengths_out = []
    for segment in layout:
        used_len = sum((math.prod(entry_item[1]) for entry_item in segment))
        lengths_out.append(-(-used_len // devices) * devices)
    return lengths_out


def split_shard(shard_vec, layout, devices):
    pieces = []
    offset = 0
    for seg_len in segment_lengths(layout, devices):
        piece_len = seg_len // devices
        pieces.append(shard_vec[offset : offset + piece_len])
        offset += piece_len
    return pieces


def unpack(seg_list, layout):
    weight_table = {}
    for seg_values, segment in zip(seg_list, layout):
        offset = 0
        for entry_label, entry_dims, spread, factor in segment:
            extent = math.prod(entry_dims)
            weight_table[entry_label] = seg_values[offset : offset + extent].reshape(entry_dims)
            offset += extent
    return weight_table


def pack(grad_table, layout, devices):
    packed = []
    for segment, seg_len in zip(layout, segment_lengths(layout, devices)):
        piece_list = [grad_table[entry_item[0]].reshape(-1) for entry_item in segment]
        used_len = sum((math.prod(entry_item[1]) for entry_item in segment))
        piece_list.append(jnp.zeros((seg_len - used_len,), jnp.float32))
        packed.append(jnp.concatenate(piece_list))
    return packed


def shard_rates(layout, devices, own_rank):
    rate_parts = []
    decay_parts = []
    for segment, seg_len in zip(layout, segment_lengths(layout, devices)):
        piece_len = seg_len // devices
        position = own_rank * piece_len + jnp.arange(piece_len, dtype=jnp.int32)
        seg_rates = jnp.zeros((piece_len,), jnp.float32)
        seg_decays = jnp.zeros((piece_len,), jnp.float32)
        offset = 0
        for entry_label, entry_dims, spread, factor in segment:
            extent = math.prod(entry_dims)
            inside = (position >= offset) & (position < offset + extent)
            seg_rates = jnp.where(inside, rate_for(spread), seg_rates)
            seg_decays = jnp.where(inside, decay_for(spread), seg_decays)
            offset += extent
        rate_parts.append(seg_rates)
        decay_parts.append(seg_decays)
    return (jnp.concatenate(rate_parts), jnp.concatenate(decay_parts))


def as_float(weight_table, entry_label):
    return weight_table[entry_label].astype(jnp.float32)


def cloud_geometry(cloud_points, cloud_counts, cloud_centres):
    grid_points = cloud_points.reshape(3, -1, GROUP)
    slot_ids = jnp.arange(GROUP, dtype=jnp.int32)
    picker = (slot_ids[None, :] == cloud_centres[:, None]).astype(jnp.float32)
    centre = jnp.sum(grid_points * picker[None], axis=2)
    relative = (grid_points - centre[:, :, None]).reshape(3, -1)
    valid_mask = (slot_ids[None, :] < cloud_counts[:, None]).astype(jnp.float32).reshape(-1)
    return (relative, valid_mask, picker)


def slot_share(valid_mask, cloud_counts):
    return valid_mask.reshape(-1, GROUP) / cloud_counts[:, None].astype(jnp.float32)


def pool_mean(values, valid_mask, cloud_counts):
    grid_vals = values.reshape(-1, GROUP, values.shape[-1])
    return jnp.sum(grid_vals * valid_mask.reshape(-1, GROUP, 1), 1) / cloud_counts[:, None].astype(
        jnp.float32
    )


def pool_low(feat_low, valid_mask, cloud_counts):
    grid_feat = feat_low.reshape(-1, GROUP, feat_low.shape[-1])
    weights_low = valid_mask.reshape(-1, GROUP).astype(jnp.bfloat16)
    summed = jnp.einsum("tgc,tg->tc", grid_feat, weights_low, preferred_element_type=jnp.float32)
    return summed / cloud_counts[:, None].astype(jnp.float32)


def batch_terms(values, valid_mask):
    masked = values * valid_mask[:, None]
    return (jnp.sum(valid_mask), jnp.sum(masked, 0), jnp.sum(masked * values, 0))


def normalize(values, totals, gain_vec, shift_vec):
    tally_all, sum_all, squares = totals
    centre_value = sum_all / tally_all
    spread_sq = squares / tally_all - centre_value * centre_value
    inverse = lax.rsqrt(spread_sq + EPS_NORM)
    unit_vals = (values - centre_value) * inverse
    return (unit_vals, inverse, unit_vals * gain_vec + shift_vec)


def layer_norm(values, gain_vec, shift_vec):
    centred = values - jnp.mean(values, -1, keepdims=True)
    inverse = lax.rsqrt(jnp.mean(centred * centred, -1, keepdims=True) + EPS_NORM)
    unit_vals = centred * inverse
    return (unit_vals, inverse, unit_vals * gain_vec + shift_vec)


def norm_back(d_unit, unit_vals, inverse):
    return inverse * (
        d_unit
        - jnp.mean(d_unit, -1, keepdims=True)
        - unit_vals * jnp.mean(d_unit * unit_vals, -1, keepdims=True)
    )


def gelu_back(inputs_pre, grad_in):
    return jax.vjp(jax.nn.gelu, inputs_pre)[1](grad_in)[0]


def row_product(left_mat, right_mat):
    return lax.dot_general(
        left_mat, right_mat, (((0,), (0,)), ((), ())), preferred_element_type=jnp.float32
    )


def back_product(left_mat, right_mat):
    return lax.dot_general(
        left_mat, right_mat, (((1,), (1,)), ((), ())), preferred_element_type=jnp.float32
    )


def first_layer(point_w, relative):
    return jnp.einsum(
        "cp,cf->pf",
        relative.astype(jnp.bfloat16),
        point_w["w1"],
        preferred_element_type=jnp.float32,
    )


def lower_net(point_w, pre_one, valid_mask, cloud_counts, first_totals):
    unit_one, inv_one, norm_one = normalize(
        pre_one, first_totals, as_float(point_w, "bn1_gain"), as_float(point_w, "bn1_shift")
    )
    act_one = jax.nn.gelu(norm_one).astype(jnp.bfloat16)
    pre_two = jnp.dot(act_one, point_w["w2"], preferred_element_type=jnp.float32) + as_float(
        point_w, "b2"
    )
    feat_two = pre_two.astype(jnp.bfloat16)
    pooled_low = pool_low(feat_two, valid_mask, cloud_counts).astype(jnp.bfloat16)
    global_part = jnp.dot(pooled_low, point_w["w3"][:C2], preferred_element_type=jnp.float32)
    local_part = jnp.dot(feat_two, point_w["w3"][C2:], preferred_element_type=jnp.float32)
    pre_three = (local_part.reshape(-1, GROUP, C3) + global_part[:, None, :]).reshape(-1, C3)
    return {
        "unit_one": unit_one,
        "inv_one": inv_one,
        "norm_one": norm_one,
        "act_one": act_one,
        "feat_two": feat_two,
        "pooled_low": pooled_low,
        "pre_three": pre_three,
    }


def global_totals(local_terms):
    return lax.psum((local_terms[0], local_terms[1], local_terms[2]), ("dp", "fsdp"))


def global_back(local_terms):
    return lax.psum((local_terms[0], local_terms[1]), ("dp", "fsdp"))


def adam_update(master, moment_one, moment_two, gradient, step_rates, decays):
    one_new = BETA_ONE * moment_one + (1.0 - BETA_ONE) * gradient
    two_new = BETA_TWO * moment_two + (1.0 - BETA_TWO) * gradient * gradient
    fix_one = 1.0 - BETA_ONE**STEP
    fix_two = 1.0 - BETA_TWO**STEP
    direction = one_new / fix_one / (jnp.sqrt(two_new / fix_two) + ADAM_EPS)
    master_new = master - step_rates * (direction + decays * master)
    return (master_new, one_new, two_new)


def on_device(
    points,
    point_count,
    centre_slot,
    cloud_length,
    cotangent,
    point_master,
    block_master,
    point_first,
    block_first,
    point_second,
    block_second,
):
    devices = lax.axis_size(("dp", "fsdp"))
    own_rank = lax.axis_index(("dp", "fsdp"))
    point_plan = point_layout()
    block_plan = block_layout()
    point_pieces = split_shard(point_master.astype(jnp.bfloat16), point_plan, devices)
    block_pieces = split_shard(block_master.astype(jnp.bfloat16), block_plan, devices)
    gathered = (
        lax.all_gather(point_pieces[0], ("dp", "fsdp"), axis=0, tiled=True),
        lax.all_gather(point_pieces[1], ("dp", "fsdp"), axis=0, tiled=True),
        lax.all_gather(point_pieces[2], ("dp", "fsdp"), axis=0, tiled=True),
        lax.all_gather(point_pieces[3], ("dp", "fsdp"), axis=0, tiled=True),
        lax.all_gather(block_pieces[0], ("dp", "fsdp"), axis=0, tiled=True),
        lax.all_gather(block_pieces[1], ("dp", "fsdp"), axis=0, tiled=True),
        lax.all_gather(block_pieces[2], ("dp", "fsdp"), axis=0, tiled=True),
        lax.all_gather(block_pieces[3], ("dp", "fsdp"), axis=0, tiled=True),
        lax.all_gather(block_pieces[4], ("dp", "fsdp"), axis=0, tiled=True),
    )
    point_w = unpack(gathered[:4], point_plan)
    block_w = unpack(gathered[4:], block_plan)
    clouds_here = cloud_length.shape[0]
    tokens_here = clouds_here * PATCHES
    relative, valid_mask, picker = cloud_geometry(points, point_count, centre_slot)
    pre_one = first_layer(point_w, relative)
    first_totals = global_totals(batch_terms(pre_one, valid_mask))
    fwd_parts = lower_net(point_w, pre_one, valid_mask, point_count, first_totals)
    third_totals = global_totals(batch_terms(fwd_parts["pre_three"], valid_mask))
    gain_three = as_float(point_w, "bn3_gain")
    unit_three, inv_three, norm_three = normalize(
        fwd_parts["pre_three"], third_totals, gain_three, as_float(point_w, "bn3_shift")
    )
    act_three = jax.nn.gelu(norm_three).astype(jnp.bfloat16)
    pre_four = jnp.dot(act_three, point_w["w4"], preferred_element_type=jnp.float32) + as_float(
        point_w, "b4"
    )
    x_zero = pool_mean(pre_four, valid_mask, point_count)
    score_scale = HEAD_DIM ** (-0.5)
    unit_a, inv_a, normed_a = layer_norm(
        x_zero, as_float(block_w, "ln1_gain"), as_float(block_w, "ln1_shift")
    )
    normed_a_low = normed_a.astype(jnp.bfloat16)
    qkv_low = jnp.dot(normed_a_low, block_w["wqkv"], preferred_element_type=jnp.float32).astype(
        jnp.bfloat16
    )
    qkv_low = qkv_low.reshape(clouds_here, PATCHES, 3, HEADS, HEAD_DIM)
    queries = qkv_low[:, :, 0]
    key_rows = qkv_low[:, :, 1]
    values = qkv_low[:, :, 2]
    key_valid = jnp.arange(PATCHES, dtype=jnp.int32)[None, :] < cloud_length[:, None]
    scores = (
        jnp.einsum("nqhe,nkhe->nhqk", queries, key_rows, preferred_element_type=jnp.float32)
        * score_scale
    )
    scores = jnp.where(key_valid[:, None, None, :], scores, NEG_FILL)
    row_top = jnp.max(scores, -1, keepdims=True)
    raised = jnp.exp(scores - row_top)
    row_total = jnp.sum(raised, -1, keepdims=True)
    soft_probs = (raised / row_total).astype(jnp.bfloat16)
    log_total = row_top + jnp.log(row_total)
    mixed_out = jnp.einsum(
        "nhqk,nkhe->nqhe", soft_probs, values, preferred_element_type=jnp.float32
    )
    mixed_low = mixed_out.astype(jnp.bfloat16).reshape(tokens_here, D)
    x_one = (
        x_zero
        + jnp.dot(mixed_low, block_w["wo"], preferred_element_type=jnp.float32)
        + as_float(block_w, "bo")
    )
    unit_b, inv_b, normed_b = layer_norm(
        x_one, as_float(block_w, "ln2_gain"), as_float(block_w, "ln2_shift")
    )
    normed_b_low = normed_b.astype(jnp.bfloat16)
    hidden_pre = jnp.dot(
        normed_b_low, block_w["wf1"], preferred_element_type=jnp.float32
    ) + as_float(block_w, "bf1")
    hidden_low = jax.nn.gelu(hidden_pre).astype(jnp.bfloat16)
    tokens_out = (
        x_one
        + jnp.dot(hidden_low, block_w["wf2"], preferred_element_type=jnp.float32)
        + as_float(block_w, "bf2")
    )
    grad_low = cotangent.astype(jnp.bfloat16)
    grad_wf2 = row_product(hidden_low, grad_low)
    d_pre = gelu_back(hidden_pre, back_product(grad_low, block_w["wf2"]))
    d_pre_low = d_pre.astype(jnp.bfloat16)
    grad_wf1 = row_product(normed_b_low, d_pre_low)
    d_normed_b = back_product(d_pre_low, block_w["wf1"])
    d_x_one = cotangent + norm_back(d_normed_b * as_float(block_w, "ln2_gain"), unit_b, inv_b)
    d_x_one_low = d_x_one.astype(jnp.bfloat16)
    grad_wo = row_product(mixed_low, d_x_one_low)
    d_mixed = (
        back_product(d_x_one_low, block_w["wo"])
        .astype(jnp.bfloat16)
        .reshape(clouds_here, PATCHES, HEADS, HEAD_DIM)
    )
    scores_again = (
        jnp.einsum("nqhe,nkhe->nhqk", queries, key_rows, preferred_element_type=jnp.float32)
        * score_scale
    )
    scores_again = jnp.where(key_valid[:, None, None, :], scores_again, NEG_FILL)
    soft_again = jnp.exp(scores_again - log_total)
    d_soft = jnp.einsum("nqhe,nkhe->nhqk", d_mixed, values, preferred_element_type=jnp.float32)
    d_values = jnp.einsum(
        "nhqk,nqhe->nkhe",
        soft_again.astype(jnp.bfloat16),
        d_mixed,
        preferred_element_type=jnp.float32,
    )
    row_dot = jnp.sum(soft_again * d_soft, -1, keepdims=True)
    d_scores = (soft_again * (d_soft - row_dot)).astype(jnp.bfloat16)
    d_queries = (
        jnp.einsum("nhqk,nkhe->nqhe", d_scores, key_rows, preferred_element_type=jnp.float32)
        * score_scale
    )
    d_keys = (
        jnp.einsum("nhqk,nqhe->nkhe", d_scores, queries, preferred_element_type=jnp.float32)
        * score_scale
    )
    d_qkv = (
        jnp.stack([d_queries, d_keys, d_values], axis=2)
        .reshape(tokens_here, 3 * D)
        .astype(jnp.bfloat16)
    )
    grad_wqkv = row_product(normed_a_low, d_qkv)
    d_normed_a = back_product(d_qkv, block_w["wqkv"])
    d_x_zero = d_x_one + norm_back(d_normed_a * as_float(block_w, "ln1_gain"), unit_a, inv_a)
    block_table = {
        "ln1_gain": jnp.sum(d_normed_a * unit_a, 0),
        "ln1_shift": jnp.sum(d_normed_a, 0),
        "bo": jnp.sum(d_x_one, 0),
        "ln2_gain": jnp.sum(d_normed_b * unit_b, 0),
        "ln2_shift": jnp.sum(d_normed_b, 0),
        "bf1": jnp.sum(d_pre, 0),
        "bf2": jnp.sum(cotangent, 0),
        "wqkv": grad_wqkv,
        "wo": grad_wo,
        "wf1": grad_wf1,
        "wf2": grad_wf2,
    }
    block_local = pack(block_table, block_plan, devices)
    share_map = slot_share(valid_mask, point_count)
    d_four = (d_x_zero[:, None, :] * share_map[:, :, None]).reshape(-1, D).astype(jnp.bfloat16)
    d_norm_three = gelu_back(norm_three, back_product(d_four, point_w["w4"]))
    third_partial = (jnp.sum(d_norm_three, 0), jnp.sum(d_norm_three * unit_three, 0))
    third_back = global_back(third_partial)
    d_pre_three = inv_three * (
        d_norm_three * gain_three
        - valid_mask[:, None]
        / third_totals[0]
        * (gain_three * third_back[0] + unit_three * gain_three * third_back[1])
    )
    d_three_low = d_pre_three.astype(jnp.bfloat16)
    per_token = jnp.einsum(
        "tgc,g->tc",
        d_three_low.reshape(-1, GROUP, C3),
        jnp.ones((GROUP,), jnp.bfloat16),
        preferred_element_type=jnp.float32,
    )
    d_pooled = jnp.dot(per_token, point_w["w3"][:C2].astype(jnp.float32).T, precision=HIGH)
    d_feat = back_product(d_three_low, point_w["w3"][C2:]) + (
        d_pooled[:, None, :] * share_map[:, :, None]
    ).reshape(-1, C2)
    d_feat_low = d_feat.astype(jnp.bfloat16)
    d_norm_one = gelu_back(fwd_parts["norm_one"], back_product(d_feat_low, point_w["w2"]))
    grad_w4 = row_product(act_three, d_four)
    grad_w3_top = jnp.dot(fwd_parts["pooled_low"].astype(jnp.float32).T, per_token, precision=HIGH)
    grad_w3_low = row_product(fwd_parts["feat_two"], d_three_low)
    grad_w2 = row_product(fwd_parts["act_one"], d_feat_low)
    shift_one = jnp.sum(d_norm_one, 0)
    gain_one_grad = jnp.sum(d_norm_one * fwd_parts["unit_one"], 0)
    first_back = global_back((shift_one, gain_one_grad))
    gain_one = as_float(point_w, "bn1_gain")
    d_pre_one = fwd_parts["inv_one"] * (
        d_norm_one * gain_one
        - valid_mask[:, None]
        / first_totals[0]
        * (gain_one * first_back[0] + fwd_parts["unit_one"] * gain_one * first_back[1])
    )
    d_one_low = d_pre_one.astype(jnp.bfloat16)
    grad_w1 = jnp.einsum(
        "cp,pf->cf", relative.astype(jnp.bfloat16), d_one_low, preferred_element_type=jnp.float32
    )
    d_relative = jnp.einsum(
        "pf,cf->cp", d_one_low, point_w["w1"], preferred_element_type=jnp.float32
    ).reshape(3, -1, GROUP)
    d_grid = d_relative - picker[None] * jnp.sum(d_relative, 2, keepdims=True)
    point_grad = d_grid.reshape(3, -1)
    point_table = {
        "w1": grad_w1,
        "bn1_gain": gain_one_grad,
        "bn1_shift": shift_one,
        "b2": jnp.sum(d_feat, 0),
        "bn3_gain": third_partial[1],
        "bn3_shift": third_partial[0],
        "b4": jnp.sum(d_x_zero, 0),
        "w2": grad_w2,
        "w3": jnp.concatenate([grad_w3_top, grad_w3_low], 0),
        "w4": grad_w4,
    }
    point_local = pack(point_table, point_plan, devices)
    all_reduced = (
        lax.psum_scatter(point_local[0], ("dp", "fsdp"), scatter_dimension=0, tiled=True),
        lax.psum_scatter(point_local[1], ("dp", "fsdp"), scatter_dimension=0, tiled=True),
        lax.psum_scatter(point_local[2], ("dp", "fsdp"), scatter_dimension=0, tiled=True),
        lax.psum_scatter(point_local[3], ("dp", "fsdp"), scatter_dimension=0, tiled=True),
        lax.psum_scatter(block_local[0], ("dp", "fsdp"), scatter_dimension=0, tiled=True),
        lax.psum_scatter(block_local[1], ("dp", "fsdp"), scatter_dimension=0, tiled=True),
        lax.psum_scatter(block_local[2], ("dp", "fsdp"), scatter_dimension=0, tiled=True),
        lax.psum_scatter(block_local[3], ("dp", "fsdp"), scatter_dimension=0, tiled=True),
        lax.psum_scatter(block_local[4], ("dp", "fsdp"), scatter_dimension=0, tiled=True),
    )
    point_reduced = all_reduced[:4]
    block_reduced = all_reduced[4:]
    point_gradient = jnp.concatenate(list(point_reduced))
    block_gradient = jnp.concatenate(list(block_reduced))
    point_rates, point_decays = shard_rates(point_plan, devices, own_rank)
    block_rates, block_decays = shard_rates(block_plan, devices, own_rank)
    point_new, point_one, point_two = adam_update(
        point_master, point_first, point_second, point_gradient, point_rates, point_decays
    )
    block_new, block_one, block_two = adam_update(
        block_master, block_first, block_second, block_gradient, block_rates, block_decays
    )
    return (
        tokens_out,
        point_grad,
        point_new,
        block_new,
        point_one,
        block_one,
        point_two,
        block_two,
        point_new.astype(jnp.bfloat16),
        block_new.astype(jnp.bfloat16),
        block_reduced[0],
    )


def solution(mesh):
    placed = (
        P(None, ("dp", "fsdp")),
        P(("dp", "fsdp")),
        P(("dp", "fsdp")),
        P(("dp", "fsdp")),
        P(("dp", "fsdp"), None),
        P(("dp", "fsdp")),
        P(("dp", "fsdp")),
        P(("dp", "fsdp")),
        P(("dp", "fsdp")),
        P(("dp", "fsdp")),
        P(("dp", "fsdp")),
    )
    return jax.shard_map(
        on_device,
        mesh=mesh,
        in_specs=placed,
        out_specs=(
            P(("dp", "fsdp"), None),
            P(None, ("dp", "fsdp")),
            P(("dp", "fsdp")),
            P(("dp", "fsdp")),
            P(("dp", "fsdp")),
            P(("dp", "fsdp")),
            P(("dp", "fsdp")),
            P(("dp", "fsdp")),
            P(("dp", "fsdp")),
            P(("dp", "fsdp")),
            P(("dp", "fsdp")),
        ),
        check_vma=False,
    )
```

profile of v0, /device:TPU:0, one launch (start us, length us, event | category | flops | bytes accessed | tf_op | source)
XLA Modules:
  0.0 1062.1 jit_solution(15147718258744061213)
XLA Ops:
  11.4 42.2 %all-reduce.17 = (bf16[3840]{0:T(1024)(128)(2,1)S(1)}, bf16[2304]{0:T(1024)(128)(2,1)S(1)}) all-reduce(bf16[3840]{0:T(1024)(128)(2,1)S(1)} %dynamic-update-slice.1, bf16[2304]{0:T(1024)(128)(2,1)S(1)} %dynamic-update-slice), channel_id=1, replica_groups=mesh['dp'=16,'fsdp'=2] {'dp','fsdp'}, use_global_device_ids=true, to_apply=%add.1 | all-reduce | flops 6144 | bytes 24576
  58.3 41.9 %all_gather.29 = bf16[262144]{0:T(1024)(128)(2,1)S(1)} all-gather(bf16[8192]{0:T(1024)(128)(2,1)S(1)} %slice.155), channel_id=1, replica_groups=mesh['dp'=16,'fsdp'=2] {'dp','fsdp'}, dimensions={0}, use_global_device_ids=true | all-gather | bytes 540672 | tf_op jit(solution)/shard_map/all_gather | solution.py:281
  106.3 36.8 %all_gather.28 = bf16[32768]{0:T(1024)(128)(2,1)S(1)} all-gather(bf16[1024]{0:T(1024)(128)(2,1)S(1)} %slice.153), channel_id=1, replica_groups=mesh['dp'=16,'fsdp'=2] {'dp','fsdp'}, dimensions={0}, use_global_device_ids=true | all-gather | bytes 67584 | tf_op jit(solution)/shard_map/all_gather | solution.py:280
  145.7 2.2 convert_divide_fusion
  152.3 39.3 %all_gather.30 = bf16[196608]{0:T(1024)(128)(2,1)S(1)} all-gather(bf16[6144]{0:T(1024)(128)(2,1)S(1)} %slice.160), channel_id=1, replica_groups=mesh['dp'=16,'fsdp'=2] {'dp','fsdp'}, dimensions={0}, use_global_device_ids=true | all-gather | bytes 405504 | tf_op jit(solution)/shard_map/all_gather | solution.py:282
  193.5 38.2 %all-gather.1 = bf16[32,1,4608]{2,1,0:T(2,128)(2,1)S(1)} all-gather(bf16[1,1,4608]{2,1,0:T(2,128)(2,1)S(1)} %reshape.455), channel_id=1, replica_groups=mesh['dp'=16,'fsdp'=2] {'dp','fsdp'}, dimensions={0}, use_global_device_ids=true | all-gather | bytes 304128 | tf_op jit(solution)/shard_map/all_gather | solution.py:285
  235.9 43.3 %all-gather = bf16[32,1,13824]{2,1,0:T(2,128)(2,1)S(1)} all-gather(bf16[1,1,13824]{2,1,0:T(2,128)(2,1)S(1)} %reshape.453), channel_id=1, replica_groups=mesh['dp'=16,'fsdp'=2] {'dp','fsdp'}, dimensions={0}, use_global_device_ids=true | all-gather | bytes 912384 | tf_op jit(solution)/shard_map/all_gather | solution.py:284
  279.2 5.3 reduce.3
  284.6 2.3 reshape.431
  286.8 4.9 fusion.20
  291.7 37.3 %all-reduce.15 = (f32[128]{0:T(128)S(1)}, f32[]{:T(128)}, f32[128]{0:T(128)S(1)}) all-reduce(f32[128]{0:T(128)S(1)} %get-tuple-element.16, f32[]{:T(128)} %get-tuple-element.82, f32[128]{0:T(128)S(1)} %get-tuple-element.15), channel_id=1, replica_groups=mesh['dp'=16,'fsdp'=2] {'dp','fsdp'}, use_global_device_ids=true, to_apply=%region_2.0 | all-reduce | flops 257 | bytes 2056 | tf_op jit(solution)/shard_map/psum | solution.py:242
  330.4 6.9 fusion.17
  339.0 16.2 %multiply_reduce_fusion = (f32[512]{0:T(512)S(1)}, f32[512]{0:T(512)S(1)}, f32[512,32,512]{2,0,1:T(8,128)}) fusion(f32[512,32]{0,1:T(8,128)S(1)} %copy-done.50, f32[512,512]{1,0:T(8,128)S(1)} %fusion.110, bf16[256,512,1]{1,0,2:T(8,128)(2,1)S(1)} %copy-done.40, bf16[512,32,256]{2,1,0:T(8,128)(2,1)S(1)} %bitcast.136), kind=kOutput, calls=%fused_computation.5 | convolution fusion | flops 4336909312 | bytes 43323392 | tf_op jit(solution)/shard_map/dot_general | solution.py:228
  355.2 31.8 %copy.87 = f32[512,32,512]{2,1,0:T(8,128)} copy(f32[512,32,512]{2,0,1:T(8,128)} %get-tuple-element.88) | data formatting | bytes 67108864 | tf_op jit(solution)/shard_map/add | solution.py:229
  387.0 41.8 %all-reduce.14 = (f32[512]{0:T(512)S(1)}, f32[512]{0:T(512)S(1)}) all-reduce(f32[512]{0:T(512)S(1)} %get-tuple-element.12, f32[512]{0:T(512)S(1)} %get-tuple-element.11), channel_id=1, replica_groups=mesh['dp'=16,'fsdp'=2] {'dp','fsdp'}, use_global_device_ids=true, to_apply=%region_10.0 | all-reduce | flops 1024 | bytes 8192 | tf_op jit(solution)/shard_map/psum | solution.py:242
  429.4 18.5 %fusion.15 = bf16[512,32,512]{2,0,1:T(8,128)(2,1)S(1)} fusion(f32[512,32,512]{2,0,1:T(8,128)} %get-tuple-element.88, f32[512]{0:T(512)S(1)} %get-tuple-element.78, f32[512]{0:T(512)S(1)} %get-tuple-element.77, f32[512]{0:T(512)S(1)} %get-tuple-element.84, f32[512]{0:T(512)S(1)} %get-tuple-element.83), kind=kLoop, calls=%fused_computation.20 | loop fusion | flops 109051904 | bytes 50339840 | tf_op jit(solution)/shard_map/convert_element_type | solution.py:302
  448.0 26.6 %copy.67 = bf16[512,32,512]{2,1,0:T(8,128)(2,1)} copy(bf16[512,32,512]{2,0,1:T(8,128)(2,1)S(1)} %fusion.15) | data formatting | bytes 33554432 | tf_op jit(solution)/shard_map/convert_element_type | solution.py:302
  474.6 12.9 %multiply_reduce_fusion.2 = f32[512,384]{1,0:T(8,128)S(1)} fusion(f32[512,32]{1,0:T(8,128)S(1)} %get-tuple-element.86, f32[384]{0:T(512)S(1)} %copy-done.89, bf16[16384,512]{1,0:T(8,128)(2,1)} %bitcast.137, bf16[512,384]{1,0:T(8,128)(2,1)S(1)} %copy-done.33), kind=kOutput, calls=%fused_computation.26 | convolution fusion | flops 6461128704 | bytes 18023936 | tf_op jit(solution)/shard_map/dot_general | solution.py:303
  494.8 2.8 copy.105
  511.0 7.5 concatenate.35
  518.5 7.5 concatenate.32
  532.1 3.5 reshape.435
  535.6 2.3 convolution_add_fusion.3
  539.5 2.8 fusion.79
  542.3 3.1 reshape.436
  545.4 5.6 fusion.128
  552.7 2.4 fusion.63
  568.1 4.5 copy.86
  572.6 3.4 convert_element_type.231
  576.1 3.0 multiply_reduce_fusion.7
  582.3 8.7 multiply_convert_fusion.1
  591.1 27.1 %fusion.44 = f32[512,384]{1,0:T(8,128)} fusion(bf16[512,32,512]{2,0,1:T(8,128)(2,1)} %copy-done.1, bf16[512,32,384]{2,1,0:T(8,128)(2,1)} %multiply_convert_fusion.1), kind=kOutput, calls=%fused_computation.84 | convolution fusion | flops 6442450944 | bytes 30146560 | tf_op jit(solution)/shard_map/dot_general | solution.py:197
  618.2 42.0 %fusion.114 = (f32[512]{0:T(512)S(1)}, f32[512]{0:T(512)S(1)}, f32[16384,512]{1,0:T(8,128)}) fusion(f32[512]{0:T(512)S(1)} %copy-done.64, f32[512]{0:T(512)S(1)} %copy-done.62, f32[512,32,512]{2,1,0:T(8,128)} %copy.87, f32[512]{0:T(512)S(1)} %copy-done.79, f32[512]{0:T(512)S(1)} %copy-done.60, bf16[16384,384]{1,0:T(8,128)(2,1)} %bitcast.138, ...), kind=kOutput, calls=%fused_computation.264 | convolution fusion | flops 6660553728 | bytes 80097280 | tf_op jit(solution)/shard_map/dot_general | solution.py:203
  660.2 39.9 %all-reduce.13 = (f32[512]{0:T(512)S(1)}, f32[512]{0:T(512)S(1)}) all-reduce(f32[512]{0:T(512)S(1)} %get-tuple-element.14, f32[512]{0:T(512)S(1)} %get-tuple-element.13), channel_id=1, replica_groups=mesh['dp'=16,'fsdp'=2] {'dp','fsdp'}, use_global_device_ids=true, to_apply=%region_26.27 | all-reduce | flops 1024 | bytes 8192 | tf_op jit(solution)/shard_map/psum | solution.py:246
  700.1 27.6 %multiply_convert_fusion = bf16[16384,512]{1,0:T(8,128)(2,1)} fusion(f32[16384,512]{1,0:T(8,128)} %get-tuple-element.97, f32[512,32,512]{2,1,0:T(8,128)} %copy.87, f32[512]{0:T(512)S(1)} %get-tuple-element.31, f32[512]{0:T(512)S(1)} %fusion.104, f32[16384]{0:T(1024)S(1)} %copy-done.30, f32[512]{0:T(512)S(1)} %copy-done.60, f32[512]{0:T(512)S(1)} %copy-done.62, ...), kind=kLoop, calls=%fused_computation.23 | loop fusion | flops 83886080 | bytes 83961856 | tf_op jit(solution)/shard_map/convert_element_type | solution.py:422
  727.7 13.7 %fusion.129 = f32[256,512]{1,0:T(8,128)} fusion(bf16[16384,256]{1,0:T(8,128)(2,1)} %copy-done.2, bf16[16384,512]{1,0:T(8,128)(2,1)} %multiply_convert_fusion), kind=kOutput, calls=%fused_computation.277 | convolution fusion | flops 4294967296 | bytes 25690112 | tf_op jit(solution)/shard_map/dot_general | solution.py:197
  741.4 2.5 fusion.105
  746.2 6.5 bitcast_multiply_fusion
  752.7 16.6 %fusion.127 = (f32[256]{0:T(256)S(1)}, bf16[16384,256]{1,0:T(8,128)(2,1)}) fusion(f32[16384,256]{1,0:T(8,128)} %bitcast_multiply_fusion, bf16[16384,512]{1,0:T(8,128)(2,1)} %multiply_convert_fusion, bf16[256,512]{1,0:T(8,128)(2,1)S(1)} %copy-done.18), kind=kOutput, calls=%fused_computation.275 | convolution fusion | flops 4307550208 | bytes 42206208 | tf_op jit(solution)/shard_map/dot_general | solution.py:203
  769.4 9.8 fusion.48
  779.2 11.5 %fusion.115 = (f32[128]{0:T(128)S(1)}, f32[128]{0:T(128)S(1)}, f32[16384,128]{1,0:T(8,128)}) fusion(f32[128]{0:T(128)S(1)} %copy-done.81, f32[16384,128]{1,0:T(8,128)} %get-tuple-element.87, f32[128]{0:T(128)S(1)} %copy-done.83, f32[128]{0:T(128)S(1)} %copy-done.95, f32[128]{0:T(128)S(1)} %copy-done.85, bf16[128,256]{1,0:T(8,128)(2,1)S(1)} %copy-done.52, ...), kind=kOutput, calls=%fused_computation.265 | convolution fusion | flops 1128267520 | bytes 25234432 | tf_op jit(solution)/shard_map/dot_general | solution.py:203
  790.7 40.5 %all-reduce.12 = (f32[128]{0:T(128)S(1)}, f32[128]{0:T(128)S(1)}) all-reduce(f32[128]{0:T(128)S(1)} %get-tuple-element.18, f32[128]{0:T(128)S(1)} %get-tuple-element.17), channel_id=1, replica_groups=mesh['dp'=16,'fsdp'=2] {'dp','fsdp'}, use_global_device_ids=true, to_apply=%region_30.31 | all-reduce | flops 256 | bytes 2048 | tf_op jit(solution)/shard_map/psum | solution.py:246
  831.1 7.4 multiply_convert_fusion.2
  840.4 3.2 reshape.448
  846.2 2.5 reshape.445
  855.8 41.9 %all-reduce.11 = (f32[2304]{0:T(1024)S(1)}, f32[3840]{0:T(1024)S(1)}) all-reduce(f32[2304]{0:T(1024)S(1)} %constant_dynamic-update-slice_fusion, f32[3840]{0:T(1024)S(1)} %constant_dynamic-update-slice_fusion.10), channel_id=2, replica_groups=mesh['dp'=16,'fsdp'=2] {'dp','fsdp'}, use_global_device_ids=true, to_apply=%region_34.35.clone | all-reduce | flops 6144 | bytes 49152
  897.8 4.4 fusion.43
  903.0 143.3 %all-reduce.20.cloned.1.call-done = (f32[32768]{0:T(1024)}, f32[262144]{0:T(1024)}, f32[196608]{0:T(1024)}, f32[442368]{0:T(1024)}, f32[147456]{0:T(1024)}, /*index=5*/f32[589824]{0:T(1024)}, f32[589824]{0:T(1024)}) async-done(((f32[32768]{0:T(1024)}, f32[262144]{0:T(1024)}, f32[196608]{0:T(1024)}, f32[442368]{0:T(1024)}, f32[147456]{0:T(1024)}, /*index=5*/f32[589824]{0:T(1024)}, f32[589824]{0:T(1024)}), ...) | async-done | bytes 9043984
  (355 shorter events, 100.2 us)
Async XLA Ops:
  7.2 227.4 %copy-start.21 = (f32[3,16384]{1,0:T(4,128)S(1)}, f32[3,16384]{1,0:T(4,128)}, u32[]{:S(2)}) copy-start(f32[3,16384]{1,0:T(4,128)} %param.11) | copy-start | bytes 589828
  7.2 524.9 %all-gather.5.cloned.1.call-start = ((), (), s32[]{:S(2)}) async-start(), calls=%async_computation | async-start | bytes 1216512 | tf_op jit(solution)/shard_map/all_gather | solution.py:286
  9.0 533.3 %all-gather.7.cloned.1.call-start = ((), (), s32[]{:S(2)}) async-start(), calls=%async_computation.1 | async-start | bytes 1216512 | tf_op jit(solution)/shard_map/all_gather | solution.py:287
  9.7 1036.6 %all-reduce.20.cloned.1.call-start = ((), (), s32[]{:S(2)}) async-start(), calls=%async_computation.2 | async-start | bytes 18087936
  53.6 181.0 %copy-start.68 = (bf16[3840]{0:T(1024)(128)(2,1)}, bf16[3840]{0:T(1024)(128)(2,1)S(1)}, u32[]{:S(2)}) copy-start(bf16[3840]{0:T(1024)(128)(2,1)S(1)} %get-tuple-element.45) | copy-start | bytes 23044
  53.6 233.3 %copy-start.66 = (bf16[2304]{0:T(1024)(128)(2,1)}, bf16[2304]{0:T(1024)(128)(2,1)S(1)}, u32[]{:S(2)}) copy-start(bf16[2304]{0:T(1024)(128)(2,1)S(1)} %get-tuple-element.46) | copy-start | bytes 13828
  55.3 374.1 %copy-start.59 = (f32[512]{0:T(512)}, f32[512]{0:T(512)S(1)}, u32[]{:S(2)}) copy-start(f32[512]{0:T(512)S(1)} %get-tuple-element.77) | copy-start | bytes 6148
  55.3 374.1 %copy-start.78 = (f32[512]{0:T(512)}, f32[512]{0:T(512)S(1)}, u32[]{:S(2)}) copy-start(f32[512]{0:T(512)S(1)} %get-tuple-element.78) | copy-start | bytes 6148
  57.5 430.6 %copy-start.45 = (f32[512]{0:T(512)}, f32[512]{0:T(512)S(1)}, u32[]{:S(2)}) copy-start(f32[512]{0:T(512)S(1)} %convert_element_type.202) | copy-start | bytes 6148
  145.0 343.1 %copy-start.71 = (f32[384]{0:T(512)}, f32[384]{0:T(512)S(1)}, u32[]{:S(2)}) copy-start(f32[384]{0:T(512)S(1)} %get-tuple-element.75) | copy-start | bytes 4612
  151.7 41.8 %copy-start.29 = (s32[16384]{0:T(1024)}, s32[16384]{0:T(1024)S(1)}, u32[]{:S(2)}) copy-start(s32[16384]{0:T(1024)S(1)} %eq.38) | copy-start | bytes 196612
  193.5 145.1 %copy-start.19 = (bf16[256,512]{1,0:T(8,128)(2,1)}, bf16[256,512]{1,0:T(8,128)(2,1)S(1)}, u32[]{:S(2)}) copy-start(bf16[256,512]{1,0:T(8,128)(2,1)S(1)} %slice.129) | copy-start | bytes 786436
  235.9 55.8 %copy-start.14 = (bf16[3,16384]{1,0:T(4,128)(2,1)}, bf16[3,16384]{1,0:T(4,128)(2,1)S(1)}, u32[]{:S(2)}) copy-start(bf16[3,16384]{1,0:T(4,128)(2,1)S(1)} %subtract_convert_fusion) | copy-start | bytes 294916
  284.5 45.8 %copy-start.51 = (bf16[128,256]{1,0:T(8,128)(2,1)S(1)}, bf16[128,256]{1,0:T(8,128)(2,1)}, u32[]{:S(2)}) copy-start(bf16[128,256]{1,0:T(8,128)(2,1)} %reshape.428) | copy-start | bytes 196612
  284.5 45.8 %copy-start.84 = (f32[128]{0:T(128)S(1)}, f32[128]{0:T(128)}, u32[]{:S(2)}) copy-start(f32[128]{0:T(128)} %get-tuple-element.79) | copy-start | bytes 1540
  284.6 45.8 %copy-start.94 = (f32[128]{0:T(128)S(1)}, f32[128]{0:T(128)}, u32[]{:S(2)}) copy-start(f32[128]{0:T(128)} %get-tuple-element.80) | copy-start | bytes 1540
  284.6 45.8 %copy-start.97 = (f32[256]{0:T(256)S(1)}, f32[256]{0:T(256)}, u32[]{:S(2)}) copy-start(f32[256]{0:T(256)} %slice_convert_fusion.10) | copy-start | bytes 3076
  337.3 17.8 %copy-start.2 = (bf16[16384,256]{1,0:T(8,128)(2,1)}, bf16[16384,256]{1,0:T(8,128)(2,1)S(1)}, u32[]{:S(2)}) copy-start(bf16[16384,256]{1,0:T(8,128)(2,1)S(1)} %fusion.17) | copy-start | bytes 25165828
  429.4 18.6 %copy-start.61 = (f32[512]{0:T(512)}, f32[512]{0:T(512)S(1)}, u32[]{:S(2)}) copy-start(f32[512]{0:T(512)S(1)} %get-tuple-element.83) | copy-start | bytes 6148
  429.4 18.6 %copy-start.63 = (f32[512]{0:T(512)}, f32[512]{0:T(512)S(1)}, u32[]{:S(2)}) copy-start(f32[512]{0:T(512)S(1)} %get-tuple-element.84) | copy-start | bytes 6148
  448.0 26.6 %copy-start.1 = (bf16[512,32,512]{2,0,1:T(8,128)(2,1)}, bf16[512,32,512]{2,0,1:T(8,128)(2,1)S(1)}, u32[]{:S(2)}) copy-start(bf16[512,32,512]{2,0,1:T(8,128)(2,1)S(1)} %fusion.15) | copy-start | bytes 50331652
  448.0 26.6 %copy-start.33 = (bf16[512,384]{1,0:T(8,128)(2,1)S(1)}, bf16[512,384]{1,0:T(8,128)(2,1)}, u32[]{:S(2)}) copy-start(bf16[512,384]{1,0:T(8,128)(2,1)} %reshape.429) | copy-start | bytes 1179652
  448.0 26.6 %copy-start.89 = (f32[384]{0:T(512)S(1)}, f32[384]{0:T(512)}, u32[]{:S(2)}) copy-start(f32[384]{0:T(512)} %slice_convert_fusion.7) | copy-start | bytes 4612
  506.1 49.0 %copy-start.5 = (f32[512,384]{1,0:T(8,128)}, f32[512,384]{1,0:T(8,128)S(1)}, u32[]{:S(2)}) copy-start(f32[512,384]{1,0:T(8,128)S(1)} %get-tuple-element.92) | copy-start | bytes 2359300
  506.1 33.4 %copy-start.27 = (f32[512,384]{1,0:T(8,128)S(1)}, f32[512,384]{1,0:T(8,128)}, u32[]{:S(2)}) copy-start(f32[512,384]{1,0:T(8,128)} %param.15) | copy-start | bytes 2359300
  591.1 27.1 %copy-start.34 = (bf16[512,384]{1,0:T(8,128)(2,1)S(1)}, bf16[512,384]{1,0:T(8,128)(2,1)}, u32[]{:S(2)}) copy-start(bf16[512,384]{1,0:T(8,128)(2,1)} %reshape.429) | copy-start | bytes 1179652
  591.1 27.1 %copy-start.60 = (f32[512]{0:T(512)S(1)}, f32[512]{0:T(512)}, u32[]{:S(2)}) copy-start(f32[512]{0:T(512)} %copy-done.59) | copy-start | bytes 6148
  591.1 27.1 %copy-start.62 = (f32[512]{0:T(512)S(1)}, f32[512]{0:T(512)}, u32[]{:S(2)}) copy-start(f32[512]{0:T(512)} %copy-done.61) | copy-start | bytes 6148
  591.1 27.1 %copy-start.64 = (f32[512]{0:T(512)S(1)}, f32[512]{0:T(512)}, u32[]{:S(2)}) copy-start(f32[512]{0:T(512)} %copy-done.63) | copy-start | bytes 6148
  591.1 27.1 %copy-start.79 = (f32[512]{0:T(512)S(1)}, f32[512]{0:T(512)}, u32[]{:S(2)}) copy-start(f32[512]{0:T(512)} %copy-done.78) | copy-start | bytes 6148
  618.2 81.9 %copy-start.67 = (bf16[2304]{0:T(1024)(128)(2,1)S(1)}, bf16[2304]{0:T(1024)(128)(2,1)}, u32[]{:S(2)}) copy-start(bf16[2304]{0:T(1024)(128)(2,1)} %copy-done.66) | copy-start | bytes 13828
  618.2 81.9 %copy-start.30 = (f32[16384]{0:T(1024)S(1)}, f32[16384]{0:T(1024)}, u32[]{:S(2)}) copy-start(f32[16384]{0:T(1024)} %broadcast_select_fusion.3) | copy-start | bytes 196612
  752.7 16.7 %copy-start.85 = (f32[128]{0:T(128)S(1)}, f32[128]{0:T(128)}, u32[]{:S(2)}) copy-start(f32[128]{0:T(128)} %get-tuple-element.79) | copy-start | bytes 1540
  752.7 16.7 %copy-start.95 = (f32[128]{0:T(128)S(1)}, f32[128]{0:T(128)}, u32[]{:S(2)}) copy-start(f32[128]{0:T(128)} %get-tuple-element.80) | copy-start | bytes 1540
  850.8 47.0 %copy-start.6 = (f32[512,384]{1,0:T(8,128)S(1)}, f32[512,384]{1,0:T(8,128)}, u32[]{:S(2)}) copy-start(f32[512,384]{1,0:T(8,128)} %copy-done.5) | copy-start | bytes 2359300
  850.8 47.0 %copy-start.86 = (f32[384]{0:T(512)S(1)}, f32[384]{0:T(512)}, u32[]{:S(2)}) copy-start(f32[384]{0:T(512)} %get-tuple-element.76) | copy-start | bytes 4612
  855.5 46.7 %copy-start.41 = (f32[16384]{0:T(1024)S(1)}, f32[16384]{0:T(1024)}, u32[]{:S(2)}) copy-start(f32[16384]{0:T(1024)} %compare_convert_fusion) | copy-start | bytes 196612
  855.5 196.6 %copy-start.37 = (f32[15432]{0:T(1024)S(1)}, f32[15432]{0:T(1024)}, u32[]{:S(2)}) copy-start(f32[15432]{0:T(1024)} %param.16) | copy-start | bytes 185188
  855.5 196.6 %copy-start.38 = (f32[15432]{0:T(1024)S(1)}, f32[15432]{0:T(1024)}, u32[]{:S(2)}) copy-start(f32[15432]{0:T(1024)} %concatenate.31) | copy-start | bytes 185188
  855.5 196.6 %copy-start.39 = (f32[15432]{0:T(1024)S(1)}, f32[15432]{0:T(1024)}, u32[]{:S(2)}) copy-start(f32[15432]{0:T(1024)} %concatenate.27) | copy-start | bytes 185188
  855.5 196.6 %copy-start.48 = (f32[15432]{0:T(1024)S(1)}, f32[15432]{0:T(1024)}, u32[]{:S(2)}) copy-start(f32[15432]{0:T(1024)} %param.18) | copy-start | bytes 185188
  855.6 196.6 %copy-start.49 = (f32[15432]{0:T(1024)S(1)}, f32[15432]{0:T(1024)}, u32[]{:S(2)}) copy-start(f32[15432]{0:T(1024)} %param.20) | copy-start | bytes 185188
  855.6 198.7 %copy-start.23 = (f32[55416]{0:T(1024)S(1)}, f32[55416]{0:T(1024)}, u32[]{:S(2)}) copy-start(f32[55416]{0:T(1024)} %param.17) | copy-start | bytes 664996
  855.6 198.7 %copy-start.24 = (f32[55416]{0:T(1024)S(1)}, f32[55416]{0:T(1024)}, u32[]{:S(2)}) copy-start(f32[55416]{0:T(1024)} %concatenate.35) | copy-start | bytes 664996
  855.6 198.7 %copy-start.25 = (f32[55416]{0:T(1024)S(1)}, f32[55416]{0:T(1024)}, u32[]{:S(2)}) copy-start(f32[55416]{0:T(1024)} %concatenate.32) | copy-start | bytes 664996
  855.6 198.7 %copy-start.42 = (f32[55416]{0:T(1024)S(1)}, f32[55416]{0:T(1024)}, u32[]{:S(2)}) copy-start(f32[55416]{0:T(1024)} %param.19) | copy-start | bytes 664996
  855.6 198.7 %copy-start.43 = (f32[55416]{0:T(1024)S(1)}, f32[55416]{0:T(1024)}, u32[]{:S(2)}) copy-start(f32[55416]{0:T(1024)} %param.21) | copy-start | bytes 664996
  897.8 157.6 %copy-start.96 = (f32[120]{0:T(128)}, f32[120]{0:T(128)S(1)}, u32[]{:S(2)}) copy-start(f32[120]{0:T(128)S(1)} %dynamic-slice.4) | copy-start | bytes 1444
  (54 other events, 393.3 us)
Sparse Core Ops, SparseCore 0:
  10.9 56.9 all-gather.4
  70.9 52.9 all-gather.6
  855.7 190.5 all-reduce.19
where the time goes:
time: 1070 us; the launch traced here: 1060 us
  blocking collectives  443 us (41%)
  matrix products  205 us (19%)
  waiting for transfers between devices  144 us (13%)
  local copies, waits for them, and re-layouts  142 us (13%)
  other arithmetic  111 us (10%)
  between operations  16.3 us (2%)
    unnamed x4, waiting for transfers between devices  144 us
    unnamed x2, blocking collectives  84.1 us
    dot_general x7, matrix products, back_product(): lax.dot_general(left_mat, right_mat, (((1,), (1,)), ((), ())), preferred_...  80.8 us
    psum x2, blocking collectives, global_back(): return lax.psum((local_terms[0], local_terms[1]), ('dp', 'fsdp'))  80.3 us
    psum x2, blocking collectives, global_totals(): lax.psum((local_terms[0], local_terms[1], local_terms[2]), ('dp', 'fsdp'))  79.1 us
    dot_general x7, matrix products, row_product(): lax.dot_general(left_mat, right_mat, (((0,), (0,)), ((), ())), preferred_...  59.1 us
    all_gather x1, blocking collectives, on_device(): lax.all_gather(block_pieces[1], ('dp', 'fsdp'), axis=0, tiled=True)  43.3 us
    all_gather x1, blocking collectives, on_device(): lax.all_gather(point_pieces[2], ('dp', 'fsdp'), axis=0, tiled=True)  41.9 us
  transfers between devices with their start and end apart: 3, of which 1 were waited for; matrix products, arithmetic and copies ran while one was open for 20% of the time, Pallas kernels for 0%

commit v1 on v0

v1 whole, which is shorter than its diff:
```python
import functools
import math

import jax
import jax.numpy as jnp
from jax import lax
from jax.experimental import pallas as pl
from jax.experimental.pallas import tpu as pltpu
from jax.sharding import PartitionSpec as P

C1 = 128
C2 = 256
C3 = 512
D = 384
HEADS = 6
HEAD_DIM = 64
FF = 1536
GROUP = 32
PATCHES = 64
STEP = 10

EPS_NORM = 1e-05
BETA_ONE = 0.9
BETA_TWO = 0.95
ADAM_EPS = 1e-08
DECAY_RATE = 0.05
NEG_FILL = -1e30

F32 = jnp.float32
BF16 = jnp.bfloat16
AXES = ("dp", "fsdp")
MESH = pl.DeviceIdType.MESH
VMEM_LIMIT = 60 * 2**20
TILE = 2048
TOK = TILE // GROUP
SUB = 512
TB = 256
PAIR = 128

NZ, NY, NX, NC = 4, 2, 2, 2
W3_AT, W4_AT, QKV_AT, WO_AT, WF1_AT, WF2_AT, WIDTH = 0, 512, 896, 2048, 2432, 3968, 5120
W2_AT, PSMALL_AT, BSMALL_AT = 896, 1152, 1280
HALF = WIDTH // 2
PROWS, BROWS = 128, 440


def point_layout():
    return [
        [
            ("w1", (3, C1), 3.0 ** (-0.5)),
            ("bn1_gain", (C1,), 0.0),
            ("bn1_shift", (C1,), -1.0),
            ("b2", (C2,), -1.0),
            ("bn3_gain", (C3,), 0.0),
            ("bn3_shift", (C3,), -1.0),
            ("b4", (D,), -1.0),
        ],
        [("w2", (C1, C2), C1 ** (-0.5))],
        [("w3", (2 * C2, C3), (2 * C2) ** (-0.5))],
        [("w4", (C3, D), C3 ** (-0.5))],
    ]


def block_layout():
    return [
        [
            ("ln1_gain", (D,), 0.0),
            ("ln1_shift", (D,), -1.0),
            ("bo", (D,), -1.0),
            ("ln2_gain", (D,), 0.0),
            ("ln2_shift", (D,), -1.0),
            ("bf1", (FF,), -1.0),
            ("bf2", (D,), -1.0),
        ],
        [("wqkv", (D, 3 * D), D ** (-0.5))],
        [("wo", (D, D), 3.0 * D ** (-0.5))],
        [("wf1", (D, FF), D ** (-0.5))],
        [("wf2", (FF, D), FF ** (-0.5))],
    ]


def rate_for(spread):
    return 2.0 * spread if spread > 0.0 else 0.5 if spread == 0.0 else 0.6


def decay_for(spread):
    return DECAY_RATE if spread > 0.0 else 0.0


def segment_lengths(layout, devices):
    lengths_out = []
    for segment in layout:
        used_len = sum((math.prod(entry[1]) for entry in segment))
        lengths_out.append(-(-used_len // devices) * devices)
    return lengths_out


def shard_rates(layout, devices, own_rank):
    rate_parts = []
    decay_parts = []
    for segment, seg_len in zip(layout, segment_lengths(layout, devices)):
        piece_len = seg_len // devices
        position = own_rank * piece_len + jnp.arange(piece_len, dtype=jnp.int32)
        seg_rates = jnp.zeros((piece_len,), F32)
        seg_decays = jnp.zeros((piece_len,), F32)
        offset = 0
        for entry_label, entry_dims, spread in segment:
            extent = math.prod(entry_dims)
            inside = (position >= offset) & (position < offset + extent)
            seg_rates = jnp.where(inside, rate_for(spread), seg_rates)
            seg_decays = jnp.where(inside, decay_for(spread), seg_decays)
            offset += extent
        rate_parts.append(seg_rates)
        decay_parts.append(seg_decays)
    return (jnp.concatenate(rate_parts), jnp.concatenate(decay_parts))


def mm(a, b):
    return jnp.dot(a, b, preferred_element_type=F32)


def mm_tn(a, b):
    return lax.dot_general(a, b, (((0,), (0,)), ((), ())), preferred_element_type=F32)


def mm_nt(a, b):
    return lax.dot_general(a, b, (((1,), (1,)), ((), ())), preferred_element_type=F32)


def low(v):
    return v.astype(BF16)


def split_three(v):
    hi = low(v)
    rest = v - hi.astype(F32)
    mid = low(rest)
    return hi, mid, low(rest - mid.astype(F32))


def mm_exact(a, b):
    hi, mid, lo = split_three(a)
    return mm(hi, b) + (mm(mid, b) + mm(lo, b))


GELU_A = math.sqrt(2.0 / math.pi)
GELU_B = GELU_A * 0.044715


def gelu_pair(v):
    square = v * v
    t = jnp.tanh(v * (GELU_A + GELU_B * square))
    h = 0.5 + 0.5 * t
    g = v * h
    return g, h + (g - g * h) * (2.0 * GELU_A + 6.0 * GELU_B * square)


def patch_ones():
    i = lax.broadcasted_iota(jnp.int32, (256, 256), 0) // GROUP
    j = lax.broadcasted_iota(jnp.int32, (256, 256), 1) // GROUP
    return (i == j).astype(F32).astype(BF16)


def token_ones():
    t = lax.broadcasted_iota(jnp.int32, (TOK, TILE), 0)
    p = lax.broadcasted_iota(jnp.int32, (TOK, TILE), 1) // GROUP
    return (t == p).astype(F32).astype(BF16)


def patch_sum(rows, ones):
    return mm_exact(rows, ones)


def groups(dp):
    lower = math.gcd(dp, 4)
    return lower, dp // lower


def ring_peers(dp, upper_stage):
    lower, upper = groups(dp)
    at, core = lax.axis_index("dp"), lax.axis_index("fsdp")
    up, down = at // lower, lax.rem(at, lower)
    peers = []
    if upper_stage:
        for k in range(1, upper):
            peers.append((lax.rem(up + k, upper) * lower + down, core))
    else:
        for k in range(1, lower * NC):
            p = lax.rem(down * NC + core + k, lower * NC)
            peers.append((up * lower + p // NC, lax.rem(p, NC)))
    return peers


def greet(peers):
    barrier = pltpu.get_barrier_semaphore()
    for peer in peers:
        pl.semaphore_signal(barrier, inc=1, device_id=peer, device_id_type=MESH)
    return len(peers)


def greeted(count):
    pl.semaphore_wait(pltpu.get_barrier_semaphore(), count)


def sum_start(dp, upper_stage, acc, slots, send, recv):
    lower, upper = groups(dp)
    first = lower * NC - 1 if upper_stage else 0
    copies = []
    for k, peer in enumerate(ring_peers(dp, upper_stage)):
        copy = pltpu.make_async_remote_copy(
            src_ref=acc,
            dst_ref=slots.at[first + k],
            send_sem=send.at[first + k],
            recv_sem=recv.at[first + k],
            device_id=peer,
            device_id_type=MESH,
        )
        copy.start()
        copies.append(copy)
    return copies


def sum_finish(dp, upper_stage, acc, slots, copies):
    lower, upper = groups(dp)
    first = lower * NC - 1 if upper_stage else 0
    for copy in copies:
        copy.wait()
    total = acc[...]
    for k in range(len(copies)):
        total = total + slots[first + k]
    acc[...] = total


def sum_over_devices(dp, acc, slots, send, recv):
    for upper_stage in (False, True):
        copies = sum_start(dp, upper_stage, acc, slots, send, recv)
        sum_finish(dp, upper_stage, acc, slots, copies)


def sum_scratch(dp, shape):
    lower, upper = groups(dp)
    count = lower * NC - 1 + upper - 1
    return [
        pltpu.VMEM(shape, F32),
        pltpu.VMEM((count,) + shape, F32),
        pltpu.SemaphoreType.DMA((count,)),
        pltpu.SemaphoreType.DMA((count,)),
    ]


def all_peers(dp):
    return ring_peers(dp, False) + ring_peers(dp, True)


def vmem(count):
    return [pl.BlockSpec(memory_space=pltpu.VMEM)] * count


def shaped(*items):
    return [jax.ShapeDtypeStruct(s, t) for s, t in items]


def params(**more):
    return pltpu.CompilerParams(vmem_limit_bytes=VMEM_LIMIT, **more)


def geometry(points_ref, slots_ref, rel_ref, moment_ref):
    ones = patch_ones()
    moment_ref[...] = jnp.zeros_like(moment_ref)
    lane = lax.rem(lax.broadcasted_iota(jnp.int32, (1, 256), 1), GROUP)

    def piece(i, carry):
        at = pl.ds(pl.multiple_of(i * 256, 256), 256)
        pts = points_ref[:, at]
        valid = (lane < slots_ref[0:1, at]).astype(F32)
        pick = (lane == slots_ref[1:2, at]).astype(F32)
        relative = (pts - patch_sum(pts * pick, ones)) * valid
        rows = low(jnp.concatenate([relative, valid, relative, valid], axis=0))
        rel_ref[:, at] = rows
        moment_ref[:, 0:8] += mm_nt(rows, rows)
        return carry

    lax.fori_loop(0, points_ref.shape[1] // 256, piece, 0, unroll=8)


def prepare_one(moments, small):
    n = moments[3:4, 3:4]
    w = [small[k : k + 1, :] for k in range(3)]
    gain, shift = small[3:4, :], small[4:5, :]
    mean = sum(w[k] * moments[k : k + 1, 3:4] for k in range(3)) / n
    square = jnp.zeros_like(mean)
    for j in range(3):
        for k in range(3):
            square = square + w[j] * w[k] * moments[j : j + 1, k : k + 1]
    inverse = lax.rsqrt(square / n - mean * mean + EPS_NORM)
    scale = inverse * gain
    scaled = [wk * scale for wk in w]
    offset = shift - mean * scale
    high = [low(v) for v in scaled + [offset]]
    rest = [low(v - h.astype(F32)) for v, h in zip(scaled + [offset], high)]
    forward = jnp.concatenate(high + rest, axis=0)
    zero = jnp.zeros((1, C1), BF16)
    backward = jnp.concatenate(high[:3] + [zero] + rest[:3] + [zero], axis=0)
    stats = jnp.concatenate(
        [mean, inverse, jnp.broadcast_to(n, (1, C1)), scale, jnp.zeros((4, C1), F32)], axis=0
    )
    return forward, backward, stats


def flat_rows(pieces, length, rows):
    lane = lax.broadcasted_iota(jnp.int32, (1, 128), 1)
    out = [jnp.zeros((1, 128), F32) for _ in range(rows)]
    for r in range(pieces.shape[0]):
        row = jnp.where(lane < length, pieces[r : r + 1, :], 0.0)
        at = length * r
        row = pltpu.roll(row, at % 128, 1) if at % 128 else row
        first = at // 128
        out[first] = out[first] + jnp.where(lane >= at % 128, row, 0.0)
        if at % 128 + length > 128:
            out[first + 1] = out[first + 1] + jnp.where(lane < at % 128, row, 0.0)
    return jnp.concatenate(out, axis=0)


def piece_of(rows, at, length):
    lane = lax.broadcasted_iota(jnp.int32, (1, 128), 1)
    first, shift = at // 128, at % 128
    row = rows[first : first + 1, :]
    if shift:
        row = pltpu.roll(row, 128 - shift, 1)
        if shift + length > 128:
            other = pltpu.roll(rows[first + 1 : first + 2, :], 128 - shift, 1)
            row = jnp.where(lane < 128 - shift, row, other)
    return jnp.where(lane < length, row, 0.0)


def where_am_i():
    at = lax.axis_index("dp")
    return at // (NY * NX), lax.rem(at // NX, NY), lax.rem(at, NX), lax.axis_index("fsdp")


def chip(z, y, x):
    return (z * NY + y) * NX + x


def rows_twelve():
    return [(QKV_AT, 3 * D), (WO_AT, D), (WF1_AT, FF)]


def gather_kernel(
    points_ref, slots_ref, pflat, bflat,
    rel_ref, moment_ref, psmall_o, bsmall_o, w2_o, w3_o, w4_o, wqkv_o, wo_o, wf1_o, wf2_o,
    blocks, stage, wide, acc, sums, ssend, srecv, gsend, grecv,
):
    z, y, x, core = where_am_i()
    dp = NZ * NY * NX
    near = [(chip(lax.rem(z + k, NZ), y, x), core) for k in range(1, NZ)]
    over_y, over_x, twin = (chip(z, 1 - y, x), core), (chip(z, y, 1 - x), core), (chip(z, y, x), 1 - core)
    count = greet(all_peers(dp) + near + [over_y, over_x, twin])

    stage[...] = jnp.zeros_like(stage)
    for at, start, rows, cols, under in (
        (W3_AT, 9, 16, C3, 0), (W4_AT, 73, 16, D, 0), (W2_AT, 1, 4, C2, 12),
    ):
        for j in range(cols // 128):
            stage[under : under + rows, at + 128 * j : at + 128 * j + 128] = pflat[
                pl.ds(start + j, rows, stride=cols // 128), :
            ]
    stage[12:13, PSMALL_AT : PSMALL_AT + 128] = pflat[0:1, :]
    stage[12:13, BSMALL_AT : BSMALL_AT + 128] = bflat[0:1, :]
    start = 1
    for at, cols in rows_twelve():
        for j in range(cols // 128):
            stage[0:12, at + 128 * j : at + 128 * j + 128] = bflat[
                pl.ds(start + j, 12, stride=cols // 128), :
            ]
        start += 12 * cols // 128
    for b in range(3):
        for j in range(D // 128):
            to = WF2_AT + D * b + 128 * j
            stage[:, to : to + 128] = bflat[pl.ds(start + 48 * b + j, 16, stride=3), :]
    blocks[z, y, x, core] = low(stage[...])

    greeted(count)
    used = [0]

    def send(view, peer):
        k = used[0]
        used[0] += 1
        copy = pltpu.make_async_remote_copy(
            src_ref=view, dst_ref=view, send_sem=gsend.at[k], recv_sem=grecv.at[k],
            device_id=peer, device_id_type=MESH,
        )
        copy.start()
        return copy

    one, two = pl.ds(0, HALF), pl.ds(HALF, HALF)
    live = [send(blocks.at[z, y, x, core], peer) for peer in near]
    geometry(points_ref, slots_ref, rel_ref, acc)
    small = sum_start(dp, False, acc, sums, ssend, srecv)
    for copy in live:
        copy.wait()
    live = [
        send(blocks.at[:, y, x, core, :, one], over_y),
        send(blocks.at[:, y, x, core, :, two], over_x),
    ]
    inner = [send(blocks.at[:, y, x, core], twin)]
    sum_finish(dp, False, acc, sums, small)
    small = sum_start(dp, True, acc, sums, ssend, srecv)
    for copy in live:
        copy.wait()
    live = [
        send(blocks.at[:, :, x, core, :, one], over_x),
        send(blocks.at[:, y, :, core, :, two], over_y),
    ]
    inner += [
        send(blocks.at[:, 1 - y, x, core, :, one], twin),
        send(blocks.at[:, y, 1 - x, core, :, two], twin),
    ]
    sum_finish(dp, True, acc, sums, small)
    moment_ref[...] = acc[...]
    for copy in live:
        copy.wait()
    inner += [
        send(blocks.at[:, :, 1 - x, core, :, one], twin),
        send(blocks.at[:, 1 - y, :, core, :, two], twin),
    ]
    for copy in inner:
        copy.wait()

    for d in range(dp * NC):
        cz, cy, cx, cc = d // 8, d // 4 % 2, d // 2 % 2, d % 2
        block = blocks.at[cz, cy, cx, cc]
        w3_o[16 * d : 16 * d + 16, :] = block[:, W3_AT : W3_AT + C3]
        w4_o[16 * d : 16 * d + 16, :] = block[:, W4_AT : W4_AT + D]
        for b in range(3):
            at = 48 * d + 16 * b
            wf2_o[at : at + 16, :] = block[:, WF2_AT + D * b : WF2_AT + D * b + D]
        under = block[:, QKV_AT:WF2_AT].astype(F32)
        wide[12 * d : 12 * d + 12, :] = under[0:12, :]
        tail = under[12:16, 0 : BSMALL_AT + 128 - QKV_AT]
        wide[384 + 4 * d : 384 + 4 * d + 4, 0 : BSMALL_AT + 128 - QKV_AT] = tail
    for at, cols, out in ((QKV_AT, 3 * D, wqkv_o), (WO_AT, D, wo_o), (WF1_AT, FF, wf1_o)):
        out[...] = low(wide[0:384, at - QKV_AT : at - QKV_AT + cols])
    w2_o[...] = low(wide[384:512, 0:C2])
    tails = wide[pl.ds(384, 32, stride=4), :] if False else None
    psmall = jnp.concatenate(
        [wide[384 + 4 * d : 385 + 4 * d, PSMALL_AT - QKV_AT : PSMALL_AT - QKV_AT + 128] for d in range(32)], 0
    )
    bsmall = jnp.concatenate(
        [wide[384 + 4 * d : 385 + 4 * d, BSMALL_AT - QKV_AT : BSMALL_AT - QKV_AT + 128] for d in range(32)], 0
    )
    psmall_o[0:18, :] = flat_rows(psmall, 72, 18)
    bsmall_o[0:30, :] = flat_rows(bsmall, 120, 30)


def gather_call(points, slots, pflat, bflat):
    dp = NZ * NY * NX
    count = points.shape[1]
    outs = shaped(
        ((8, count), BF16), ((8, 128), F32), ((24, 128), F32), ((32, 128), F32),
        ((C1, C2), BF16), ((2 * C2, C3), BF16), ((C3, D), BF16),
        ((D, 3 * D), BF16), ((D, D), BF16), ((D, FF), BF16), ((FF, D), BF16),
    )
    return pl.pallas_call(
        gather_kernel,
        out_shape=outs,
        in_specs=vmem(4),
        out_specs=vmem(len(outs)),
        scratch_shapes=[
            pltpu.VMEM((NZ, NY, NX, NC, 16, WIDTH), BF16),
            pltpu.VMEM((16, WIDTH), F32),
            pltpu.VMEM((512, WF2_AT - QKV_AT), F32),
        ]
        + sum_scratch(dp, (8, 128))
        + [pltpu.SemaphoreType.DMA((16,)), pltpu.SemaphoreType.DMA((16,))],
        compiler_params=params(collective_id=0, has_side_effects=True),
        name="gather",
    )(points, slots, pflat, bflat)


def first_kernel(
    rel_ref, moment_ref, psmall_ref, w2_ref, w3_ref,
    ext_o, gp_o, f_o, ft_o, gram_o, fs_o, cnt_o, g_o, fw_o, pooled_o, sums_o, stats_o, wd_o,
    e_s, wn_s, w2_s,
):
    step = pl.program_id(0)

    @pl.when(step == 0)
    def _():
        gram_o[...] = jnp.zeros_like(gram_o)
        e_s[...] = token_ones()
        small = psmall_ref[...]
        forward, backward, stats = prepare_one(moment_ref[:, 0:8], small)
        wn_s[...] = forward
        wd_o[...] = backward
        stats_o[...] = stats
        w2_s[0:C1, :] = w2_ref[...]
        b2 = jnp.concatenate([small[5:6, :], small[6:7, :]], axis=1)
        w2_s[C1:, :] = low(jnp.concatenate([b2, jnp.zeros((15, C2), F32)], axis=0))

    rel = rel_ref[...]
    valid = rel[3:4, :].astype(F32)
    for j in range(TILE // 256):
        at = slice(256 * j, 256 * j + 256)
        g, gp = gelu_pair(mm_tn(wn_s[...], rel[:, at]))
        ext_o[0:C1, at] = low(g * valid[:, at])
        gp_o[:, at] = low(gp * valid[:, at])
    ext_o[C1:, :] = jnp.concatenate([rel[3:4], jnp.zeros((15, TILE), BF16)], axis=0)
    ext = ext_o[...]
    ft = low(mm_tn(w2_s[...], ext))
    f = low(mm_tn(ext, w2_s[...]))
    ft_o[...] = ft
    f_o[...] = f
    gram_o[...] += mm(ft, f)
    at = pl.ds(pl.multiple_of(step * TOK, TOK), TOK)
    fs_o[at, :] = mm(e_s[...], f)
    cnt_o[at, :] = jnp.broadcast_to(mm_nt(e_s[...], rel)[:, 3:4], (TOK, 128))

    @pl.when(step == pl.num_programs(0) - 1)
    def _():
        count = cnt_o[:, 0:1]
        fs = fs_o[...]
        pooled = low(fs / count)
        pooled_o[...] = pooled
        g = mm(pooled, w3_ref[0:C2, :])
        g_o[...] = g
        lower = w3_ref[C2:, :]
        fw = mm_exact(fs, lower)
        fw_o[...] = fw
        one = jnp.sum(fw + count * g, axis=0, keepdims=True)
        two = jnp.sum(mm_exact(gram_o[...], lower) * lower.astype(F32), axis=0, keepdims=True)
        two = two + jnp.sum(g * (2.0 * fw + count * g), axis=0, keepdims=True)
        sums_o[...] = jnp.concatenate([one, two, jnp.zeros((6, C3), F32)], axis=0)


def first_call(rel, moments, psmall, w2, w3):
    count = rel.shape[1]
    tokens = count // GROUP
    full = lambda *s: pl.BlockSpec(s, lambda i: (0, 0))
    cols = lambda r: pl.BlockSpec((r, TILE), lambda i: (0, i))
    return pl.pallas_call(
        first_kernel,
        grid=(count // TILE,),
        in_specs=[cols(8), full(8, 128), full(24, 128), full(C1, C2), full(2 * C2, C3)],
        out_specs=[
            cols(C1 + 16), cols(C1), pl.BlockSpec((TILE, C2), lambda i: (i, 0)), cols(C2),
            full(C2, C2), full(tokens, C2), full(tokens, 128), full(tokens, C3), full(tokens, C3),
            full(tokens, C2), full(8, C3), full(8, C1), full(8, C1),
        ],
        out_shape=shaped(
            ((C1 + 16, count), BF16), ((C1, count), BF16), ((count, C2), BF16), ((C2, count), BF16),
            ((C2, C2), F32), ((tokens, C2), F32), ((tokens, 128), F32), ((tokens, C3), F32),
            ((tokens, C3), F32), ((tokens, C2), BF16), ((8, C3), F32), ((8, C1), F32), ((8, C1), BF16),
        ),
        scratch_shapes=[pltpu.VMEM((TOK, TILE), BF16), pltpu.VMEM((8, C1), BF16), pltpu.VMEM((C1 + 16, C2), BF16)],
        compiler_params=params(),
        name="first",
    )(rel, moments, psmall, w2, w3)


def third_kernel(dp, sums_ref, g_ref, stats_ref, psmall_ref, gm_o, sv_o, acc, slots, send, recv):
    count = greet(all_peers(dp))
    acc[...] = sums_ref[...]
    greeted(count)
    sum_over_devices(dp, acc, slots, send, recv)
    n = stats_ref[2:3, 0:1]
    mean = acc[0:1, :] / n
    inverse = lax.rsqrt(acc[1:2, :] / n - mean * mean + EPS_NORM)
    gain = jnp.concatenate([psmall_ref[k : k + 1, :] for k in range(7, 11)], axis=1)
    shift = jnp.concatenate([psmall_ref[k : k + 1, :] for k in range(11, 15)], axis=1)
    gm_o[...] = g_ref[...] - mean
    sv_o[...] = jnp.concatenate(
        [inverse * gain, shift, mean, inverse, jnp.zeros((4, C3), F32)], axis=0
    )


def third_call(dp, sums, g, stats, psmall):
    return pl.pallas_call(
        functools.partial(third_kernel, dp),
        out_shape=shaped((g.shape, F32), ((8, C3), F32)),
        in_specs=vmem(4),
        out_specs=vmem(2),
        scratch_shapes=sum_scratch(dp, (8, C3)),
        compiler_params=params(collective_id=1, has_side_effects=True),
        name="third",
    )(sums, g, stats, psmall)


def second_kernel(f_ref, rel_ref, w3_ref, gm_ref, sv_ref, gp_o, pa_o, pg_o, pc_o, e_s):
    @pl.when(pl.program_id(0) == 0)
    def _():
        e_s[...] = token_ones()

    mask = e_s[...] * rel_ref[3:4, :]
    lower = w3_ref[C2:, :]
    scale, shift = low(sv_ref[0:1, :]), low(sv_ref[1:2, :])
    tokens = SUB // GROUP
    for j in range(TILE // SUB):
        at, ts = slice(SUB * j, SUB * j + SUB), slice(tokens * j, tokens * j + tokens)
        c = mm(f_ref[at, :], lower).reshape(tokens, GROUP, C3) + gm_ref[ts, :][:, None, :]
        c = low(c)
        g, gp = gelu_pair(c * scale[None] + shift[None])
        gc = (gp * c).reshape(SUB, C3)
        gp = gp.reshape(SUB, C3)
        gp_o[at, :] = gp
        m = mask[ts, at]
        pa_o[ts, :] = mm(m, g.reshape(SUB, C3))
        pg_o[ts, :] = mm(m, gp)
        pc_o[ts, :] = mm(m, gc)


def second_call(f, rel, w3, gm, sv):
    count = f.shape[0]
    tokens = count // GROUP
    full = lambda *s: pl.BlockSpec(s, lambda i: (0, 0))
    rows = lambda r, c: pl.BlockSpec((r, c), lambda i: (i, 0))
    return pl.pallas_call(
        second_kernel,
        grid=(count // TILE,),
        in_specs=[rows(TILE, C2), pl.BlockSpec((8, TILE), lambda i: (0, i)), full(2 * C2, C3), rows(TOK, C3), full(8, C3)],
        out_specs=[rows(TILE, C3), rows(TOK, C3), rows(TOK, C3), rows(TOK, C3)],
        out_shape=shaped(((count, C3), BF16), ((tokens, C3), F32), ((tokens, C3), F32), ((tokens, C3), F32)),
        scratch_shapes=[pltpu.VMEM((TOK, TILE), BF16)],
        compiler_params=params(),
        name="second",
    )(f, rel, w3, gm, sv)


def wide_row(ref, first, rows):
    return jnp.concatenate([ref[k : k + 1, :] for k in range(first, first + rows)], axis=1)


def layer_norm(v, gain, shift):
    centred = v - jnp.mean(v, -1, keepdims=True)
    inverse = lax.rsqrt(jnp.mean(centred * centred, -1, keepdims=True) + EPS_NORM)
    unit = centred * inverse
    return unit, inverse, low(unit * gain + shift)


def norm_back(d_unit, unit, inverse):
    return inverse * (
        d_unit - jnp.mean(d_unit, -1, keepdims=True) - unit * jnp.mean(d_unit * unit, -1, keepdims=True)
    )


def col_sum(v):
    return jnp.sum(v, axis=0, keepdims=True)


def block_kernel(
    pa_ref, pg_ref, pc_ref, cnt_ref, len_ref, cot_ref, psmall_ref, bsmall_ref, sv_ref,
    w4_ref, wqkv_ref, wo_ref, wf1_ref, wf2_ref,
    out_o, gw4_o, gwqkv_o, gwo_o, gwf1_o, gwf2_o, small_o, tok_o, tg_o, back_o,
    qkv_s, mixed_s, soft_s, dmix_s, dqkv_s,
):
    step = pl.program_id(0)

    @pl.when(step == 0)
    def _():
        for ref in (gw4_o, gwqkv_o, gwo_o, gwf1_o, gwf2_o, small_o, back_o):
            ref[...] = jnp.zeros_like(ref)

    count = cnt_ref[:, 0:1]
    scale = HEAD_DIM ** (-0.5)
    b4 = wide_row(psmall_ref, 15, 3)
    ln1_gain, ln1_shift, bo = wide_row(bsmall_ref, 0, 3), wide_row(bsmall_ref, 3, 3), wide_row(bsmall_ref, 6, 3)
    ln2_gain, ln2_shift = wide_row(bsmall_ref, 9, 3), wide_row(bsmall_ref, 12, 3)
    bf1, bf2 = wide_row(bsmall_ref, 15, 12), wide_row(bsmall_ref, 27, 3)

    act = low(pa_ref[...] / count)
    x_zero = mm(act, w4_ref[...]) + b4
    unit_a, inv_a, normed_a = layer_norm(x_zero, ln1_gain, ln1_shift)
    qkv_s[...] = low(mm(normed_a, wqkv_ref[...]))

    row_cloud = lax.broadcasted_iota(jnp.int32, (PAIR, PAIR), 0) // PATCHES
    col = lax.broadcasted_iota(jnp.int32, (PAIR, PAIR), 1)
    left = lax.broadcasted_iota(jnp.int32, (1, 128), 1) < HEAD_DIM
    zero = jnp.zeros((1, 1), BF16)

    def halves(v):
        return jnp.where(left, v, zero), jnp.where(left, zero, v)

    tiles = TB // PAIR
    for s in range(tiles):
        first = (step * tiles + s) * 2
        visible = (row_cloud == col // PATCHES) & (
            lax.rem(col, PATCHES) < jnp.where(col < PATCHES, len_ref[first], len_ref[first + 1])
        )
        rows = slice(PAIR * s, PAIR * s + PAIR)
        for p in range(HEADS // 2):
            at = 128 * p
            q = qkv_s[rows, at : at + 128]
            k = qkv_s[rows, D + at : D + at + 128]
            v = qkv_s[rows, 2 * D + at : 2 * D + at + 128]
            mixed = []
            for a, q_half in enumerate(halves(q)):
                score = jnp.where(visible, mm_nt(q_half, k) * scale, NEG_FILL)
                raised = jnp.exp(score - jnp.max(score, -1, keepdims=True))
                soft = raised / jnp.sum(raised, -1, keepdims=True)
                soft_s[(s * (HEADS // 2) + p) * 2 + a] = soft
                mixed.append(mm(low(soft), v))
            mixed_s[rows, at : at + 128] = low(jnp.where(left, mixed[0], mixed[1]))

    mixed_low = mixed_s[...]
    x_one = x_zero + mm(mixed_low, wo_ref[...]) + bo
    unit_b, inv_b, normed_b = layer_norm(x_one, ln2_gain, ln2_shift)
    hidden, d_hidden = gelu_pair(mm(normed_b, wf1_ref[...]) + bf1)
    hidden = low(hidden)
    out_o[...] = x_one + mm(hidden, wf2_ref[...]) + bf2

    cot = cot_ref[...]
    grad = low(cot)
    gwf2_o[...] += mm_tn(hidden, grad)
    d_pre = mm_nt(grad, wf2_ref[...]) * d_hidden
    d_pre_low = low(d_pre)
    gwf1_o[...] += mm_tn(normed_b, d_pre_low)
    d_normed_b = mm_nt(d_pre_low, wf1_ref[...])
    d_x_one = cot + norm_back(d_normed_b * ln2_gain, unit_b, inv_b)
    d_x_low = low(d_x_one)
    gwo_o[...] += mm_tn(mixed_low, d_x_low)
    dmix_s[...] = low(mm_nt(d_x_low, wo_ref[...]))

    for s in range(tiles):
        rows = slice(PAIR * s, PAIR * s + PAIR)
        for p in range(HEADS // 2):
            at = 128 * p
            q = qkv_s[rows, at : at + 128]
            k = qkv_s[rows, D + at : D + at + 128]
            v = qkv_s[rows, 2 * D + at : 2 * D + at + 128]
            dm = dmix_s[rows, at : at + 128]
            d_q, d_k, d_v = [], [], []
            for a, dm_half in enumerate(halves(dm)):
                soft = soft_s[(s * (HEADS // 2) + p) * 2 + a]
                d_soft = mm_nt(dm_half, v)
                d_v.append(mm_tn(low(soft), dm))
                d_score = low(soft * (d_soft - jnp.sum(soft * d_soft, -1, keepdims=True)))
                d_q.append(mm(d_score, k))
                d_k.append(mm_tn(d_score, q))
            dqkv_s[rows, at : at + 128] = low(jnp.where(left, d_q[0], d_q[1]) * scale)
            dqkv_s[rows, D + at : D + at + 128] = low(jnp.where(left, d_k[0], d_k[1]) * scale)
            dqkv_s[rows, 2 * D + at : 2 * D + at + 128] = low(jnp.where(left, d_v[0], d_v[1]))

    d_qkv = dqkv_s[...]
    gwqkv_o[...] += mm_tn(normed_a, d_qkv)
    d_normed_a = mm_nt(d_qkv, wqkv_ref[...])
    d_x_zero = d_x_one + norm_back(d_normed_a * ln1_gain, unit_a, inv_a)
    d_x_low = low(d_x_zero)
    gw4_o[...] += mm_tn(act, d_x_low)
    token = mm_nt(d_x_low, w4_ref[...]) / count
    tok_o[...] = token
    grouped = token * pg_ref[...]
    tg_o[...] = grouped
    back_o[0:1, :] += col_sum(grouped)
    back_o[1:2, :] += col_sum(token * pc_ref[...]) * sv_ref[3:4, :]
    narrow = [
        col_sum(d_normed_a * unit_a), col_sum(d_normed_a), col_sum(d_x_one),
        col_sum(d_normed_b * unit_b), col_sum(d_normed_b), col_sum(cot), col_sum(d_x_zero),
    ]
    for k, row in enumerate(narrow):
        small_o[k : k + 1, 0:D] += row
    small_o[7:8, :] += col_sum(d_pre)


def block_call(pa, pg, pc, cnt, length, cot, psmall, bsmall, sv, w4, wqkv, wo, wf1, wf2):
    tokens = pa.shape[0]
    full = lambda *s: pl.BlockSpec(s, lambda i: (0, 0))
    rows = lambda c: pl.BlockSpec((TB, c), lambda i: (i, 0))
    return pl.pallas_call(
        block_kernel,
        grid=(tokens // TB,),
        in_specs=[
            rows(C3), rows(C3), rows(C3), rows(128), pl.BlockSpec(memory_space=pltpu.SMEM), rows(D),
            full(24, 128), full(32, 128), full(8, C3),
            full(C3, D), full(D, 3 * D), full(D, D), full(D, FF), full(FF, D),
        ],
        out_specs=[
            rows(D), full(C3, D), full(D, 3 * D), full(D, D), full(D, FF), full(FF, D), full(8, FF),
            rows(C3), rows(C3), full(8, C3),
        ],
        out_shape=shaped(
            ((tokens, D), F32), ((C3, D), F32), ((D, 3 * D), F32), ((D, D), F32), ((D, FF), F32),
            ((FF, D), F32), ((8, FF), F32), ((tokens, C3), F32), ((tokens, C3), F32), ((8, C3), F32),
        ),
        scratch_shapes=[
            pltpu.VMEM((TB, 3 * D), BF16), pltpu.VMEM((TB, D), BF16),
            pltpu.VMEM((TB // PAIR * HEADS, PAIR, PAIR), F32), pltpu.VMEM((TB, D), BF16),
            pltpu.VMEM((TB, 3 * D), BF16),
        ],
        compiler_params=params(),
        name="block",
    )(pa, pg, pc, cnt, length, cot, psmall, bsmall, sv, w4, wqkv, wo, wf1, wf2)


def third_back_kernel(
    dp, back_ref, tok_ref, tg_ref, fs_ref, fw_ref, gm_ref, cnt_ref, pooled_ref, gram_ref, w3_ref, sv_ref, stats_ref,
    tot_o, tok_o, kap_o, k_o, ws_o, top_o, corr_o, acc, slots, send, recv,
):
    greeting = greet(all_peers(dp))
    acc[...] = back_ref[...]
    tok_o[...] = low(tok_ref[...])
    lower = w3_ref[C2:, :].astype(F32)
    gain = sv_ref[0:1, :]
    ws_o[...] = low(lower * gain)
    greeted(greeting)
    sum_over_devices(dp, acc, slots, send, recv)
    tot_o[...] = acc[...]
    n = stats_ref[2:3, 0:1]
    alpha = gain * acc[0:1, :] / n
    beta = gain * acc[1:2, :] * sv_ref[3:4, :] / n
    count = cnt_ref[:, 0:1]
    gm = gm_ref[...]
    per_token = low(gain * tg_ref[...] - (count * alpha + beta * (fw_ref[...] + count * gm)))
    d_pooled = mm_nt(per_token, w3_ref[0:C2, :])
    shifted = low(alpha + beta * gm)
    kap_o[...] = d_pooled / count - mm_nt(shifted, w3_ref[C2:, :])
    k_o[...] = low(-mm_nt(low(lower * beta), w3_ref[C2:, :]))
    top_o[...] = mm_tn(pooled_ref[...], per_token)
    corr_o[...] = mm_tn(low(fs_ref[...]), shifted) + beta * mm(low(gram_ref[...]), w3_ref[C2:, :])


def third_back_call(dp, back, tok, tg, fs, fw, gm, cnt, pooled, gram, w3, sv, stats):
    tokens = tok.shape[0]
    outs = shaped(
        ((8, C3), F32), ((tokens, C3), BF16), ((tokens, C2), F32), ((C2, C2), BF16), ((C2, C3), BF16),
        ((C2, C3), F32), ((C2, C3), F32),
    )
    return pl.pallas_call(
        functools.partial(third_back_kernel, dp),
        out_shape=outs,
        in_specs=vmem(12),
        out_specs=vmem(len(outs)),
        scratch_shapes=sum_scratch(dp, (8, C3)),
        compiler_params=params(collective_id=2, has_side_effects=True),
        name="third_back",
    )(back, tok, tg, fs, fw, gm, cnt, pooled, gram, w3, sv, stats)


def last_kernel(
    gp_ref, f_ref, ft_ref, ext_ref, gp1_ref, rel_ref, tok_ref, kap_ref, k_ref, ws_ref, w2_ref, wd_ref,
    h_o, gw2_o, q_o, d_o, dn_s,
):
    @pl.when(pl.program_id(0) == 0)
    def _():
        for ref in (h_o, gw2_o, q_o):
            ref[...] = jnp.zeros_like(ref)

    tokens = SUB // GROUP
    for j in range(TILE // SUB):
        at, ts = slice(SUB * j, SUB * j + SUB), slice(tokens * j, tokens * j + tokens)
        gp = gp_ref[at, :].reshape(tokens, GROUP, C3)
        dn_s[at, :] = (gp * tok_ref[ts, :][:, None, :]).reshape(SUB, C3)
    dn = dn_s[...]
    h_o[...] += mm(ft_ref[...], dn)
    d_feat = mm_nt(dn, ws_ref[...]) + mm(f_ref[...], k_ref[...])
    d_feat = (d_feat.reshape(TOK, GROUP, C2) + kap_ref[...][:, None, :]).reshape(TILE, C2)
    d_feat = low(d_feat)
    gw2_o[...] += mm(ext_ref[...], d_feat)
    d_one = low(mm_nt(w2_ref[...], d_feat) * gp1_ref[...].astype(F32))
    d_o[...] = mm(wd_ref[...], d_one)
    q_o[...] += mm_nt(rel_ref[...], d_one)


def last_call(gp, f, ft, ext, gp1, rel, tok, kap, k, ws, w2, wd):
    count = f.shape[0]
    full = lambda *s: pl.BlockSpec(s, lambda i: (0, 0))
    rows = lambda r, c: pl.BlockSpec((r, c), lambda i: (i, 0))
    cols = lambda r: pl.BlockSpec((r, TILE), lambda i: (0, i))
    return pl.pallas_call(
        last_kernel,
        grid=(count // TILE,),
        in_specs=[
            rows(TILE, C3), rows(TILE, C2), cols(C2), cols(C1 + 16), cols(C1), cols(8), rows(TOK, C3), rows(TOK, C2),
            full(C2, C2), full(C2, C3), full(C1, C2), full(8, C1),
        ],
        out_specs=[full(C2, C3), full(C1 + 16, C2), full(8, C1), cols(8)],
        out_shape=shaped(((C2, C3), F32), ((C1 + 16, C2), F32), ((8, C1), F32), ((8, count), F32)),
        scratch_shapes=[pltpu.VMEM((TILE, C3), BF16)],
        compiler_params=params(),
        name="last",
    )(gp, f, ft, ext, gp1, rel, tok, kap, k, ws, w2, wd)


def first_grads(q, moments, psmall, stats):
    mean, inverse, n, scale = stats[0:1], stats[1:2], stats[2:3], stats[3:4]
    w = [psmall[k : k + 1, :] for k in range(3)]
    one = q[3:4, :]
    two = inverse * (sum(w[k] * q[k : k + 1, :] for k in range(3)) - mean * one)
    grad_w = []
    for k in range(3):
        along = sum(w[j] * moments[k : k + 1, j : j + 1] for j in range(3)) - mean * moments[k : k + 1, 3:4]
        grad_w.append(scale * (q[k : k + 1, :] - (one * moments[k : k + 1, 3:4] + two * inverse * along) / n))
    flat = [
        jnp.sum(scale * w[k] * (one - two * inverse * mean) / n, axis=1, keepdims=True) for k in range(3)
    ]
    slope = [
        [jnp.sum(scale * w[k] * two * inverse * w[j] / n, axis=1, keepdims=True) for j in range(3)]
        for k in range(3)
    ]
    return grad_w, two, one, flat, slope


def point_gradient(d_ref, rel_ref, slots_ref, flat, slope, out_ref):
    ones = patch_ones()
    lane = lax.rem(lax.broadcasted_iota(jnp.int32, (1, 256), 1), GROUP)
    base = jnp.concatenate(flat, axis=0)
    columns = [jnp.concatenate([slope[k][j] for k in range(3)], axis=0) for j in range(3)]

    def piece(i, carry):
        at = pl.ds(pl.multiple_of(i * 256, 256), 256)
        rel = rel_ref[:, at].astype(F32)
        d = d_ref[:, at]
        out = d[0:3] + d[4:7] - rel[3:4] * base
        for j in range(3):
            out = out - columns[j] * rel[j : j + 1]
        pick = (lane == slots_ref[1:2, at]).astype(F32)
        out_ref[:, at] = out - pick * patch_sum(out, ones)
        return carry

    lax.fori_loop(0, d_ref.shape[1] // 256, piece, 0, unroll=8)


def point_small_rows(grad_w, gain1, shift1, b2, tot, b4):
    rows = list(grad_w) + [gain1, shift1]
    rows += [b2[:, 128 * k : 128 * k + 128] for k in range(2)]
    rows += [tot[1:2, 128 * k : 128 * k + 128] for k in range(4)]
    rows += [tot[0:1, 128 * k : 128 * k + 128] for k in range(4)]
    rows += [b4[:, 128 * k : 128 * k + 128] for k in range(3)]
    return jnp.concatenate(rows, axis=0)


def block_small_rows(small_ref):
    rows = [small_ref[k : k + 1, 128 * j : 128 * j + 128] for k in range(5) for j in range(3)]
    rows += [small_ref[7:8, 128 * j : 128 * j + 128] for j in range(12)]
    rows += [small_ref[5:6, 128 * j : 128 * j + 128] for j in range(3)]
    return jnp.concatenate(rows, axis=0)


def scatter_kernel(
    q_ref, moment_ref, psmall_ref, stats_ref, tot_ref, small_ref, d_ref, rel_ref, slots_ref,
    gw2_ref, top_ref, h_ref, corr_ref, sv_ref, gw4_ref, gwqkv_ref, gwo_ref, gwf1_ref, gwf2_ref,
    pg_o, pflat_o, bflat_o,
    blocks, stage, land1, land2, land3, land4, acc, slots, ssend, srecv, gsend, grecv,
):
    z, y, x, core = where_am_i()
    dp = NZ * NY * NX
    near = [(chip(lax.rem(z + k, NZ), y, x), core) for k in range(1, NZ)]
    over_y, over_x, twin = (chip(z, 1 - y, x), core), (chip(z, y, 1 - x), core), (chip(z, y, x), 1 - core)
    count = greet(all_peers(dp) + near + [over_y, over_x, twin])
    acc[...] = q_ref[...]
    greeted(count)
    small = sum_start(dp, False, acc, slots, ssend, srecv)

    none = jnp.zeros((1, 128), F32)
    prow = point_small_rows(
        [none] * 3, none, none, gw2_ref[C1 : C1 + 1, :], jnp.zeros((8, C3), F32), small_ref[6:7, 0:D]
    )
    brow = block_small_rows(small_ref)
    stage[...] = jnp.zeros_like(stage)
    gain = sv_ref[0:1, :]
    for d in range(dp * NC):
        cz, cy, cx, cc = d // 8, d // 4 % 2, d // 2 % 2, d % 2
        if d < 16:
            stage[:, W3_AT : W3_AT + C3] = top_ref[16 * d : 16 * d + 16, :]
        else:
            rows = slice(16 * (d - 16), 16 * (d - 16) + 16)
            stage[:, W3_AT : W3_AT + C3] = h_ref[rows, :] * gain - corr_ref[rows, :]
        stage[:, W4_AT : W4_AT + D] = gw4_ref[16 * d : 16 * d + 16, :]
        stage[0:12, QKV_AT : QKV_AT + 3 * D] = gwqkv_ref[12 * d : 12 * d + 12, :]
        stage[0:12, WO_AT : WO_AT + D] = gwo_ref[12 * d : 12 * d + 12, :]
        stage[0:12, WF1_AT : WF1_AT + FF] = gwf1_ref[12 * d : 12 * d + 12, :]
        stage[12:16, W2_AT : W2_AT + C2] = gw2_ref[4 * d : 4 * d + 4, :]
        stage[12:13, PSMALL_AT : PSMALL_AT + 128] = piece_of(prow, 72 * d, 72)
        stage[12:13, BSMALL_AT : BSMALL_AT + 128] = piece_of(brow, 120 * d, 120)
        for b in range(3):
            at = 48 * d + 16 * b
            stage[:, WF2_AT + D * b : WF2_AT + D * b + D] = gwf2_ref[at : at + 16, :]
        blocks[cc, cz, cy, cx] = low(stage[...])

    used = [0]

    def send(src, dst, peer):
        k = used[0]
        used[0] += 1
        copy = pltpu.make_async_remote_copy(
            src_ref=src, dst_ref=dst, send_sem=gsend.at[k], recv_sem=grecv.at[k],
            device_id=peer, device_id_type=MESH,
        )
        copy.start()
        return copy

    one, two = pl.ds(0, HALF), pl.ds(HALF, HALF)
    mine = blocks.at[core]
    live = [send(blocks.at[1 - core], land1, twin)]
    sum_finish(dp, False, acc, slots, small)
    small = sum_start(dp, True, acc, slots, ssend, srecv)
    for copy in live:
        copy.wait()

    def add(dst, index, landed):
        dst[index] = low(dst[index].astype(F32) + landed.astype(F32))

    for cz in range(NZ):
        for cy in range(NY):
            for cx in range(NX):
                add(mine, (cz, cy, cx), land1[cz, cy, cx])
    live = [
        send(mine.at[:, :, 1 - x, :, one], land2.at[0], over_x),
        send(mine.at[:, 1 - y, :, :, two], land2.at[1], over_y),
    ]
    sum_finish(dp, True, acc, slots, small)
    totals = acc[...]
    moments = moment_ref[...]
    grad_w, gain1, shift1, flat, slope = first_grads(totals, moments, psmall_ref[...], stats_ref[...])
    for copy in live:
        copy.wait()
    for cz in range(NZ):
        for k in range(2):
            add(mine, (cz, k, x, slice(None), one), land2[0, cz, k])
            add(mine, (cz, y, k, slice(None), two), land2[1, cz, k])
    live = [
        send(mine.at[:, 1 - y, x, :, one], land3.at[0], over_y),
        send(mine.at[:, y, 1 - x, :, two], land3.at[1], over_x),
    ]
    point_gradient(d_ref, rel_ref, slots_ref, flat, slope, pg_o)
    for copy in live:
        copy.wait()
    for cz in range(NZ):
        add(mine, (cz, y, x, slice(None), one), land3[0, cz])
        add(mine, (cz, y, x, slice(None), two), land3[1, cz])
    live = [
        send(mine.at[lax.rem(z + k, NZ), y, x], land4.at[k - 1], near[k - 1]) for k in range(1, NZ)
    ]
    for copy in live:
        copy.wait()
    total = mine[z, y, x].astype(F32)
    for k in range(NZ - 1):
        total = total + land4[k].astype(F32)
    stage[...] = total

    full_rows = point_small_rows(grad_w, gain1, shift1, jnp.zeros((1, C2), F32), tot_ref[...], jnp.zeros((1, D), F32))
    rank = chip(z, y, x) * NC + core
    lane = lax.broadcasted_iota(jnp.int32, (1, 128), 1)
    own = jnp.zeros((1, 128), F32)
    for d in range(dp * NC):
        own = own + jnp.where(rank == d, piece_of(full_rows, 72 * d, 72), 0.0)
    pflat_o[0:1, :] = stage[12:13, PSMALL_AT : PSMALL_AT + 128] + own
    bflat_o[0:1, :] = stage[12:13, BSMALL_AT : BSMALL_AT + 128]
    for at, start, rows, cols, under in (
        (W3_AT, 9, 16, C3, 0), (W4_AT, 73, 16, D, 0), (W2_AT, 1, 4, C2, 12),
    ):
        for j in range(cols // 128):
            pflat_o[pl.ds(start + j, rows, stride=cols // 128), :] = stage[
                under : under + rows, at + 128 * j : at + 128 * j + 128
            ]
    start = 1
    for at, cols in rows_twelve():
        for j in range(cols // 128):
            bflat_o[pl.ds(start + j, 12, stride=cols // 128), :] = stage[
                0:12, at + 128 * j : at + 128 * j + 128
            ]
        start += 12 * cols // 128
    for b in range(3):
        for j in range(D // 128):
            at = WF2_AT + D * b + 128 * j
            bflat_o[pl.ds(start + 48 * b + j, 16, stride=3), :] = stage[:, at : at + 128]


def scatter_call(*args):
    dp = NZ * NY * NX
    count = args[7].shape[1]
    outs = shaped(((3, count), F32), ((PROWS, 128), F32), ((BROWS, 128), F32))
    return pl.pallas_call(
        scatter_kernel,
        out_shape=outs,
        in_specs=vmem(len(args)),
        out_specs=vmem(len(outs)),
        scratch_shapes=[
            pltpu.VMEM((NC, NZ, NY, NX, 16, WIDTH), BF16),
            pltpu.VMEM((16, WIDTH), F32),
            pltpu.VMEM((NZ, NY, NX, 16, WIDTH), BF16),
            pltpu.VMEM((2, NZ, 2, 16, HALF), BF16),
            pltpu.VMEM((2, NZ, 16, HALF), BF16),
            pltpu.VMEM((NZ - 1, 16, WIDTH), BF16),
        ]
        + sum_scratch(dp, (8, 128))
        + [pltpu.SemaphoreType.DMA((16,)), pltpu.SemaphoreType.DMA((16,))],
        compiler_params=params(collective_id=3, has_side_effects=True),
        name="scatter",
    )(*args)


def geometry_call(points, slots):
    outs = shaped(((8, points.shape[1]), BF16), ((8, 128), F32))
    return pl.pallas_call(
        geometry, out_shape=outs, in_specs=vmem(2), out_specs=vmem(2),
        compiler_params=params(), name="geometry",
    )(points, slots)


def gather_plain(points, slots, point_master, block_master, devices):
    rel, moments = geometry_call(points, slots)
    moments = lax.psum(moments, AXES)
    tables = []
    for master, layout in ((point_master, point_layout()), (block_master, block_layout())):
        offset = 0
        parts = []
        for segment, seg_len in zip(layout, segment_lengths(layout, devices)):
            piece = master[offset : offset + seg_len // devices].astype(BF16)
            offset += seg_len // devices
            parts.append(lax.all_gather(piece, AXES, axis=0, tiled=True))
        tables.append(parts)
    (ps, w2, w3, w4), (bs, wqkv, wo, wf1, wf2) = tables

    def rows_of(v, rows, used):
        v = v[:used].astype(F32).reshape(-1, 128)
        return jnp.concatenate([v, jnp.zeros((rows - v.shape[0], 128), F32)], axis=0)

    return (
        rel, moments, rows_of(ps, 24, 18 * 128), rows_of(bs, 32, 30 * 128),
        w2.reshape(C1, C2), w3.reshape(2 * C2, C3), w4.reshape(C3, D),
        wqkv.reshape(D, 3 * D), wo.reshape(D, D), wf1.reshape(D, FF), wf2.reshape(FF, D),
    )


def point_gradient_kernel(d_ref, rel_ref, slots_ref, table_ref, out_ref):
    flat = [table_ref[k : k + 1, 3:4] for k in range(3)]
    slope = [[table_ref[k : k + 1, j : j + 1] for j in range(3)] for k in range(3)]
    point_gradient(d_ref, rel_ref, slots_ref, flat, slope, out_ref)


def scatter_plain(
    devices, q, moments, psmall, stats, tot, small, d, rel, slots,
    gw2, top, h, corr, sv, gw4, gwqkv, gwo, gwf1, gwf2,
):
    q = lax.psum(q, AXES)
    grad_w, gain1, shift1, flat, slope = first_grads(q, moments, psmall, stats)
    table = jnp.concatenate([jnp.concatenate(slope[k] + [flat[k]], axis=1) for k in range(3)], axis=0)
    table = jnp.pad(table, ((0, 5), (0, 124)))
    point_grad = pl.pallas_call(
        point_gradient_kernel, out_shape=jax.ShapeDtypeStruct((3, d.shape[1]), F32),
        in_specs=vmem(4), out_specs=vmem(1)[0], compiler_params=params(), name="point_gradient",
    )(d, rel, slots, table)
    none = jnp.zeros((1, 128), F32)
    local = point_small_rows(
        [none] * 3, none, none, gw2[C1 : C1 + 1, :], jnp.zeros((8, C3), F32), small[6:7, 0:D]
    )
    known = point_small_rows(grad_w, gain1, shift1, jnp.zeros((1, C2), F32), tot, jnp.zeros((1, D), F32))
    w3 = jnp.concatenate([top, h * sv[0:1, :] - corr], axis=0)
    pieces = []
    for layout, tables in (
        (point_layout(), (local + known / devices, gw2[:C1], w3, gw4)),
        (block_layout(), (block_small_rows(small), gwqkv, gwo, gwf1, gwf2)),
    ):
        parts = []
        for values, seg_len in zip(tables, segment_lengths(layout, devices)):
            values = values.reshape(-1)
            values = jnp.concatenate([values, jnp.zeros((seg_len - values.shape[0],), F32)])
            parts.append(lax.psum_scatter(values, AXES, scatter_dimension=0, tiled=True))
        pieces.append(parts)
    return point_grad, pieces[0], pieces[1]


def adam_update(master, moment_one, moment_two, gradient, step_rates, decays):
    one_new = BETA_ONE * moment_one + (1.0 - BETA_ONE) * gradient
    two_new = BETA_TWO * moment_two + (1.0 - BETA_TWO) * gradient * gradient
    fix_one = 1.0 - BETA_ONE**STEP
    fix_two = 1.0 - BETA_TWO**STEP
    direction = one_new / fix_one / (jnp.sqrt(two_new / fix_two) + ADAM_EPS)
    master_new = master - step_rates * (direction + decays * master)
    return (master_new, one_new, two_new)


def flat_of(vector, small, rows):
    pad = jnp.zeros((128 - small,), F32)
    tail = jnp.zeros((rows * 128 - 128 - (vector.shape[0] - small),), F32)
    return jnp.concatenate([vector[:small], pad, vector[small:], tail]).reshape(rows, 128)


def on_device(
    points, point_count, centre_slot, cloud_length, cotangent, point_master, block_master,
    point_first, block_first, point_second, block_second,
):
    dp, fsdp = lax.axis_size("dp"), lax.axis_size("fsdp")
    devices = dp * fsdp
    own_rank = lax.axis_index(AXES)
    known = dp == NZ * NY * NX and fsdp == NC
    slots = jnp.repeat(jnp.stack([point_count, centre_slot]), GROUP, axis=1)
    if known:
        gathered = gather_call(
            points, slots, flat_of(point_master, 72, PROWS), flat_of(block_master, 120, BROWS)
        )
    else:
        gathered = gather_plain(points, slots, point_master, block_master, devices)
    rel, moments, psmall, bsmall, w2, w3, w4, wqkv, wo, wf1, wf2 = gathered
    ext, gp1, f, ft, gram, fs, cnt, g, fw, pooled, sums, stats, wd = first_call(rel, moments, psmall, w2, w3)
    gm, sv = third_call(dp, sums, g, stats, psmall)
    gp, pa, pg, pc = second_call(f, rel, w3, gm, sv)
    tokens_out, gw4, gwqkv, gwo, gwf1, gwf2, small, tok, tg, back = block_call(
        pa, pg, pc, cnt, cloud_length, cotangent, psmall, bsmall, sv, w4, wqkv, wo, wf1, wf2
    )
    tot, tok_low, kap, k, ws, top, corr = third_back_call(
        dp, back, tok, tg, fs, fw, gm, cnt, pooled, gram, w3, sv, stats
    )
    h, gw2, q, d = last_call(gp, f, ft, ext, gp1, rel, tok_low, kap, k, ws, w2, wd)
    grads = (
        q, moments, psmall, stats, tot, small, d, rel, slots,
        gw2, top, h, corr, sv, gw4, gwqkv, gwo, gwf1, gwf2,
    )
    if known:
        point_grad, pflat, bflat = scatter_call(*grads)
        pflat, bflat = pflat.reshape(-1), bflat.reshape(-1)
        block_small = bflat[:120]
        point_gradient_vec = jnp.concatenate([pflat[:72], pflat[128 : 128 + point_master.shape[0] - 72]])
        block_gradient = jnp.concatenate([block_small, bflat[128 : 128 + block_master.shape[0] - 120]])
    else:
        point_grad, point_parts, block_parts = scatter_plain(devices, *grads)
        block_small = block_parts[0]
        point_gradient_vec = jnp.concatenate(point_parts)
        block_gradient = jnp.concatenate(block_parts)
    point_rates, point_decays = shard_rates(point_layout(), devices, own_rank)
    block_rates, block_decays = shard_rates(block_layout(), devices, own_rank)
    point_new, point_one, point_two = adam_update(
        point_master, point_first, point_second, point_gradient_vec, point_rates, point_decays
    )
    block_new, block_one, block_two = adam_update(
        block_master, block_first, block_second, block_gradient, block_rates, block_decays
    )
    return (
        tokens_out, point_grad, point_new, block_new, point_one, block_one, point_two, block_two,
        point_new.astype(BF16), block_new.astype(BF16), block_small,
    )


def solution(mesh):
    split = P(AXES)
    return jax.shard_map(
        on_device,
        mesh=mesh,
        in_specs=(P(None, AXES), split, split, split, P(AXES, None)) + (split,) * 6,
        out_specs=(P(AXES, None), P(None, AXES)) + (split,) * 9,
        check_vma=False,
    )
```

time: 1070 us -> 257 us (0.24)
  blocking collectives: 443 us -> 0 us
  Pallas kernels: 0 us -> 237 us
  matrix products: 205 us -> 0 us
  waiting for transfers between devices: 144 us -> 0 us
  local copies, waits for them, and re-layouts: 142 us -> 15.7 us
  other arithmetic: 111 us -> 2.73 us
  between operations: 16.3 us -> 0.94 us
    pallas_call x0 -> x8, Pallas kernels: none -> 237 us  [the longest x1 52.5 us: scatter_call(): pl.pallas_call(scatter_kernel, out_shape=outs, in_specs=vmem(len(args)),...]
    dot_general x35 -> x0, matrix products: 205 us -> none  [the longest x7 80.8 us: back_product(): lax.dot_general(left_mat, right_mat, (((1,), (1,)), ((), ())), preferred_...]
    all_gather x5 -> x0, blocking collectives: 199 us -> none  [the longest x1 43.3 us: on_device(): lax.all_gather(block_pieces[1], ('dp', 'fsdp'), axis=0, tiled=True)]
    psum x4 -> x0, blocking collectives: 159 us -> none  [the longest x2 80.3 us: global_back(): return lax.psum((local_terms[0], local_terms[1]), ('dp', 'fsdp'))]
    unnamed x4 -> x0, waiting for transfers between devices: 144 us -> none
    unnamed x2 -> x0, blocking collectives: 84.1 us -> none
    convert_element_type x22 -> x2, other arithmetic: 76.6 us -> 1.91 us  [the longest x1 1.11 us: on_device(): block_new.astype(BF16)]
    convert_element_type x6 -> x0, local copies, waits for them, and re-layouts: 37.4 us -> none  [the longest x1 26.6 us: on_device(): act_three = jax.nn.gelu(norm_three).astype(jnp.bfloat16)]
  transfers between devices with their start and end apart: 3 -> 0, of which waited for: 1 -> 0; matrix products, arithmetic and copies ran while one was open for 20% -> 0% of each run, Pallas kernels for 0% -> 0%
where the time goes in v1:
time: 257 us
  Pallas kernels  237 us (92%)
  local copies, waits for them, and re-layouts  15.7 us (6%)
  other arithmetic  2.73 us (1%)
    pallas_call x1, Pallas kernels, scatter_call(): pl.pallas_call(scatter_kernel, out_shape=outs, in_specs=vmem(len(args)),...  52.5 us
    pallas_call x1, Pallas kernels, gather_call(): pl.pallas_call(gather_kernel, out_shape=outs, in_specs=vmem(4), out_specs...  52 us
    pallas_call x1, Pallas kernels, block_call(): pl.pallas_call(block_kernel, grid=(tokens // TB,), in_specs=[rows(C3), ro...  30.5 us
    pallas_call x1, Pallas kernels, last_call(): pl.pallas_call(last_kernel, grid=(count // TILE,), in_specs=[rows(TILE, C...  30.4 us
    pallas_call x1, Pallas kernels, second_call(): pl.pallas_call(second_kernel, grid=(count // TILE,), in_specs=[rows(TILE,...  24 us
    pallas_call x1, Pallas kernels, first_call(): pl.pallas_call(first_kernel, grid=(count // TILE,), in_specs=[cols(8), fu...  22 us
    pallas_call x1, Pallas kernels, third_back_call(): pl.pallas_call(functools.partial(third_back_kernel, dp), out_shape=outs,...  14 us
    pallas_call x1, Pallas kernels, third_call(): pl.pallas_call(functools.partial(third_kernel, dp), out_shape=shaped((g.s...  11.7 us

profile of v1, /device:TPU:0, one launch (start us, length us, event | category | flops | bytes accessed | tf_op | source)
XLA Modules:
  0.0 256.5 jit_solution(1791574678899956103)
XLA Ops:
  0.6 0.7 pad_add_fusion
  1.4 0.2 broadcast_in_dim.94
  1.5 1.0 reshape.39.slots_ref
  2.5 1.0 slice.33
  3.6 0.7 slice.32
  4.3 3.5 %concatenate.25 = f32[56320]{0:T(1024)} concatenate(f32[120]{0:T(128)S(1)} %slice.32, f32[8]{0:T(128)S(1)} %broadcast.75, f32[55296]{0:T(1024)S(1)} %slice.33, f32[896]{0:T(1024)S(1)} %broadcast.74), dimensions={0} | concatenate | bytes 450560 | tf_op jit(solution)/shard_map/concatenate | solution.py:1176
  7.7 0.9 slice.31
  8.7 0.7 slice.30
  9.4 0.7 concatenate.24
  10.1 52.0 %gather.1 = (bf16[8,16384]{1,0:T(8,128)(2,1)}, f32[8,128]{1,0:T(8,128)}, f32[24,128]{1,0:T(8,128)}, f32[32,128]{1,0:T(8,128)}, bf16[128,256]{1,0:T(8,128)(2,1)},...) custom-call(f32[3,16384]{1,0:T(4,128)} %points_ref.1, ...), custom_call_target="tpu_custom_call" | custom-call | tf_op jit(solution)/shard_map/gather/pallas_call | solution.py:464
  62.1 22.0 %first.1 = (bf16[144,16384]{1,0:T(8,128)(2,1)}, bf16[128,16384]{1,0:T(8,128)(2,1)}, bf16[16384,256]{1,0:T(8,128)(2,1)}, bf16[256,16384]{1,0:T(8,128)(2,1)}, f32[...) custom-call(bf16[8,16384]{1,0:T(8,128)(2,1)} %get-tuple-element.65.r, ...), custom_call_target="tpu_custom_call" | custom-call | tf_op jit(solution)/shard_map/first/pallas_call | solution.py:541
  84.1 11.7 %third.1 = (f32[512,512]{1,0:T(8,128)}, f32[8,512]{1,0:T(8,128)}) custom-call(f32[8,512]{1,0:T(8,128)} %get-tuple-element.71.sums_ref, f32[512,512]{1,0:T(8,128)} %get-tuple-element.72.g_ref, f32[8,128]{1,0:T(8,128)} %get-tuple-element.73.stats_ref, f32[24,128]{1,0:T(8,128)} %get-tuple-element.67.psmall_ref), custom_call_target="tpu_custom_call" | custom-call | tf_op jit(solution)/shard_map/third/pallas_call | solution.py:578
  95.8 24.0 %second.1 = (bf16[16384,512]{1,0:T(8,128)(2,1)}, f32[512,512]{1,0:T(8,128)}, f32[512,512]{1,0:T(8,128)}, f32[512,512]{1,0:T(8,128)}) custom-call(bf16[16384,256]{1,0:T(8,128)(2,1)} %get-tuple-element.70.f_ref, bf16[8,16384]{1,0:T(8,128)(2,1)} %get-tuple-element.65.rel_ref, bf16[512,512]{1,0:T(8,128)(2,1)} %get-tuple-element.69.w3_ref, ...), custom_call_target="tpu_custom_call" | custom-call | tf_op jit(solution)/shard_map/second/pallas_call | solution.py:617
  119.8 30.5 %block.1 = (f32[512,384]{1,0:T(8,128)}, f32[512,384]{1,0:T(8,128)}, f32[384,1152]{1,0:T(8,128)}, f32[384,384]{1,0:T(8,128)}, f32[384,1536]{1,0:T(8,128)}, /*inde...) custom-call(f32[512,512]{1,0:T(8,128)} %get-tuple-element.76.pa_ref, ...), custom_call_target="tpu_custom_call" | custom-call | tf_op jit(solution)/shard_map/block/pallas_call | solution.py:768
  150.3 14.0 %third_back.1 = (f32[8,512]{1,0:T(8,128)}, bf16[512,512]{1,0:T(8,128)(2,1)}, f32[512,256]{1,0:T(8,128)}, bf16[256,256]{1,0:T(8,128)(2,1)}, bf16[256,512]{1,0:T(8...) custom-call(f32[8,512]{1,0:T(8,128)} %get-tuple-element.91.back_ref, f32[512,512]{1,0:T(8,128)} %get-tuple-element.92.tok_ref, ...), custom_call_target="tpu_custom_call" | custom-call | tf_op jit(solution)/shard_map/third_back/pallas_call | solution.py:827
  164.3 30.4 %last.1 = (f32[256,512]{1,0:T(8,128)}, f32[144,256]{1,0:T(8,128)}, f32[8,128]{1,0:T(8,128)}, f32[8,16384]{1,0:T(8,128)}) custom-call(bf16[16384,512]{1,0:T(8,128)(2,1)} %get-tuple-element.87.gp_ref, bf16[16384,256]{1,0:T(8,128)(2,1)} %get-tuple-element.70.f_ref, bf16[256,16384]{1,0:T(8,128)(2,1)} %get-tuple-element.88.ft_ref, ...), custom_call_target="tpu_custom_call" | custom-call | tf_op jit(solution)/shard_map/last/pallas_call | solution.py:868
  194.7 0.0 copy-start
  194.7 0.0 copy-start.3
  194.7 0.0 copy-start.4
  194.7 52.5 %scatter.1 = (f32[3,16384]{1,0:T(4,128)}, f32[128,128]{1,0:T(8,128)}, f32[440,128]{1,0:T(8,128)}) custom-call(f32[8,128]{1,0:T(8,128)} %get-tuple-element.103.q_ref, f32[8,128]{1,0:T(8,128)} %get-tuple-element.66.moment_ref, f32[24,128]{1,0:T(8,128)} %get-tuple-element.67.psmall_ref, f32[8,128]{1,0:T(8,128)} %get-tuple-element.73.stats_ref, ...), custom_call_target="tpu_custom_call" | custom-call | tf_op jit(solution)/shard_map/scatter/pallas_call | solution.py:1072
  247.3 0.0 copy-start.2
  247.3 0.0 copy-start.5
  247.3 0.0 copy-start.6
  247.3 0.0 copy-start.1
  247.3 1.0 slice_bitcast_fusion
  248.4 0.7 slice.41
  249.0 0.0 copy-start.7
  249.2 1.4 concatenate.29
  250.6 1.4 concatenate.31
  252.1 0.0 copy-done
  252.1 0.0 copy-done.3
  252.1 0.0 copy-done.4
  252.1 1.1 fusion.20
  253.2 0.8 slice_bitcast_fusion.1
  254.1 0.7 slice.40
  254.8 0.1 concatenate.26
  254.9 0.1 concatenate.28
  255.0 0.0 copy-done.2
  255.0 0.0 copy-done.5
  255.0 0.0 copy-done.6
  255.0 0.8 fusion.22
  255.8 0.0 copy-done.1
  255.8 0.7 copy.23
  256.5 0.0 copy-done.7
  (13 shorter events, 0.1 us)
Async XLA Ops:
  194.7 57.4 %copy-start = (f32[55416]{0:T(1024)S(1)}, f32[55416]{0:T(1024)}, u32[]{:S(2)}) copy-start(f32[55416]{0:T(1024)} %param.17) | copy-start | bytes 664996
  194.7 57.4 %copy-start.3 = (f32[55416]{0:T(1024)S(1)}, f32[55416]{0:T(1024)}, u32[]{:S(2)}) copy-start(f32[55416]{0:T(1024)} %param.19) | copy-start | bytes 664996
  194.7 57.4 %copy-start.4 = (f32[55416]{0:T(1024)S(1)}, f32[55416]{0:T(1024)}, u32[]{:S(2)}) copy-start(f32[55416]{0:T(1024)} %param.21) | copy-start | bytes 664996
  247.3 7.7 %copy-start.2 = (f32[15432]{0:T(1024)S(1)}, f32[15432]{0:T(1024)}, u32[]{:S(2)}) copy-start(f32[15432]{0:T(1024)} %param.16) | copy-start | bytes 185188
  247.3 7.7 %copy-start.5 = (f32[15432]{0:T(1024)S(1)}, f32[15432]{0:T(1024)}, u32[]{:S(2)}) copy-start(f32[15432]{0:T(1024)} %param.18) | copy-start | bytes 185188
  247.3 7.7 %copy-start.6 = (f32[15432]{0:T(1024)S(1)}, f32[15432]{0:T(1024)}, u32[]{:S(2)}) copy-start(f32[15432]{0:T(1024)} %param.20) | copy-start | bytes 185188
  247.3 8.5 %copy-start.1 = (f32[3,16384]{1,0:T(4,128)S(1)}, f32[3,16384]{1,0:T(4,128)}, u32[]{:S(2)}) copy-start(f32[3,16384]{1,0:T(4,128)} %get-tuple-element.153) | copy-start | bytes 589828
  249.0 7.5 %copy-start.7 = (f32[120]{0:T(128)}, f32[120]{0:T(128)S(1)}, u32[]{:S(2)}) copy-start(f32[120]{0:T(128)S(1)} %slice.41) | copy-start | bytes 1444

commit v2 on v1

--- a/solution.py
+++ b/solution.py
@@ -344,138 +344,6 @@
 
 def rows_twelve():
     return [(QKV_AT, 3 * D), (WO_AT, D), (WF1_AT, FF)]
-
-
-def gather_kernel(
-    points_ref, slots_ref, pflat, bflat,
-    rel_ref, moment_ref, psmall_o, bsmall_o, w2_o, w3_o, w4_o, wqkv_o, wo_o, wf1_o, wf2_o,
-    blocks, stage, wide, acc, sums, ssend, srecv, gsend, grecv,
-):
-    z, y, x, core = where_am_i()
-    dp = NZ * NY * NX
-    near = [(chip(lax.rem(z + k, NZ), y, x), core) for k in range(1, NZ)]
-    over_y, over_x, twin = (chip(z, 1 - y, x), core), (chip(z, y, 1 - x), core), (chip(z, y, x), 1 - core)
-    count = greet(all_peers(dp) + near + [over_y, over_x, twin])
-
-    stage[...] = jnp.zeros_like(stage)
-    for at, start, rows, cols, under in (
-        (W3_AT, 9, 16, C3, 0), (W4_AT, 73, 16, D, 0), (W2_AT, 1, 4, C2, 12),
-    ):
-        for j in range(cols // 128):
-            stage[under : under + rows, at + 128 * j : at + 128 * j + 128] = pflat[
-                pl.ds(start + j, rows, stride=cols // 128), :
-            ]
-    stage[12:13, PSMALL_AT : PSMALL_AT + 128] = pflat[0:1, :]
-    stage[12:13, BSMALL_AT : BSMALL_AT + 128] = bflat[0:1, :]
-    start = 1
-    for at, cols in rows_twelve():
-        for j in range(cols // 128):
-            stage[0:12, at + 128 * j : at + 128 * j + 128] = bflat[
-                pl.ds(start + j, 12, stride=cols // 128), :
-            ]
-        start += 12 * cols // 128
-    for b in range(3):
-        for j in range(D // 128):
-            to = WF2_AT + D * b + 128 * j
-            stage[:, to : to + 128] = bflat[pl.ds(start + 48 * b + j, 16, stride=3), :]
-    blocks[z, y, x, core] = low(stage[...])
-
-    greeted(count)
-    used = [0]
-
-    def send(view, peer):
-        k = used[0]
-        used[0] += 1
-        copy = pltpu.make_async_remote_copy(
-            src_ref=view, dst_ref=view, send_sem=gsend.at[k], recv_sem=grecv.at[k],
-            device_id=peer, device_id_type=MESH,
-        )
-        copy.start()
-        return copy
-
-    one, two = pl.ds(0, HALF), pl.ds(HALF, HALF)
-    live = [send(blocks.at[z, y, x, core], peer) for peer in near]
-    geometry(points_ref, slots_ref, rel_ref, acc)
-    small = sum_start(dp, False, acc, sums, ssend, srecv)
-    for copy in live:
-        copy.wait()
-    live = [
-        send(blocks.at[:, y, x, core, :, one], over_y),
-        send(blocks.at[:, y, x, core, :, two], over_x),
-    ]
-    inner = [send(blocks.at[:, y, x, core], twin)]
-    sum_finish(dp, False, acc, sums, small)
-    small = sum_start(dp, True, acc, sums, ssend, srecv)
-    for copy in live:
-        copy.wait()
-    live = [
-        send(blocks.at[:, :, x, core, :, one], over_x),
-        send(blocks.at[:, y, :, core, :, two], over_y),
-    ]
-    inner += [
-        send(blocks.at[:, 1 - y, x, core, :, one], twin),
-        send(blocks.at[:, y, 1 - x, core, :, two], twin),
-    ]
-    sum_finish(dp, True, acc, sums, small)
-    moment_ref[...] = acc[...]
-    for copy in live:
-        copy.wait()
-    inner += [
-        send(blocks.at[:, :, 1 - x, core, :, one], twin),
-        send(blocks.at[:, 1 - y, :, core, :, two], twin),
-    ]
-    for copy in inner:
-        copy.wait()
-
-    for d in range(dp * NC):
-        cz, cy, cx, cc = d // 8, d // 4 % 2, d // 2 % 2, d % 2
-        block = blocks.at[cz, cy, cx, cc]
-        w3_o[16 * d : 16 * d + 16, :] = block[:, W3_AT : W3_AT + C3]
-        w4_o[16 * d : 16 * d + 16, :] = block[:, W4_AT : W4_AT + D]
-        for b in range(3):
-            at = 48 * d + 16 * b
-            wf2_o[at : at + 16, :] = block[:, WF2_AT + D * b : WF2_AT + D * b + D]
-        under = block[:, QKV_AT:WF2_AT].astype(F32)
-        wide[12 * d : 12 * d + 12, :] = under[0:12, :]
-        tail = under[12:16, 0 : BSMALL_AT + 128 - QKV_AT]
-        wide[384 + 4 * d : 384 + 4 * d + 4, 0 : BSMALL_AT + 128 - QKV_AT] = tail
-    for at, cols, out in ((QKV_AT, 3 * D, wqkv_o), (WO_AT, D, wo_o), (WF1_AT, FF, wf1_o)):
-        out[...] = low(wide[0:384, at - QKV_AT : at - QKV_AT + cols])
-    w2_o[...] = low(wide[384:512, 0:C2])
-    tails = wide[pl.ds(384, 32, stride=4), :] if False else None
-    psmall = jnp.concatenate(
-        [wide[384 + 4 * d : 385 + 4 * d, PSMALL_AT - QKV_AT : PSMALL_AT - QKV_AT + 128] for d in range(32)], 0
-    )
-    bsmall = jnp.concatenate(
-        [wide[384 + 4 * d : 385 + 4 * d, BSMALL_AT - QKV_AT : BSMALL_AT - QKV_AT + 128] for d in range(32)], 0
-    )
-    psmall_o[0:18, :] = flat_rows(psmall, 72, 18)
-    bsmall_o[0:30, :] = flat_rows(bsmall, 120, 30)
-
-
-def gather_call(points, slots, pflat, bflat):
-    dp = NZ * NY * NX
-    count = points.shape[1]
-    outs = shaped(
-        ((8, count), BF16), ((8, 128), F32), ((24, 128), F32), ((32, 128), F32),
-        ((C1, C2), BF16), ((2 * C2, C3), BF16), ((C3, D), BF16),
-        ((D, 3 * D), BF16), ((D, D), BF16), ((D, FF), BF16), ((FF, D), BF16),
-    )
-    return pl.pallas_call(
-        gather_kernel,
-        out_shape=outs,
-        in_specs=vmem(4),
-        out_specs=vmem(len(outs)),
-        scratch_shapes=[
-            pltpu.VMEM((NZ, NY, NX, NC, 16, WIDTH), BF16),
-            pltpu.VMEM((16, WIDTH), F32),
-            pltpu.VMEM((512, WF2_AT - QKV_AT), F32),
-        ]
-        + sum_scratch(dp, (8, 128))
-        + [pltpu.SemaphoreType.DMA((16,)), pltpu.SemaphoreType.DMA((16,))],
-        compiler_params=params(collective_id=0, has_side_effects=True),
-        name="gather",
-    )(points, slots, pflat, bflat)
 
 
 def first_kernel(
@@ -624,6 +492,299 @@
         compiler_params=params(),
         name="second",
     )(f, rel, w3, gm, sv)
+
+
+def first_tile(rel, wn, w2, ext_ref, gp_ref):
+    valid = rel[3:4, :].astype(F32)
+    for j in range(TILE // 256):
+        at = slice(256 * j, 256 * j + 256)
+        g, gp = gelu_pair(mm_tn(wn, rel[:, at]))
+        ext_ref[0:C1, at] = low(g * valid[:, at])
+        gp_ref[:, at] = low(gp * valid[:, at])
+    ext_ref[C1:, :] = jnp.concatenate([rel[3:4], jnp.zeros((15, TILE), BF16)], axis=0)
+    ext = ext_ref[...]
+    return low(mm_tn(ext, w2)), low(mm_tn(w2, ext))
+
+
+def first_tokens(cnt_ref, fs_ref, gram_ref, w3_ref, pooled_o, g_o, fw_o):
+    count = cnt_ref[:, 0:1]
+    fs = fs_ref[...]
+    pooled = low(fs / count)
+    pooled_o[...] = pooled
+    g = mm(pooled, w3_ref[0:C2, :])
+    g_o[...] = g
+    lower = w3_ref[C2:, :]
+    fw = mm_exact(fs, lower)
+    fw_o[...] = fw
+    one = jnp.sum(fw + count * g, axis=0, keepdims=True)
+    two = jnp.sum(mm_exact(gram_ref[...], lower) * lower.astype(F32), axis=0, keepdims=True)
+    two = two + jnp.sum(g * (2.0 * fw + count * g), axis=0, keepdims=True)
+    return jnp.concatenate([one, two, jnp.zeros((6, C3), F32)], axis=0)
+
+
+def third_vectors(totals, n, psmall_ref):
+    mean = totals[0:1, :] / n
+    inverse = lax.rsqrt(totals[1:2, :] / n - mean * mean + EPS_NORM)
+    gain = jnp.concatenate([psmall_ref[k : k + 1, :] for k in range(7, 11)], axis=1)
+    shift = jnp.concatenate([psmall_ref[k : k + 1, :] for k in range(11, 15)], axis=1)
+    return jnp.concatenate([inverse * gain, shift, mean, inverse, jnp.zeros((4, C3), F32)], axis=0)
+
+
+def second_tile(f_at, mask, lower, gm_at, sv_ref, gp_o, pa_o, pg_o, pc_o, first):
+    scale, shift = low(sv_ref[0:1, :]), low(sv_ref[1:2, :])
+    tokens = SUB // GROUP
+    for j in range(TILE // SUB):
+        at, ts = slice(SUB * j, SUB * j + SUB), slice(tokens * j, tokens * j + tokens)
+        to = pl.ds(pl.multiple_of(first + tokens * j, tokens), tokens)
+        c = mm(f_at(SUB * j, SUB), lower).reshape(tokens, GROUP, C3) + gm_at(to)[:, None, :]
+        c = low(c)
+        g, gp = gelu_pair(c * scale[None] + shift[None])
+        gc = (gp * c).reshape(SUB, C3)
+        gp = gp.reshape(SUB, C3)
+        gp_o[at, :] = gp
+        m = mask[ts, at]
+        pa_o[to, :] = mm(m, g.reshape(SUB, C3))
+        pg_o[to, :] = mm(m, gp)
+        pc_o[to, :] = mm(m, gc)
+
+
+class Gather:
+    def __init__(self, blocks, send, recv, base):
+        self.blocks, self.sems, self.base = blocks, (send, recv), base
+        z, y, x, core = where_am_i()
+        half = blocks.shape[-1] // 2
+        one, two = pl.ds(0, half), pl.ds(half, half)
+        every = slice(None)
+        near = [(chip(lax.rem(z + k, NZ), y, x), core) for k in range(1, NZ)]
+        over_y, over_x, twin = (chip(z, 1 - y, x), core), (chip(z, y, 1 - x), core), (chip(z, y, x), 1 - core)
+        self.stages = [
+            [((z, y, x, core), peer) for peer in near],
+            [((every, y, x, core, every, one), over_y), ((every, y, x, core, every, two), over_x)],
+            [((every, every, x, core, every, one), over_x), ((every, y, every, core, every, two), over_y)],
+            [],
+        ]
+        self.inner = [
+            [],
+            [((every, y, x, core), twin)],
+            [((every, 1 - y, x, core, every, one), twin), ((every, y, 1 - x, core, every, two), twin)],
+            [((every, every, 1 - x, core, every, one), twin), ((every, 1 - y, every, core, every, two), twin)],
+        ]
+
+    def copies(self, stage, inner):
+        table = self.inner if inner else self.stages
+        k = self.base + (7 if inner else 0) + sum(len(s) for s in table[:stage])
+        out = []
+        for i, (index, peer) in enumerate(table[stage]):
+            view = self.blocks.at[index]
+            out.append(
+                pltpu.make_async_remote_copy(
+                    src_ref=view, dst_ref=view, send_sem=self.sems[0].at[k + i], recv_sem=self.sems[1].at[k + i],
+                    device_id=peer, device_id_type=MESH,
+                )
+            )
+        return out
+
+    def advance(self, stage):
+        if stage > 0:
+            for copy in self.copies(stage - 1, False):
+                copy.wait()
+        if stage < 4:
+            for copy in self.copies(stage, False) + self.copies(stage, True):
+                copy.start()
+        else:
+            for inner_stage in range(4):
+                for copy in self.copies(inner_stage, True):
+                    copy.wait()
+
+
+GATHER_SEMS = 12
+REST = [("w4", 0, D), ("wqkv", 384, 3 * D), ("wo", 1536, D), ("wf1", 1920, FF), ("wf2", 3456, 3 * D)]
+REST_WIDTH = 4608
+
+
+def forward_kernel(
+    points_ref, slots_ref, pflat, bflat,
+    rel_o, moment_o, psmall_o, bsmall_o, w2_o, w3_o, w4_o, wqkv_o, wo_o, wf1_o, wf2_o,
+    ext_o, gp1_o, f_o, ft_o, gram_o, fs_o, cnt_o, gm_o, fw_o, pooled_o, sv_o, stats_o, wd_o,
+    gp_o, pa_o, pg_o, pc_o,
+    tiny, rest, stage, wide, f_s, e_s, wn_s, w2_s,
+    acc, sums, ssend, srecv, acc3, sums3, ssend3, srecv3, tsend, trecv, gsend, grecv, fsem, three, flat2,
+):
+    step = pl.program_id(0)
+    tiles = pl.num_programs(0) // 2
+    z, y, x, core = where_am_i()
+    dp = NZ * NY * NX
+    plane = (y * NX + x) * NC + core
+    gather_w3 = Gather(three, gsend, grecv, 0)
+    gather_rest = Gather(rest, gsend, grecv, GATHER_SEMS)
+    f_copy = pltpu.make_async_copy(f_s, f_o, fsem)
+
+    @pl.when(step == 0)
+    def _():
+        count = greet(all_peers(dp) + [(chip(z, 1 - y, x), core), (chip(z, y, 1 - x), core), (chip(z, y, x), 1 - core)])
+        rows = [pflat[1:9, :], pflat[0:1, :], bflat[0:1, :], jnp.zeros((6, 128), F32)]
+        tiny[z, plane] = low(jnp.concatenate(rows, axis=0))
+        for j in range(C3 // 128):
+            three[z, y, x, core, :, 128 * j : 128 * j + 128] = low(pflat[pl.ds(9 + j, 16, stride=C3 // 128), :])
+        stage[...] = jnp.zeros_like(stage)
+        for j in range(D // 128):
+            stage[:, 128 * j : 128 * j + 128] = pflat[pl.ds(73 + j, 16, stride=D // 128), :]
+        start = 1
+        for name, at, cols in REST[1:4]:
+            for j in range(cols // 128):
+                stage[0:12, at + 128 * j : at + 128 * j + 128] = bflat[pl.ds(start + j, 12, stride=cols // 128), :]
+            start += 12 * cols // 128
+        for b in range(3):
+            for j in range(D // 128):
+                to = REST[4][1] + D * b + 128 * j
+                stage[:, to : to + 128] = bflat[pl.ds(start + 48 * b + j, 16, stride=3), :]
+        rest[z, y, x, core] = low(stage[...])
+        geometry(points_ref, slots_ref, rel_o, acc)
+        e_s[...] = token_ones()
+        gram_o[...] = jnp.zeros_like(gram_o)
+        greeted(count)
+
+        def tiny_copies(upper_stage):
+            view = tiny.at[z] if upper_stage else tiny.at[z, plane]
+            first = 7 if upper_stage else 0
+            return [
+                pltpu.make_async_remote_copy(
+                    src_ref=view, dst_ref=view, send_sem=tsend.at[first + k], recv_sem=trecv.at[first + k],
+                    device_id=peer, device_id_type=MESH,
+                )
+                for k, peer in enumerate(ring_peers(dp, upper_stage))
+            ]
+
+        for upper_stage in (False, True):
+            copies = tiny_copies(upper_stage)
+            small = sum_start(dp, upper_stage, acc, sums, ssend, srecv)
+            for copy in copies:
+                copy.start()
+            sum_finish(dp, upper_stage, acc, sums, small)
+            for copy in copies:
+                copy.wait()
+        gather_w3.advance(0)
+        moment_o[...] = acc[...]
+        psmall, bsmall = [], []
+        for d in range(dp * NC):
+            rows = tiny[d // 8, d % 8].astype(F32)
+            flat2[8 * d : 8 * d + 8, :] = rows[0:8, :]
+            psmall.append(rows[8:9, :])
+            bsmall.append(rows[9:10, :])
+        psmall_o[0:18, :] = flat_rows(jnp.concatenate(psmall, axis=0), 72, 18)
+        bsmall_o[0:30, :] = flat_rows(jnp.concatenate(bsmall, axis=0), 120, 30)
+        for j in range(2):
+            w2_o[:, 128 * j : 128 * j + 128] = low(flat2[pl.ds(j, C1, stride=2), :])
+        small = psmall_o[...]
+        forward, backward, stats = prepare_one(acc[:, 0:8], small)
+        wn_s[...] = forward
+        wd_o[...] = backward
+        stats_o[...] = stats
+        w2_s[0:C1, :] = w2_o[...]
+        b2 = jnp.concatenate([small[5:6, :], small[6:7, :]], axis=1)
+        w2_s[C1:, :] = low(jnp.concatenate([b2, jnp.zeros((15, C2), F32)], axis=0))
+
+    for at_step, work in (
+        (1, lambda: gather_rest.advance(0)),
+        (2, lambda: gather_w3.advance(1)),
+        (3, lambda: gather_w3.advance(2)),
+        (5, lambda: gather_w3.advance(3)),
+        (6, lambda: gather_rest.advance(1)),
+        (7, lambda: gather_w3.advance(4)),
+        (9, lambda: gather_rest.advance(2)),
+        (12, lambda: gather_rest.advance(3)),
+    ):
+        pl.when(step == at_step)(work)
+
+    at_points = pl.multiple_of(lax.rem(step, tiles) * TILE, TILE)
+    rel = rel_o[:, pl.ds(at_points, TILE)]
+    first = pl.multiple_of(lax.rem(step, tiles) * TOK, TOK)
+
+    @pl.when(step < tiles)
+    def _():
+        f, ft = first_tile(rel, wn_s[...], w2_s[...], ext_o, gp1_o)
+        ft_o[...] = ft
+        f_s[pl.ds(at_points, TILE), :] = f
+        gram_o[...] += mm(ft, f)
+        fs_o[pl.ds(first, TOK), :] = mm(e_s[...], f)
+        cnt_o[pl.ds(first, TOK), :] = jnp.broadcast_to(mm_nt(e_s[...], rel)[:, 3:4], (TOK, 128))
+
+    @pl.when(step == tiles)
+    def _():
+        f_copy.start()
+        for d in range(dp * NC):
+            w3_o[16 * d : 16 * d + 16, :] = three[d // 8, d // 4 % 2, d // 2 % 2, d % 2]
+        acc3[...] = first_tokens(cnt_o, fs_o, gram_o, w3_o, pooled_o, gm_o, fw_o)
+        sum_over_devices(dp, acc3, sums3, ssend3, srecv3)
+        sv_o[...] = third_vectors(acc3[...], stats_o[2:3, 0:1], psmall_o)
+        gm_o[...] = gm_o[...] - sv_o[2:3, :]
+
+    @pl.when(step >= tiles)
+    def _():
+        mask = e_s[...] * rel[3:4, :]
+        second_tile(
+            lambda start, size: f_s[pl.ds(pl.multiple_of(at_points + start, SUB), size), :],
+            mask, w3_o[C2:, :], lambda to: gm_o[to, :], sv_o, gp_o, pa_o, pg_o, pc_o, first,
+        )
+
+    @pl.when(step == 2 * tiles - 1)
+    def _():
+        f_copy.wait()
+        gather_rest.advance(4)
+        for d in range(dp * NC):
+            block = rest.at[d // 8, d // 4 % 2, d // 2 % 2, d % 2]
+            w4_o[16 * d : 16 * d + 16, :] = block[:, 0:D]
+            for b in range(3):
+                at = 48 * d + 16 * b
+                wf2_o[at : at + 16, :] = block[:, 3456 + D * b : 3456 + D * b + D]
+            wide[12 * d : 12 * d + 12, :] = block[:, 384:3456].astype(F32)[0:12, :]
+        for out, at, cols in ((wqkv_o, 0, 3 * D), (wo_o, 1152, D), (wf1_o, 1536, FF)):
+            out[...] = low(wide[:, at : at + cols])
+
+
+def forward_call(points, slots, pflat, bflat):
+    dp = NZ * NY * NX
+    count = points.shape[1]
+    tokens, tiles = count // GROUP, count // TILE
+    single = dict(pipeline_mode=pl.Buffered(1))
+    full = lambda *s: pl.BlockSpec(s, lambda i: (0, 0), **single)
+    early = lambda r: pl.BlockSpec((r, TILE), lambda i: (0, jnp.minimum(i, tiles - 1)))
+    outs = [
+        (full(8, count), (8, count), BF16), (full(8, 128), (8, 128), F32), (full(24, 128), (24, 128), F32),
+        (full(32, 128), (32, 128), F32), (full(C1, C2), (C1, C2), BF16), (full(2 * C2, C3), (2 * C2, C3), BF16),
+        (full(C3, D), (C3, D), BF16), (full(D, 3 * D), (D, 3 * D), BF16), (full(D, D), (D, D), BF16),
+        (full(D, FF), (D, FF), BF16), (full(FF, D), (FF, D), BF16),
+        (early(C1 + 16), (C1 + 16, count), BF16), (early(C1), (C1, count), BF16),
+        (pl.BlockSpec(memory_space=pl.ANY), (count, C2), BF16), (early(C2), (C2, count), BF16),
+        (full(C2, C2), (C2, C2), F32), (full(tokens, C2), (tokens, C2), F32), (full(tokens, 128), (tokens, 128), F32),
+        (full(tokens, C3), (tokens, C3), F32), (full(tokens, C3), (tokens, C3), F32),
+        (full(tokens, C2), (tokens, C2), BF16), (full(8, C3), (8, C3), F32), (full(8, C1), (8, C1), F32),
+        (full(8, C1), (8, C1), BF16),
+        (pl.BlockSpec((TILE, C3), lambda i: (jnp.maximum(i - tiles, 0), 0)), (count, C3), BF16),
+        (full(tokens, C3), (tokens, C3), F32), (full(tokens, C3), (tokens, C3), F32), (full(tokens, C3), (tokens, C3), F32),
+    ]
+    return pl.pallas_call(
+        forward_kernel,
+        grid=(2 * tiles,),
+        in_specs=[full(3, count), full(2, count), full(PROWS, 128), full(BROWS, 128)],
+        out_specs=[o[0] for o in outs],
+        out_shape=shaped(*[o[1:] for o in outs]),
+        scratch_shapes=[
+            pltpu.VMEM((NZ, 2 * NY * NX, 16, 128), BF16),
+            pltpu.VMEM((NZ, NY, NX, NC, 16, REST_WIDTH), BF16),
+            pltpu.VMEM((16, REST_WIDTH), F32),
+            pltpu.VMEM((384, 3456 - 384), F32),
+            pltpu.VMEM((count, C2), BF16),
+            pltpu.VMEM((TOK, TILE), BF16), pltpu.VMEM((8, C1), BF16), pltpu.VMEM((C1 + 16, C2), BF16),
+        ]
+        + sum_scratch(dp, (8, 128))
+        + sum_scratch(dp, (8, C3))
+        + [pltpu.SemaphoreType.DMA((10,)), pltpu.SemaphoreType.DMA((10,))]
+        + [pltpu.SemaphoreType.DMA((2 * GATHER_SEMS,)), pltpu.SemaphoreType.DMA((2 * GATHER_SEMS,))]
+        + [pltpu.SemaphoreType.DMA, pltpu.VMEM((NZ, NY, NX, NC, 16, C3), BF16), pltpu.VMEM((256, 128), F32)],
+        compiler_params=params(collective_id=0, has_side_effects=True),
+        name="forward",
+    )(points, slots, pflat, bflat)
 
 
 def wide_row(ref, first, rows):
@@ -1186,15 +1347,17 @@
     known = dp == NZ * NY * NX and fsdp == NC
     slots = jnp.repeat(jnp.stack([point_count, centre_slot]), GROUP, axis=1)
     if known:
-        gathered = gather_call(
-            points, slots, flat_of(point_master, 72, PROWS), flat_of(block_master, 120, BROWS)
+        (
+            rel, moments, psmall, bsmall, w2, w3, w4, wqkv, wo, wf1, wf2, ext, gp1, f, ft,
+            gram, fs, cnt, gm, fw, pooled, sv, stats, wd, gp, pa, pg, pc,
+        ) = forward_call(points, slots, flat_of(point_master, 72, PROWS), flat_of(block_master, 120, BROWS))
+    else:
+        rel, moments, psmall, bsmall, w2, w3, w4, wqkv, wo, wf1, wf2 = gather_plain(
+            points, slots, point_master, block_master, devices
         )
-    else:
-        gathered = gather_plain(points, slots, point_master, block_master, devices)
-    rel, moments, psmall, bsmall, w2, w3, w4, wqkv, wo, wf1, wf2 = gathered
-    ext, gp1, f, ft, gram, fs, cnt, g, fw, pooled, sums, stats, wd = first_call(rel, moments, psmall, w2, w3)
-    gm, sv = third_call(dp, sums, g, stats, psmall)
-    gp, pa, pg, pc = second_call(f, rel, w3, gm, sv)
+        ext, gp1, f, ft, gram, fs, cnt, g, fw, pooled, sums, stats, wd = first_call(rel, moments, psmall, w2, w3)
+        gm, sv = third_call(dp, sums, g, stats, psmall)
+        gp, pa, pg, pc = second_call(f, rel, w3, gm, sv)
     tokens_out, gw4, gwqkv, gwo, gwf1, gwf2, small, tok, tg, back = block_call(
         pa, pg, pc, cnt, cloud_length, cotangent, psmall, bsmall, sv, w4, wqkv, wo, wf1, wf2
     )

time: 257 us -> 239 us (0.930)
  Pallas kernels: 237 us -> 219 us
    pallas_call x4 -> x1, Pallas kernels: 110 us -> 92.9 us  [forward_call(): pl.pallas_call(forward_kernel, grid=(2 * tiles,), in_specs=[full(3, count...]
where the time goes in v2:
time: 239 us
  Pallas kernels  219 us (92%)
  local copies, waits for them, and re-layouts  15.7 us (7%)
  other arithmetic  2.73 us (1%)
    pallas_call x1, Pallas kernels, forward_call(): pl.pallas_call(forward_kernel, grid=(2 * tiles,), in_specs=[full(3, count...  92.9 us
    pallas_call x1, Pallas kernels, scatter_call(): pl.pallas_call(scatter_kernel, out_shape=outs, in_specs=vmem(len(args)),...  51.9 us
    pallas_call x1, Pallas kernels, block_call(): pl.pallas_call(block_kernel, grid=(tokens // TB,), in_specs=[rows(C3), ro...  30.5 us
    pallas_call x1, Pallas kernels, last_call(): pl.pallas_call(last_kernel, grid=(count // TILE,), in_specs=[rows(TILE, C...  30.4 us
    pallas_call x1, Pallas kernels, third_back_call(): pl.pallas_call(functools.partial(third_back_kernel, dp), out_shape=outs,...  13.8 us

profile of v2, /device:TPU:0, one launch (start us, length us, event | category | flops | bytes accessed | tf_op | source)
XLA Modules:
  0.0 238.9 jit_solution(13818852021757723000)
XLA Ops:
  0.6 0.7 pad_add_fusion
  1.4 0.2 broadcast_in_dim.94
  1.5 1.0 reshape.39.slots_ref
  2.5 1.0 slice.33
  3.6 0.7 slice.32
  4.3 3.5 %concatenate.25 = f32[56320]{0:T(1024)} concatenate(f32[120]{0:T(128)S(1)} %slice.32, f32[8]{0:T(128)S(1)} %broadcast.75, f32[55296]{0:T(1024)S(1)} %slice.33, f32[896]{0:T(1024)S(1)} %broadcast.74), dimensions={0} | concatenate | bytes 450560 | tf_op jit(solution)/shard_map/concatenate | solution.py:1337
  7.7 0.9 slice.31
  8.7 0.7 slice.30
  9.4 0.7 concatenate.24
  10.1 92.9 %forward.1 = (bf16[8,16384]{1,0:T(8,128)(2,1)}, f32[8,128]{1,0:T(8,128)}, f32[24,128]{1,0:T(8,128)}, f32[32,128]{1,0:T(8,128)}, bf16[128,256]{1,0:T(8,128)(2,1)}...) custom-call(f32[3,16384]{1,0:T(4,128)} %points_ref.1, ...), custom_call_target="tpu_custom_call" | custom-call | tf_op jit(solution)/shard_map/forward/pallas_call | solution.py:766
  103.0 30.5 %block.1 = (f32[512,384]{1,0:T(8,128)}, f32[512,384]{1,0:T(8,128)}, f32[384,1152]{1,0:T(8,128)}, f32[384,384]{1,0:T(8,128)}, f32[384,1536]{1,0:T(8,128)}, /*inde...) custom-call(f32[512,512]{1,0:T(8,128)} %get-tuple-element.63.pa_ref, ...), custom_call_target="tpu_custom_call" | custom-call | tf_op jit(solution)/shard_map/block/pallas_call | solution.py:929
  133.5 13.8 %third_back.1 = (f32[8,512]{1,0:T(8,128)}, bf16[512,512]{1,0:T(8,128)(2,1)}, f32[512,256]{1,0:T(8,128)}, bf16[256,256]{1,0:T(8,128)(2,1)}, bf16[256,512]{1,0:T(8...) custom-call(f32[8,512]{1,0:T(8,128)} %get-tuple-element.82.back_ref, f32[512,512]{1,0:T(8,128)} %get-tuple-element.83.tok_ref, ...), custom_call_target="tpu_custom_call" | custom-call | tf_op jit(solution)/shard_map/third_back/pallas_call | solution.py:988
  147.3 30.4 %last.1 = (f32[256,512]{1,0:T(8,128)}, f32[144,256]{1,0:T(8,128)}, f32[8,128]{1,0:T(8,128)}, f32[8,16384]{1,0:T(8,128)}) custom-call(bf16[16384,512]{1,0:T(8,128)(2,1)} %get-tuple-element.76.gp_ref, bf16[16384,256]{1,0:T(8,128)(2,1)} %get-tuple-element.77.f_ref, bf16[256,16384]{1,0:T(8,128)(2,1)} %get-tuple-element.78.ft_ref, ...), custom_call_target="tpu_custom_call" | custom-call | tf_op jit(solution)/shard_map/last/pallas_call | solution.py:1029
  177.6 0.0 copy-start
  177.7 0.0 copy-start.3
  177.7 0.0 copy-start.4
  177.7 51.9 %scatter.1 = (f32[3,16384]{1,0:T(4,128)}, f32[128,128]{1,0:T(8,128)}, f32[440,128]{1,0:T(8,128)}) custom-call(f32[8,128]{1,0:T(8,128)} %get-tuple-element.98.q_ref, f32[8,128]{1,0:T(8,128)} %get-tuple-element.99.moment_ref, f32[24,128]{1,0:T(8,128)} %get-tuple-element.67.psmall_ref, f32[8,128]{1,0:T(8,128)} %get-tuple-element.91.stats_ref, ...), custom_call_target="tpu_custom_call" | custom-call | tf_op jit(solution)/shard_map/scatter/pallas_call | solution.py:1233
  229.6 0.0 copy-start.2
  229.6 0.0 copy-start.5
  229.6 0.0 copy-start.6
  229.6 0.0 copy-start.1
  229.7 1.0 slice_bitcast_fusion
  230.7 0.7 slice.41
  231.4 0.0 copy-start.7
  231.5 1.4 concatenate.29
  232.9 1.4 concatenate.31
  234.4 0.0 copy-done
  234.4 0.0 copy-done.3
  234.4 0.0 copy-done.4
  234.4 1.1 fusion.20
  235.5 0.8 slice_bitcast_fusion.1
  236.4 0.7 slice.40
  237.1 0.1 concatenate.26
  237.2 0.1 concatenate.28
  237.3 0.0 copy-done.2
  237.3 0.0 copy-done.5
  237.4 0.0 copy-done.6
  237.4 0.8 fusion.22
  238.2 0.0 copy-done.1
  238.2 0.7 copy.23
  238.9 0.0 copy-done.7
  (13 shorter events, 0.1 us)
Async XLA Ops:
  177.6 56.8 %copy-start = (f32[55416]{0:T(1024)S(1)}, f32[55416]{0:T(1024)}, u32[]{:S(2)}) copy-start(f32[55416]{0:T(1024)} %param.17) | copy-start | bytes 664996
  177.7 56.8 %copy-start.3 = (f32[55416]{0:T(1024)S(1)}, f32[55416]{0:T(1024)}, u32[]{:S(2)}) copy-start(f32[55416]{0:T(1024)} %param.19) | copy-start | bytes 664996
  177.7 56.8 %copy-start.4 = (f32[55416]{0:T(1024)S(1)}, f32[55416]{0:T(1024)}, u32[]{:S(2)}) copy-start(f32[55416]{0:T(1024)} %param.21) | copy-start | bytes 664996
  229.6 7.7 %copy-start.2 = (f32[15432]{0:T(1024)S(1)}, f32[15432]{0:T(1024)}, u32[]{:S(2)}) copy-start(f32[15432]{0:T(1024)} %param.16) | copy-start | bytes 185188
  229.6 7.7 %copy-start.5 = (f32[15432]{0:T(1024)S(1)}, f32[15432]{0:T(1024)}, u32[]{:S(2)}) copy-start(f32[15432]{0:T(1024)} %param.18) | copy-start | bytes 185188
  229.6 7.7 %copy-start.6 = (f32[15432]{0:T(1024)S(1)}, f32[15432]{0:T(1024)}, u32[]{:S(2)}) copy-start(f32[15432]{0:T(1024)} %param.20) | copy-start | bytes 185188
  229.6 8.5 %copy-start.1 = (f32[3,16384]{1,0:T(4,128)S(1)}, f32[3,16384]{1,0:T(4,128)}, u32[]{:S(2)}) copy-start(f32[3,16384]{1,0:T(4,128)} %get-tuple-element.149) | copy-start | bytes 589828
  231.4 7.5 %copy-start.7 = (f32[120]{0:T(128)}, f32[120]{0:T(128)S(1)}, u32[]{:S(2)}) copy-start(f32[120]{0:T(128)S(1)} %slice.41) | copy-start | bytes 1444

commit v3 on v2

--- a/solution.py
+++ b/solution.py
@@ -246,6 +246,16 @@
         pltpu.SemaphoreType.DMA((count,)),
         pltpu.SemaphoreType.DMA((count,)),
     ]
+
+
+def as_rows(*vectors):
+    return jnp.concatenate(
+        [v[:, 128 * k : 128 * k + 128] for v in vectors for k in range(v.shape[1] // 128)], axis=0
+    )
+
+
+def as_vector(rows, first, count):
+    return jnp.concatenate([rows[k : k + 1, :] for k in range(first, first + count)], axis=1)
 
 
 def all_peers(dp):
@@ -367,16 +377,7 @@
         w2_s[C1:, :] = low(jnp.concatenate([b2, jnp.zeros((15, C2), F32)], axis=0))
 
     rel = rel_ref[...]
-    valid = rel[3:4, :].astype(F32)
-    for j in range(TILE // 256):
-        at = slice(256 * j, 256 * j + 256)
-        g, gp = gelu_pair(mm_tn(wn_s[...], rel[:, at]))
-        ext_o[0:C1, at] = low(g * valid[:, at])
-        gp_o[:, at] = low(gp * valid[:, at])
-    ext_o[C1:, :] = jnp.concatenate([rel[3:4], jnp.zeros((15, TILE), BF16)], axis=0)
-    ext = ext_o[...]
-    ft = low(mm_tn(w2_s[...], ext))
-    f = low(mm_tn(ext, w2_s[...]))
+    f, ft = first_tile(rel, wn_s[...], w2_s[...], ext_o, gp_o)
     ft_o[...] = ft
     f_o[...] = f
     gram_o[...] += mm(ft, f)
@@ -386,19 +387,7 @@
 
     @pl.when(step == pl.num_programs(0) - 1)
     def _():
-        count = cnt_o[:, 0:1]
-        fs = fs_o[...]
-        pooled = low(fs / count)
-        pooled_o[...] = pooled
-        g = mm(pooled, w3_ref[0:C2, :])
-        g_o[...] = g
-        lower = w3_ref[C2:, :]
-        fw = mm_exact(fs, lower)
-        fw_o[...] = fw
-        one = jnp.sum(fw + count * g, axis=0, keepdims=True)
-        two = jnp.sum(mm_exact(gram_o[...], lower) * lower.astype(F32), axis=0, keepdims=True)
-        two = two + jnp.sum(g * (2.0 * fw + count * g), axis=0, keepdims=True)
-        sums_o[...] = jnp.concatenate([one, two, jnp.zeros((6, C3), F32)], axis=0)
+        sums_o[...] = first_tokens(cnt_o, fs_o, gram_o, w3_ref, pooled_o, g_o, fw_o)
 
 
 def first_call(rel, moments, psmall, w2, w3):
@@ -413,12 +402,12 @@
         out_specs=[
             cols(C1 + 16), cols(C1), pl.BlockSpec((TILE, C2), lambda i: (i, 0)), cols(C2),
             full(C2, C2), full(tokens, C2), full(tokens, 128), full(tokens, C3), full(tokens, C3),
-            full(tokens, C2), full(8, C3), full(8, C1), full(8, C1),
+            full(tokens, C2), full(8, 128), full(8, C1), full(8, C1),
         ],
         out_shape=shaped(
             ((C1 + 16, count), BF16), ((C1, count), BF16), ((count, C2), BF16), ((C2, count), BF16),
             ((C2, C2), F32), ((tokens, C2), F32), ((tokens, 128), F32), ((tokens, C3), F32),
-            ((tokens, C3), F32), ((tokens, C2), BF16), ((8, C3), F32), ((8, C1), F32), ((8, C1), BF16),
+            ((tokens, C3), F32), ((tokens, C2), BF16), ((8, 128), F32), ((8, C1), F32), ((8, C1), BF16),
         ),
         scratch_shapes=[pltpu.VMEM((TOK, TILE), BF16), pltpu.VMEM((8, C1), BF16), pltpu.VMEM((C1 + 16, C2), BF16)],
         compiler_params=params(),
@@ -431,15 +420,8 @@
     acc[...] = sums_ref[...]
     greeted(count)
     sum_over_devices(dp, acc, slots, send, recv)
-    n = stats_ref[2:3, 0:1]
-    mean = acc[0:1, :] / n
-    inverse = lax.rsqrt(acc[1:2, :] / n - mean * mean + EPS_NORM)
-    gain = jnp.concatenate([psmall_ref[k : k + 1, :] for k in range(7, 11)], axis=1)
-    shift = jnp.concatenate([psmall_ref[k : k + 1, :] for k in range(11, 15)], axis=1)
-    gm_o[...] = g_ref[...] - mean
-    sv_o[...] = jnp.concatenate(
-        [inverse * gain, shift, mean, inverse, jnp.zeros((4, C3), F32)], axis=0
-    )
+    sv_o[...] = third_vectors(acc[...], stats_ref[2:3, 0:1], psmall_ref)
+    gm_o[...] = g_ref[...] - sv_o[2:3, :]
 
 
 def third_call(dp, sums, g, stats, psmall):
@@ -448,7 +430,7 @@
         out_shape=shaped((g.shape, F32), ((8, C3), F32)),
         in_specs=vmem(4),
         out_specs=vmem(2),
-        scratch_shapes=sum_scratch(dp, (8, C3)),
+        scratch_shapes=sum_scratch(dp, (8, 128)),
         compiler_params=params(collective_id=1, has_side_effects=True),
         name="third",
     )(sums, g, stats, psmall)
@@ -459,22 +441,10 @@
     def _():
         e_s[...] = token_ones()
 
-    mask = e_s[...] * rel_ref[3:4, :]
-    lower = w3_ref[C2:, :]
-    scale, shift = low(sv_ref[0:1, :]), low(sv_ref[1:2, :])
-    tokens = SUB // GROUP
-    for j in range(TILE // SUB):
-        at, ts = slice(SUB * j, SUB * j + SUB), slice(tokens * j, tokens * j + tokens)
-        c = mm(f_ref[at, :], lower).reshape(tokens, GROUP, C3) + gm_ref[ts, :][:, None, :]
-        c = low(c)
-        g, gp = gelu_pair(c * scale[None] + shift[None])
-        gc = (gp * c).reshape(SUB, C3)
-        gp = gp.reshape(SUB, C3)
-        gp_o[at, :] = gp
-        m = mask[ts, at]
-        pa_o[ts, :] = mm(m, g.reshape(SUB, C3))
-        pg_o[ts, :] = mm(m, gp)
-        pc_o[ts, :] = mm(m, gc)
+    second_tile(
+        lambda start, size: f_ref[start : start + size, :], e_s[...] * rel_ref[3:4, :], w3_ref[C2:, :],
+        lambda to: gm_ref[to, :], sv_ref, gp_o, pa_o, pg_o, pc_o, 0,
+    )
 
 
 def second_call(f, rel, w3, gm, sv):
@@ -519,12 +489,12 @@
     one = jnp.sum(fw + count * g, axis=0, keepdims=True)
     two = jnp.sum(mm_exact(gram_ref[...], lower) * lower.astype(F32), axis=0, keepdims=True)
     two = two + jnp.sum(g * (2.0 * fw + count * g), axis=0, keepdims=True)
-    return jnp.concatenate([one, two, jnp.zeros((6, C3), F32)], axis=0)
+    return as_rows(one, two)
 
 
 def third_vectors(totals, n, psmall_ref):
-    mean = totals[0:1, :] / n
-    inverse = lax.rsqrt(totals[1:2, :] / n - mean * mean + EPS_NORM)
+    mean = as_vector(totals, 0, 4) / n
+    inverse = lax.rsqrt(as_vector(totals, 4, 4) / n - mean * mean + EPS_NORM)
     gain = jnp.concatenate([psmall_ref[k : k + 1, :] for k in range(7, 11)], axis=1)
     shift = jnp.concatenate([psmall_ref[k : k + 1, :] for k in range(11, 15)], axis=1)
     return jnp.concatenate([inverse * gain, shift, mean, inverse, jnp.zeros((4, C3), F32)], axis=0)
@@ -535,7 +505,7 @@
     tokens = SUB // GROUP
     for j in range(TILE // SUB):
         at, ts = slice(SUB * j, SUB * j + SUB), slice(tokens * j, tokens * j + tokens)
-        to = pl.ds(pl.multiple_of(first + tokens * j, tokens), tokens)
+        to = pl.ds(first + tokens * j, tokens)
         c = mm(f_at(SUB * j, SUB), lower).reshape(tokens, GROUP, C3) + gm_at(to)[:, None, :]
         c = low(c)
         g, gp = gelu_pair(c * scale[None] + shift[None])
@@ -778,7 +748,7 @@
             pltpu.VMEM((TOK, TILE), BF16), pltpu.VMEM((8, C1), BF16), pltpu.VMEM((C1 + 16, C2), BF16),
         ]
         + sum_scratch(dp, (8, 128))
-        + sum_scratch(dp, (8, C3))
+        + sum_scratch(dp, (8, 128))
         + [pltpu.SemaphoreType.DMA((10,)), pltpu.SemaphoreType.DMA((10,))]
         + [pltpu.SemaphoreType.DMA((2 * GATHER_SEMS,)), pltpu.SemaphoreType.DMA((2 * GATHER_SEMS,))]
         + [pltpu.SemaphoreType.DMA, pltpu.VMEM((NZ, NY, NX, NC, 16, C3), BF16), pltpu.VMEM((256, 128), F32)],
@@ -952,22 +922,15 @@
     )(pa, pg, pc, cnt, length, cot, psmall, bsmall, sv, w4, wqkv, wo, wf1, wf2)
 
 
-def third_back_kernel(
-    dp, back_ref, tok_ref, tg_ref, fs_ref, fw_ref, gm_ref, cnt_ref, pooled_ref, gram_ref, w3_ref, sv_ref, stats_ref,
-    tot_o, tok_o, kap_o, k_o, ws_o, top_o, corr_o, acc, slots, send, recv,
+def third_back_tokens(
+    totals, tg_ref, fs_ref, fw_ref, gm_ref, cnt_ref, pooled_ref, gram_ref, w3_ref, sv_ref, stats_ref,
+    kap_o, k_o, top_o, corr_o,
 ):
-    greeting = greet(all_peers(dp))
-    acc[...] = back_ref[...]
-    tok_o[...] = low(tok_ref[...])
     lower = w3_ref[C2:, :].astype(F32)
     gain = sv_ref[0:1, :]
-    ws_o[...] = low(lower * gain)
-    greeted(greeting)
-    sum_over_devices(dp, acc, slots, send, recv)
-    tot_o[...] = acc[...]
     n = stats_ref[2:3, 0:1]
-    alpha = gain * acc[0:1, :] / n
-    beta = gain * acc[1:2, :] * sv_ref[3:4, :] / n
+    alpha = gain * as_vector(totals, 0, 4) / n
+    beta = gain * as_vector(totals, 4, 4) * sv_ref[3:4, :] / n
     count = cnt_ref[:, 0:1]
     gm = gm_ref[...]
     per_token = low(gain * tg_ref[...] - (count * alpha + beta * (fw_ref[...] + count * gm)))
@@ -979,10 +942,27 @@
     corr_o[...] = mm_tn(low(fs_ref[...]), shifted) + beta * mm(low(gram_ref[...]), w3_ref[C2:, :])
 
 
+def third_back_kernel(
+    dp, back_ref, tok_ref, tg_ref, fs_ref, fw_ref, gm_ref, cnt_ref, pooled_ref, gram_ref, w3_ref, sv_ref, stats_ref,
+    tot_o, tok_o, kap_o, k_o, ws_o, top_o, corr_o, acc, slots, send, recv,
+):
+    greeting = greet(all_peers(dp))
+    acc[...] = as_rows(back_ref[0:1, :], back_ref[1:2, :])
+    tok_o[...] = low(tok_ref[...])
+    ws_o[...] = low(w3_ref[C2:, :].astype(F32) * sv_ref[0:1, :])
+    greeted(greeting)
+    sum_over_devices(dp, acc, slots, send, recv)
+    tot_o[...] = acc[...]
+    third_back_tokens(
+        acc[...], tg_ref, fs_ref, fw_ref, gm_ref, cnt_ref, pooled_ref, gram_ref, w3_ref, sv_ref, stats_ref,
+        kap_o, k_o, top_o, corr_o,
+    )
+
+
 def third_back_call(dp, back, tok, tg, fs, fw, gm, cnt, pooled, gram, w3, sv, stats):
     tokens = tok.shape[0]
     outs = shaped(
-        ((8, C3), F32), ((tokens, C3), BF16), ((tokens, C2), F32), ((C2, C2), BF16), ((C2, C3), BF16),
+        ((8, 128), F32), ((tokens, C3), BF16), ((tokens, C2), F32), ((C2, C2), BF16), ((C2, C3), BF16),
         ((C2, C3), F32), ((C2, C3), F32),
     )
     return pl.pallas_call(
@@ -990,10 +970,28 @@
         out_shape=outs,
         in_specs=vmem(12),
         out_specs=vmem(len(outs)),
-        scratch_shapes=sum_scratch(dp, (8, C3)),
+        scratch_shapes=sum_scratch(dp, (8, 128)),
         compiler_params=params(collective_id=2, has_side_effects=True),
         name="third_back",
     )(back, tok, tg, fs, fw, gm, cnt, pooled, gram, w3, sv, stats)
+
+
+def last_tile(
+    gp_ref, f_ref, ft_ref, ext_ref, gp1_ref, rel, tok, kap, k_ref, ws_ref, w2_ref, wd_ref, h_o, gw2_o, q_o, d_at, dn_s
+):
+    tokens = SUB // GROUP
+    for j in range(TILE // SUB):
+        at, ts = slice(SUB * j, SUB * j + SUB), slice(tokens * j, tokens * j + tokens)
+        gp = gp_ref[at, :].reshape(tokens, GROUP, C3)
+        dn_s[at, :] = (gp * tok[ts, :][:, None, :]).reshape(SUB, C3)
+    dn = dn_s[...]
+    h_o[...] += mm(ft_ref[...], dn)
+    d_feat = mm_nt(dn, ws_ref[...]) + mm(f_ref[...], k_ref[...])
+    d_feat = low((d_feat.reshape(TOK, GROUP, C2) + kap[:, None, :]).reshape(TILE, C2))
+    gw2_o[...] += mm(ext_ref[...], d_feat)
+    d_one = low(mm_nt(w2_ref[...], d_feat) * gp1_ref[...].astype(F32))
+    d_at(mm(wd_ref[...], d_one))
+    q_o[...] += mm_nt(rel, d_one)
 
 
 def last_kernel(
@@ -1005,20 +1003,13 @@
         for ref in (h_o, gw2_o, q_o):
             ref[...] = jnp.zeros_like(ref)
 
-    tokens = SUB // GROUP
-    for j in range(TILE // SUB):
-        at, ts = slice(SUB * j, SUB * j + SUB), slice(tokens * j, tokens * j + tokens)
-        gp = gp_ref[at, :].reshape(tokens, GROUP, C3)
-        dn_s[at, :] = (gp * tok_ref[ts, :][:, None, :]).reshape(SUB, C3)
-    dn = dn_s[...]
-    h_o[...] += mm(ft_ref[...], dn)
-    d_feat = mm_nt(dn, ws_ref[...]) + mm(f_ref[...], k_ref[...])
-    d_feat = (d_feat.reshape(TOK, GROUP, C2) + kap_ref[...][:, None, :]).reshape(TILE, C2)
-    d_feat = low(d_feat)
-    gw2_o[...] += mm(ext_ref[...], d_feat)
-    d_one = low(mm_nt(w2_ref[...], d_feat) * gp1_ref[...].astype(F32))
-    d_o[...] = mm(wd_ref[...], d_one)
-    q_o[...] += mm_nt(rel_ref[...], d_one)
+    def put(d):
+        d_o[...] = d
+
+    last_tile(
+        gp_ref, f_ref, ft_ref, ext_ref, gp1_ref, rel_ref[...], tok_ref[...], kap_ref[...], k_ref, ws_ref, w2_ref,
+        wd_ref, h_o, gw2_o, q_o, put, dn_s,
+    )
 
 
 def last_call(gp, f, ft, ext, gp1, rel, tok, kap, k, ws, w2, wd):
@@ -1083,8 +1074,7 @@
 def point_small_rows(grad_w, gain1, shift1, b2, tot, b4):
     rows = list(grad_w) + [gain1, shift1]
     rows += [b2[:, 128 * k : 128 * k + 128] for k in range(2)]
-    rows += [tot[1:2, 128 * k : 128 * k + 128] for k in range(4)]
-    rows += [tot[0:1, 128 * k : 128 * k + 128] for k in range(4)]
+    rows += [tot[4:8, :], tot[0:4, :]]
     rows += [b4[:, 128 * k : 128 * k + 128] for k in range(3)]
     return jnp.concatenate(rows, axis=0)
 
@@ -1096,157 +1086,258 @@
     return jnp.concatenate(rows, axis=0)
 
 
-def scatter_kernel(
-    q_ref, moment_ref, psmall_ref, stats_ref, tot_ref, small_ref, d_ref, rel_ref, slots_ref,
-    gw2_ref, top_ref, h_ref, corr_ref, sv_ref, gw4_ref, gwqkv_ref, gwo_ref, gwf1_ref, gwf2_ref,
-    pg_o, pflat_o, bflat_o,
-    blocks, stage, land1, land2, land3, land4, acc, slots, ssend, srecv, gsend, grecv,
+class Scatter:
+    def __init__(self, blocks, lands, send, recv, base):
+        self.blocks, self.lands, self.sems, self.base = blocks, lands, (send, recv), base
+        z, y, x, core = self.at = where_am_i()
+        half = blocks.shape[-1] // 2
+        self.one, self.two = pl.ds(0, half), pl.ds(half, half)
+        every = slice(None)
+        mine = blocks.at[core]
+        near = [(chip(lax.rem(z + k, NZ), y, x), core) for k in range(1, NZ)]
+        over_y, over_x, twin = (chip(z, 1 - y, x), core), (chip(z, y, 1 - x), core), (chip(z, y, x), 1 - core)
+        land1, land2, land3, land4 = lands
+        self.stages = [
+            [(blocks.at[1 - core], land1, twin)],
+            [
+                (mine.at[:, :, 1 - x, :, self.one], land2.at[0], over_x),
+                (mine.at[:, 1 - y, :, :, self.two], land2.at[1], over_y),
+            ],
+            [
+                (mine.at[:, 1 - y, x, :, self.one], land3.at[0], over_y),
+                (mine.at[:, y, 1 - x, :, self.two], land3.at[1], over_x),
+            ],
+            [(mine.at[lax.rem(z + k, NZ), y, x], land4.at[k - 1], near[k - 1]) for k in range(1, NZ)],
+        ]
+
+    def copies(self, stage):
+        k = self.base + sum(len(s) for s in self.stages[:stage])
+        return [
+            pltpu.make_async_remote_copy(
+                src_ref=src, dst_ref=dst, send_sem=self.sems[0].at[k + i], recv_sem=self.sems[1].at[k + i],
+                device_id=peer, device_id_type=MESH,
+            )
+            for i, (src, dst, peer) in enumerate(self.stages[stage])
+        ]
+
+    def advance(self, stage):
+        z, y, x, core = self.at
+        mine = self.blocks.at[core]
+        land1, land2, land3, land4 = self.lands
+        if stage > 0:
+            for copy in self.copies(stage - 1):
+                copy.wait()
+        if stage == 1:
+            for cz in range(NZ):
+                for cy in range(NY):
+                    for cx in range(NX):
+                        mine[cz, cy, cx] = mine[cz, cy, cx] + land1[cz, cy, cx]
+        if stage == 2:
+            for cz in range(NZ):
+                for k in range(2):
+                    mine[cz, k, x, :, self.one] = mine[cz, k, x, :, self.one] + land2[0, cz, k]
+                    mine[cz, y, k, :, self.two] = mine[cz, y, k, :, self.two] + land2[1, cz, k]
+        if stage == 3:
+            for cz in range(NZ):
+                mine[cz, y, x, :, self.one] = mine[cz, y, x, :, self.one] + land3[0, cz]
+                mine[cz, y, x, :, self.two] = mine[cz, y, x, :, self.two] + land3[1, cz]
+        if stage < 4:
+            for copy in self.copies(stage):
+                copy.start()
+            return None
+        total = mine[z, y, x].astype(F32)
+        for k in range(NZ - 1):
+            total = total + land4[k].astype(F32)
+        return total
+
+
+SCATTER_SEMS = 8
+POINT_WIDTH = 1024
+
+
+def scatter_scratch(width):
+    return [
+        pltpu.VMEM((NC, NZ, NY, NX, 16, width), BF16),
+        pltpu.VMEM((NZ, NY, NX, 16, width), BF16),
+        pltpu.VMEM((2, NZ, 2, 16, width // 2), BF16),
+        pltpu.VMEM((2, NZ, 16, width // 2), BF16),
+        pltpu.VMEM((NZ - 1, 16, width), BF16),
+    ]
+
+
+def backward_kernel(
+    pa_ref, pg_ref, pc_ref, cnt_ref, len_ref, cot_ref, psmall_ref, bsmall_ref, sv_ref, stats_ref, moment_ref,
+    w2_ref, w3_ref, w4_ref, wqkv_ref, wo_ref, wf1_ref, wf2_ref,
+    fs_ref, fw_ref, gm_ref, pooled_ref, gram_ref, wd_ref, rel_ref, slots_ref,
+    gp_ref, f_ref, ft_ref, ext_ref, gp1_ref,
+    out_o, pg_o, pflat_o, bflat_o,
+    gw4_s, gwqkv_s, gwo_s, gwf1_s, gwf2_s, small_s, tok_s, tg_s, back_s,
+    qkv_s, mixed_s, soft_s, dmix_s, dqkv_s,
+    tot_s, kap_s, k_s, ws_s, top_s, corr_s, h_s, gw2_s, q_s, d_s, dn_s,
+    rest0, rest1, rest2, rest3, rest4, point0, point1, point2, point3, point4, stage, pstage,
+    acc, slots, ssend, srecv, acc3, slots3, ssend3, srecv3, gsend, grecv,
 ):
+    step = pl.program_id(0)
+    steps = pl.num_programs(0)
     z, y, x, core = where_am_i()
     dp = NZ * NY * NX
-    near = [(chip(lax.rem(z + k, NZ), y, x), core) for k in range(1, NZ)]
-    over_y, over_x, twin = (chip(z, 1 - y, x), core), (chip(z, y, 1 - x), core), (chip(z, y, x), 1 - core)
-    count = greet(all_peers(dp) + near + [over_y, over_x, twin])
-    acc[...] = q_ref[...]
-    greeted(count)
-    small = sum_start(dp, False, acc, slots, ssend, srecv)
-
-    none = jnp.zeros((1, 128), F32)
-    prow = point_small_rows(
-        [none] * 3, none, none, gw2_ref[C1 : C1 + 1, :], jnp.zeros((8, C3), F32), small_ref[6:7, 0:D]
-    )
-    brow = block_small_rows(small_ref)
-    stage[...] = jnp.zeros_like(stage)
-    gain = sv_ref[0:1, :]
-    for d in range(dp * NC):
-        cz, cy, cx, cc = d // 8, d // 4 % 2, d // 2 % 2, d % 2
-        if d < 16:
-            stage[:, W3_AT : W3_AT + C3] = top_ref[16 * d : 16 * d + 16, :]
-        else:
-            rows = slice(16 * (d - 16), 16 * (d - 16) + 16)
-            stage[:, W3_AT : W3_AT + C3] = h_ref[rows, :] * gain - corr_ref[rows, :]
-        stage[:, W4_AT : W4_AT + D] = gw4_ref[16 * d : 16 * d + 16, :]
-        stage[0:12, QKV_AT : QKV_AT + 3 * D] = gwqkv_ref[12 * d : 12 * d + 12, :]
-        stage[0:12, WO_AT : WO_AT + D] = gwo_ref[12 * d : 12 * d + 12, :]
-        stage[0:12, WF1_AT : WF1_AT + FF] = gwf1_ref[12 * d : 12 * d + 12, :]
-        stage[12:16, W2_AT : W2_AT + C2] = gw2_ref[4 * d : 4 * d + 4, :]
-        stage[12:13, PSMALL_AT : PSMALL_AT + 128] = piece_of(prow, 72 * d, 72)
-        stage[12:13, BSMALL_AT : BSMALL_AT + 128] = piece_of(brow, 120 * d, 120)
+    rest = Scatter(rest0, (rest1, rest2, rest3, rest4), gsend, grecv, 0)
+    point = Scatter(point0, (point1, point2, point3, point4), gsend, grecv, SCATTER_SEMS)
+    peers = all_peers(dp) + [(chip(z, 1 - y, x), core), (chip(z, y, 1 - x), core), (chip(z, y, x), 1 - core)]
+    blocks = cnt_ref.shape[0] // TB
+
+    @pl.when(step == 0)
+    def _():
+        greet(peers)
+
+    @pl.when(step < blocks)
+    def _():
+        rows = pl.ds(pl.multiple_of(step * TB, TB), TB)
+        block_kernel(
+            pa_ref, pg_ref, pc_ref, cnt_ref.at[rows], len_ref, cot_ref, psmall_ref, bsmall_ref, sv_ref,
+            w4_ref, wqkv_ref, wo_ref, wf1_ref, wf2_ref,
+            out_o, gw4_s, gwqkv_s, gwo_s, gwf1_s, gwf2_s, small_s, tok_s.at[rows], tg_s.at[rows], back_s,
+            qkv_s, mixed_s, soft_s, dmix_s, dqkv_s,
+        )
+
+    @pl.when(step == blocks - 1)
+    def _():
+        greeted(len(peers))
+        acc3[...] = as_rows(back_s[0:1, :], back_s[1:2, :])
+        copies = sum_start(dp, False, acc3, slots3, ssend3, srecv3)
+        brow = block_small_rows(small_s)
+        stage[...] = jnp.zeros_like(stage)
+        for d in range(dp * NC):
+            stage[:, 0:D] = gw4_s[16 * d : 16 * d + 16, :]
+            for ref, at, cols in ((gwqkv_s, 384, 3 * D), (gwo_s, 1536, D), (gwf1_s, 1920, FF)):
+                stage[0:12, at : at + cols] = ref[12 * d : 12 * d + 12, :]
+            for b in range(3):
+                at = 48 * d + 16 * b
+                stage[:, 3456 + D * b : 3456 + D * b + D] = gwf2_s[at : at + 16, :]
+            stage[12:13, 384:512] = piece_of(brow, 120 * d, 120)
+            rest0[d % 2, d // 8, d // 4 % 2, d // 2 % 2] = low(stage[...])
+        rest.advance(0)
+        sum_finish(dp, False, acc3, slots3, copies)
+        copies = sum_start(dp, True, acc3, slots3, ssend3, srecv3)
+        ws_s[...] = low(w3_ref[C2:, :].astype(F32) * sv_ref[0:1, :])
+        for ref in (h_s, gw2_s, q_s):
+            ref[...] = jnp.zeros_like(ref)
+        sum_finish(dp, True, acc3, slots3, copies)
+        tot_s[...] = acc3[...]
+        third_back_tokens(
+            acc3[...], tg_s, fs_ref, fw_ref, gm_ref, cnt_ref, pooled_ref, gram_ref, w3_ref, sv_ref, stats_ref,
+            kap_s, k_s, top_s, corr_s,
+        )
+        rest.advance(1)
+
+    for at_step, number in ((5, 2), (7, 3)):
+        pl.when(step == at_step)(functools.partial(rest.advance, number))
+
+    @pl.when(step >= blocks)
+    def _():
+        tile = step - blocks
+        at = pl.ds(pl.multiple_of(tile * TILE, TILE), TILE)
+        ts = pl.ds(pl.multiple_of(tile * TOK, TOK), TOK)
+
+        def put(d):
+            d_s[:, at] = d
+
+        last_tile(
+            gp_ref, f_ref, ft_ref, ext_ref, gp1_ref, rel_ref[:, at], low(tok_s[ts, :]), kap_s[ts, :], k_s, ws_s,
+            w2_ref, wd_ref, h_s, gw2_s, q_s, put, dn_s,
+        )
+
+    @pl.when(step == steps - 1)
+    def _():
+        acc[...] = q_s[...]
+        copies = sum_start(dp, False, acc, slots, ssend, srecv)
+        none = jnp.zeros((1, 128), F32)
+        prow = point_small_rows(
+            [none] * 3, none, none, gw2_s[C1 : C1 + 1, :], jnp.zeros((8, 128), F32), small_s[6:7, 0:D]
+        )
+        pstage[...] = jnp.zeros_like(pstage)
+        for d in range(dp * NC):
+            if d < 16:
+                pstage[:, 0:C3] = top_s[16 * d : 16 * d + 16, :]
+            else:
+                rows = slice(16 * (d - 16), 16 * (d - 16) + 16)
+                pstage[:, 0:C3] = h_s[rows, :] * sv_ref[0:1, :] - corr_s[rows, :]
+            pstage[0:4, C3 : C3 + C2] = gw2_s[4 * d : 4 * d + 4, :]
+            pstage[0:1, 768:896] = piece_of(prow, 72 * d, 72)
+            point0[d % 2, d // 8, d // 4 % 2, d // 2 % 2] = low(pstage[...])
+        point.advance(0)
+        sum_finish(dp, False, acc, slots, copies)
+        copies = sum_start(dp, True, acc, slots, ssend, srecv)
+        point.advance(1)
+        sum_finish(dp, True, acc, slots, copies)
+        grad_w, gain1, shift1, flat, slope = first_grads(acc[...], moment_ref[...], psmall_ref[...], stats_ref[...])
+        point.advance(2)
+        stage[...] = rest.advance(4)
+        point.advance(3)
+        point_gradient(d_s, rel_ref, slots_ref, flat, slope, pg_o)
+        pstage[...] = point.advance(4)
+
+        full_rows = point_small_rows(grad_w, gain1, shift1, jnp.zeros((1, C2), F32), tot_s[...], jnp.zeros((1, D), F32))
+        rank = chip(z, y, x) * NC + core
+        own = jnp.zeros((1, 128), F32)
+        for d in range(dp * NC):
+            own = own + jnp.where(rank == d, piece_of(full_rows, 72 * d, 72), 0.0)
+        pflat_o[0:1, :] = pstage[0:1, 768:896] + own
+        bflat_o[0:1, :] = stage[12:13, 384:512]
+        for j in range(C2 // 128):
+            pflat_o[pl.ds(1 + j, 4, stride=2), :] = pstage[0:4, C3 + 128 * j : C3 + 128 * j + 128]
+        for j in range(C3 // 128):
+            pflat_o[pl.ds(9 + j, 16, stride=4), :] = pstage[:, 128 * j : 128 * j + 128]
+        for j in range(D // 128):
+            pflat_o[pl.ds(73 + j, 16, stride=3), :] = stage[:, 128 * j : 128 * j + 128]
+        start = 1
+        for name, at, cols in REST[1:4]:
+            for j in range(cols // 128):
+                bflat_o[pl.ds(start + j, 12, stride=cols // 128), :] = stage[0:12, at + 128 * j : at + 128 * j + 128]
+            start += 12 * cols // 128
         for b in range(3):
-            at = 48 * d + 16 * b
-            stage[:, WF2_AT + D * b : WF2_AT + D * b + D] = gwf2_ref[at : at + 16, :]
-        blocks[cc, cz, cy, cx] = low(stage[...])
-
-    used = [0]
-
-    def send(src, dst, peer):
-        k = used[0]
-        used[0] += 1
-        copy = pltpu.make_async_remote_copy(
-            src_ref=src, dst_ref=dst, send_sem=gsend.at[k], recv_sem=grecv.at[k],
-            device_id=peer, device_id_type=MESH,
-        )
-        copy.start()
-        return copy
-
-    one, two = pl.ds(0, HALF), pl.ds(HALF, HALF)
-    mine = blocks.at[core]
-    live = [send(blocks.at[1 - core], land1, twin)]
-    sum_finish(dp, False, acc, slots, small)
-    small = sum_start(dp, True, acc, slots, ssend, srecv)
-    for copy in live:
-        copy.wait()
-
-    def add(dst, index, landed):
-        dst[index] = low(dst[index].astype(F32) + landed.astype(F32))
-
-    for cz in range(NZ):
-        for cy in range(NY):
-            for cx in range(NX):
-                add(mine, (cz, cy, cx), land1[cz, cy, cx])
-    live = [
-        send(mine.at[:, :, 1 - x, :, one], land2.at[0], over_x),
-        send(mine.at[:, 1 - y, :, :, two], land2.at[1], over_y),
-    ]
-    sum_finish(dp, True, acc, slots, small)
-    totals = acc[...]
-    moments = moment_ref[...]
-    grad_w, gain1, shift1, flat, slope = first_grads(totals, moments, psmall_ref[...], stats_ref[...])
-    for copy in live:
-        copy.wait()
-    for cz in range(NZ):
-        for k in range(2):
-            add(mine, (cz, k, x, slice(None), one), land2[0, cz, k])
-            add(mine, (cz, y, k, slice(None), two), land2[1, cz, k])
-    live = [
-        send(mine.at[:, 1 - y, x, :, one], land3.at[0], over_y),
-        send(mine.at[:, y, 1 - x, :, two], land3.at[1], over_x),
-    ]
-    point_gradient(d_ref, rel_ref, slots_ref, flat, slope, pg_o)
-    for copy in live:
-        copy.wait()
-    for cz in range(NZ):
-        add(mine, (cz, y, x, slice(None), one), land3[0, cz])
-        add(mine, (cz, y, x, slice(None), two), land3[1, cz])
-    live = [
-        send(mine.at[lax.rem(z + k, NZ), y, x], land4.at[k - 1], near[k - 1]) for k in range(1, NZ)
-    ]
-    for copy in live:
-        copy.wait()
-    total = mine[z, y, x].astype(F32)
-    for k in range(NZ - 1):
-        total = total + land4[k].astype(F32)
-    stage[...] = total
-
-    full_rows = point_small_rows(grad_w, gain1, shift1, jnp.zeros((1, C2), F32), tot_ref[...], jnp.zeros((1, D), F32))
-    rank = chip(z, y, x) * NC + core
-    lane = lax.broadcasted_iota(jnp.int32, (1, 128), 1)
-    own = jnp.zeros((1, 128), F32)
-    for d in range(dp * NC):
-        own = own + jnp.where(rank == d, piece_of(full_rows, 72 * d, 72), 0.0)
-    pflat_o[0:1, :] = stage[12:13, PSMALL_AT : PSMALL_AT + 128] + own
-    bflat_o[0:1, :] = stage[12:13, BSMALL_AT : BSMALL_AT + 128]
-    for at, start, rows, cols, under in (
-        (W3_AT, 9, 16, C3, 0), (W4_AT, 73, 16, D, 0), (W2_AT, 1, 4, C2, 12),
-    ):
-        for j in range(cols // 128):
-            pflat_o[pl.ds(start + j, rows, stride=cols // 128), :] = stage[
-                under : under + rows, at + 128 * j : at + 128 * j + 128
-            ]
-    start = 1
-    for at, cols in rows_twelve():
-        for j in range(cols // 128):
-            bflat_o[pl.ds(start + j, 12, stride=cols // 128), :] = stage[
-                0:12, at + 128 * j : at + 128 * j + 128
-            ]
-        start += 12 * cols // 128
-    for b in range(3):
-        for j in range(D // 128):
-            at = WF2_AT + D * b + 128 * j
-            bflat_o[pl.ds(start + 48 * b + j, 16, stride=3), :] = stage[:, at : at + 128]
-
-
-def scatter_call(*args):
+            for j in range(D // 128):
+                at = 3456 + D * b + 128 * j
+                bflat_o[pl.ds(start + 48 * b + j, 16, stride=3), :] = stage[:, at : at + 128]
+
+
+def backward_call(*args):
     dp = NZ * NY * NX
-    count = args[7].shape[1]
-    outs = shaped(((3, count), F32), ((PROWS, 128), F32), ((BROWS, 128), F32))
+    count = args[24].shape[1]
+    tokens, blocks, tiles = count // GROUP, count // GROUP // TB, count // TILE
+    single = dict(pipeline_mode=pl.Buffered(1))
+    full = lambda *s: pl.BlockSpec(s, lambda i: (0, 0), **single)
+    chunk = lambda c: pl.BlockSpec((TB, c), lambda i: (jnp.minimum(i, blocks - 1), 0))
+    rows = lambda c: pl.BlockSpec((TILE, c), lambda i: (jnp.maximum(i - blocks, 0), 0))
+    cols = lambda r: pl.BlockSpec((r, TILE), lambda i: (0, jnp.maximum(i - blocks, 0)))
+    specs = [chunk(C3), chunk(C3), chunk(C3), full(tokens, 128), pl.BlockSpec(memory_space=pltpu.SMEM), chunk(D)]
+    specs += [full(*a.shape) for a in args[6:26]]
+    specs += [rows(C3), rows(C2), cols(C2), cols(C1 + 16), cols(C1)]
     return pl.pallas_call(
-        scatter_kernel,
-        out_shape=outs,
-        in_specs=vmem(len(args)),
-        out_specs=vmem(len(outs)),
+        backward_kernel,
+        grid=(blocks + tiles,),
+        in_specs=specs,
+        out_specs=[chunk(D), full(3, count), full(PROWS, 128), full(BROWS, 128)],
+        out_shape=shaped(((tokens, D), F32), ((3, count), F32), ((PROWS, 128), F32), ((BROWS, 128), F32)),
         scratch_shapes=[
-            pltpu.VMEM((NC, NZ, NY, NX, 16, WIDTH), BF16),
-            pltpu.VMEM((16, WIDTH), F32),
-            pltpu.VMEM((NZ, NY, NX, 16, WIDTH), BF16),
-            pltpu.VMEM((2, NZ, 2, 16, HALF), BF16),
-            pltpu.VMEM((2, NZ, 16, HALF), BF16),
-            pltpu.VMEM((NZ - 1, 16, WIDTH), BF16),
+            pltpu.VMEM((C3, D), F32), pltpu.VMEM((D, 3 * D), F32), pltpu.VMEM((D, D), F32), pltpu.VMEM((D, FF), F32),
+            pltpu.VMEM((FF, D), F32), pltpu.VMEM((8, FF), F32), pltpu.VMEM((tokens, C3), F32),
+            pltpu.VMEM((tokens, C3), F32), pltpu.VMEM((8, C3), F32),
+            pltpu.VMEM((TB, 3 * D), BF16), pltpu.VMEM((TB, D), BF16),
+            pltpu.VMEM((TB // PAIR * HEADS, PAIR, PAIR), F32), pltpu.VMEM((TB, D), BF16), pltpu.VMEM((TB, 3 * D), BF16),
+            pltpu.VMEM((8, 128), F32), pltpu.VMEM((tokens, C2), F32), pltpu.VMEM((C2, C2), BF16),
+            pltpu.VMEM((C2, C3), BF16), pltpu.VMEM((C2, C3), F32), pltpu.VMEM((C2, C3), F32), pltpu.VMEM((C2, C3), F32),
+            pltpu.VMEM((C1 + 16, C2), F32), pltpu.VMEM((8, C1), F32), pltpu.VMEM((8, count), F32),
+            pltpu.VMEM((TILE, C3), BF16),
         ]
+        + scatter_scratch(REST_WIDTH)
+        + scatter_scratch(POINT_WIDTH)
+        + [pltpu.VMEM((16, REST_WIDTH), F32), pltpu.VMEM((16, POINT_WIDTH), F32)]
         + sum_scratch(dp, (8, 128))
-        + [pltpu.SemaphoreType.DMA((16,)), pltpu.SemaphoreType.DMA((16,))],
+        + sum_scratch(dp, (8, 128))
+        + [pltpu.SemaphoreType.DMA((2 * SCATTER_SEMS,)), pltpu.SemaphoreType.DMA((2 * SCATTER_SEMS,))],
         compiler_params=params(collective_id=3, has_side_effects=True),
-        name="scatter",
+        name="backward",
     )(*args)
 
 
@@ -1303,7 +1394,7 @@
     )(d, rel, slots, table)
     none = jnp.zeros((1, 128), F32)
     local = point_small_rows(
-        [none] * 3, none, none, gw2[C1 : C1 + 1, :], jnp.zeros((8, C3), F32), small[6:7, 0:D]
+        [none] * 3, none, none, gw2[C1 : C1 + 1, :], jnp.zeros((8, 128), F32), small[6:7, 0:D]
     )
     known = point_small_rows(grad_w, gain1, shift1, jnp.zeros((1, C2), F32), tot, jnp.zeros((1, D), F32))
     w3 = jnp.concatenate([top, h * sv[0:1, :] - corr], axis=0)
@@ -1358,25 +1449,27 @@
         ext, gp1, f, ft, gram, fs, cnt, g, fw, pooled, sums, stats, wd = first_call(rel, moments, psmall, w2, w3)
         gm, sv = third_call(dp, sums, g, stats, psmall)
         gp, pa, pg, pc = second_call(f, rel, w3, gm, sv)
-    tokens_out, gw4, gwqkv, gwo, gwf1, gwf2, small, tok, tg, back = block_call(
-        pa, pg, pc, cnt, cloud_length, cotangent, psmall, bsmall, sv, w4, wqkv, wo, wf1, wf2
-    )
-    tot, tok_low, kap, k, ws, top, corr = third_back_call(
-        dp, back, tok, tg, fs, fw, gm, cnt, pooled, gram, w3, sv, stats
-    )
-    h, gw2, q, d = last_call(gp, f, ft, ext, gp1, rel, tok_low, kap, k, ws, w2, wd)
-    grads = (
-        q, moments, psmall, stats, tot, small, d, rel, slots,
-        gw2, top, h, corr, sv, gw4, gwqkv, gwo, gwf1, gwf2,
-    )
     if known:
-        point_grad, pflat, bflat = scatter_call(*grads)
+        tokens_out, point_grad, pflat, bflat = backward_call(
+            pa, pg, pc, cnt, cloud_length, cotangent, psmall, bsmall, sv, stats, moments,
+            w2, w3, w4, wqkv, wo, wf1, wf2, fs, fw, gm, pooled, gram, wd, rel, slots, gp, f, ft, ext, gp1,
+        )
         pflat, bflat = pflat.reshape(-1), bflat.reshape(-1)
         block_small = bflat[:120]
         point_gradient_vec = jnp.concatenate([pflat[:72], pflat[128 : 128 + point_master.shape[0] - 72]])
         block_gradient = jnp.concatenate([block_small, bflat[128 : 128 + block_master.shape[0] - 120]])
     else:
-        point_grad, point_parts, block_parts = scatter_plain(devices, *grads)
+        tokens_out, gw4, gwqkv, gwo, gwf1, gwf2, small, tok, tg, back = block_call(
+            pa, pg, pc, cnt, cloud_length, cotangent, psmall, bsmall, sv, w4, wqkv, wo, wf1, wf2
+        )
+        tot, tok_low, kap, k, ws, top, corr = third_back_call(
+            dp, back, tok, tg, fs, fw, gm, cnt, pooled, gram, w3, sv, stats
+        )
+        h, gw2, q, d = last_call(gp, f, ft, ext, gp1, rel, tok_low, kap, k, ws, w2, wd)
+        point_grad, point_parts, block_parts = scatter_plain(
+            devices, q, moments, psmall, stats, tot, small, d, rel, slots,
+            gw2, top, h, corr, sv, gw4, gwqkv, gwo, gwf1, gwf2,
+        )
         block_small = block_parts[0]
         point_gradient_vec = jnp.concatenate(point_parts)
         block_gradient = jnp.concatenate(block_parts)

time: 239 us -> 202 us (0.85)
  Pallas kernels: 219 us -> 181 us
    pallas_call x4 -> x1, Pallas kernels: 127 us -> 88.6 us  [backward_call(): pl.pallas_call(backward_kernel, grid=(blocks + tiles,), in_specs=specs, o...]
where the time goes in v3:
time: 202 us; the launch traced here: 201 us
  Pallas kernels  181 us (90%)
  local copies, waits for them, and re-layouts  16.7 us (8%)
  other arithmetic  2.73 us (1%)
    pallas_call x1, Pallas kernels, forward_call(): pl.pallas_call(forward_kernel, grid=(2 * tiles,), in_specs=[full(3, count...  92.4 us
    pallas_call x1, Pallas kernels, backward_call(): pl.pallas_call(backward_kernel, grid=(blocks + tiles,), in_specs=specs, o...  88.6 us
    concatenate x2, local copies, waits for them, and re-layouts, flat_of(): jnp.concatenate([vector[:small], pad, vector[small:], tail])  4.17 us

profile of v3, /device:TPU:0, one launch (start us, length us, event | category | flops | bytes accessed | tf_op | source)
XLA Modules:
  0.0 201.3 jit_solution(5873903183221495987)
XLA Ops:
  0.6 0.7 pad_add_fusion
  1.4 0.2 broadcast_in_dim.94
  1.5 1.0 reshape.39.slots_ref
  2.5 1.0 slice.33
  3.6 0.7 slice.32
  4.3 3.5 %concatenate.25 = f32[56320]{0:T(1024)} concatenate(f32[120]{0:T(128)S(1)} %slice.32, f32[8]{0:T(128)S(1)} %broadcast.75, f32[55296]{0:T(1024)S(1)} %slice.33, f32[896]{0:T(1024)S(1)} %broadcast.74), dimensions={0} | concatenate | bytes 450560 | tf_op jit(solution)/shard_map/concatenate | solution.py:1428
  7.7 0.9 slice.31
  8.7 0.7 slice.30
  9.4 0.7 concatenate.24
  10.1 92.4 %forward.1 = (bf16[8,16384]{1,0:T(8,128)(2,1)}, f32[8,128]{1,0:T(8,128)}, f32[24,128]{1,0:T(8,128)}, f32[32,128]{1,0:T(8,128)}, bf16[128,256]{1,0:T(8,128)(2,1)}...) custom-call(f32[3,16384]{1,0:T(4,128)} %points_ref.1, ...), custom_call_target="tpu_custom_call" | custom-call | tf_op jit(solution)/shard_map/forward/pallas_call | solution.py:736
  102.4 0.0 copy-start
  102.5 0.0 copy-start.4
  102.5 0.0 copy-start.5
  102.5 0.0 copy-start.3
  102.5 0.0 copy-start.6
  102.5 0.0 copy-start.7
  102.5 88.6 %backward.1 = (f32[512,384]{1,0:T(8,128)}, f32[3,16384]{1,0:T(4,128)}, f32[128,128]{1,0:T(8,128)}, f32[440,128]{1,0:T(8,128)}) custom-call(f32[512,512]{1,0:T(8,128)} %get-tuple-element.43.pa_ref, f32[512,512]{1,0:T(8,128)} %get-tuple-element.44.pg_ref, f32[512,512]{1,0:T(8,128)} %get-tuple-element.45.pc_ref, f32[512,128]{1,0:T(8,128)} %get-tuple-element.46.cnt_ref, ...), custom_call_target="tpu_custom_call" | custom-call | tf_op jit(solution)/shard_map/backward/pallas_call | solution.py:1316
  191.1 0.0 copy-start.1
  191.1 0.0 copy-start.2
  191.1 1.0 slice_bitcast_fusion
  192.2 0.7 slice.41
  192.9 0.0 copy-start.8
  193.0 1.4 concatenate.29
  194.5 1.4 concatenate.31
  195.9 0.0 copy-done
  195.9 0.0 copy-done.4
  195.9 0.0 copy-done.5
  195.9 1.1 fusion.20
  197.1 0.8 slice_bitcast_fusion.1
  197.9 0.7 slice.40
  198.7 0.1 concatenate.26
  198.7 0.1 concatenate.28
  198.8 0.0 copy-done.3
  198.9 0.0 copy-done.6
  198.9 0.0 copy-done.7
  198.9 0.8 fusion.22
  199.7 0.0 copy-done.1
  199.7 0.9 copy.24
  200.6 0.0 copy-done.2
  200.6 0.7 copy.25
  201.3 0.0 copy-done.8
  (13 shorter events, 0.1 us)
Async XLA Ops:
  102.4 93.5 %copy-start = (f32[55416]{0:T(1024)S(1)}, f32[55416]{0:T(1024)}, u32[]{:S(2)}) copy-start(f32[55416]{0:T(1024)} %param.17) | copy-start | bytes 664996
  102.5 93.5 %copy-start.4 = (f32[55416]{0:T(1024)S(1)}, f32[55416]{0:T(1024)}, u32[]{:S(2)}) copy-start(f32[55416]{0:T(1024)} %param.19) | copy-start | bytes 664996
  102.5 93.5 %copy-start.5 = (f32[55416]{0:T(1024)S(1)}, f32[55416]{0:T(1024)}, u32[]{:S(2)}) copy-start(f32[55416]{0:T(1024)} %param.21) | copy-start | bytes 664996
  102.5 96.4 %copy-start.3 = (f32[15432]{0:T(1024)S(1)}, f32[15432]{0:T(1024)}, u32[]{:S(2)}) copy-start(f32[15432]{0:T(1024)} %param.16) | copy-start | bytes 185188
  102.5 96.4 %copy-start.6 = (f32[15432]{0:T(1024)S(1)}, f32[15432]{0:T(1024)}, u32[]{:S(2)}) copy-start(f32[15432]{0:T(1024)} %param.18) | copy-start | bytes 185188
  102.5 96.4 %copy-start.7 = (f32[15432]{0:T(1024)S(1)}, f32[15432]{0:T(1024)}, u32[]{:S(2)}) copy-start(f32[15432]{0:T(1024)} %param.20) | copy-start | bytes 185188
  191.1 8.6 %copy-start.1 = (f32[512,384]{1,0:T(8,128)S(1)}, f32[512,384]{1,0:T(8,128)}, u32[]{:S(2)}) copy-start(f32[512,384]{1,0:T(8,128)} %get-tuple-element.108) | copy-start | bytes 2359300
  191.1 9.4 %copy-start.2 = (f32[3,16384]{1,0:T(4,128)S(1)}, f32[3,16384]{1,0:T(4,128)}, u32[]{:S(2)}) copy-start(f32[3,16384]{1,0:T(4,128)} %get-tuple-element.109) | copy-start | bytes 589828
  192.9 8.4 %copy-start.8 = (f32[120]{0:T(128)}, f32[120]{0:T(128)S(1)}, u32[]{:S(2)}) copy-start(f32[120]{0:T(128)S(1)} %slice.41) | copy-start | bytes 1444

commit v4 on v3

v4 whole, which is shorter than its diff:
```python
import functools
import math

import jax
import jax.numpy as jnp
from jax import lax
from jax.experimental import pallas as pl
from jax.experimental.pallas import tpu as pltpu
from jax.sharding import PartitionSpec as P

C1 = 128
C2 = 256
C3 = 512
D = 384
HEADS = 6
HEAD_DIM = 64
FF = 1536
GROUP = 32
PATCHES = 64
STEP = 10

EPS_NORM = 1e-05
BETA_ONE = 0.9
BETA_TWO = 0.95
ADAM_EPS = 1e-08
DECAY_RATE = 0.05
NEG_FILL = -1e30

F32 = jnp.float32
BF16 = jnp.bfloat16
AXES = ("dp", "fsdp")
MESH = pl.DeviceIdType.MESH
VMEM_LIMIT = 60 * 2**20
TILE = 2048
TOK = TILE // GROUP
TB = 256
PAIR = 128

NZ, NY, NX, NC = 4, 2, 2, 2
PROWS, BROWS = 128, 440
PSMALL, BSMALL = 72, 120


def point_layout():
    return [
        [
            ("w1", (3, C1), 3.0 ** (-0.5)),
            ("bn1_gain", (C1,), 0.0),
            ("bn1_shift", (C1,), -1.0),
            ("b2", (C2,), -1.0),
            ("bn3_gain", (C3,), 0.0),
            ("bn3_shift", (C3,), -1.0),
            ("b4", (D,), -1.0),
        ],
        [("w2", (C1, C2), C1 ** (-0.5))],
        [("w3", (2 * C2, C3), (2 * C2) ** (-0.5))],
        [("w4", (C3, D), C3 ** (-0.5))],
    ]


def block_layout():
    return [
        [
            ("ln1_gain", (D,), 0.0),
            ("ln1_shift", (D,), -1.0),
            ("bo", (D,), -1.0),
            ("ln2_gain", (D,), 0.0),
            ("ln2_shift", (D,), -1.0),
            ("bf1", (FF,), -1.0),
            ("bf2", (D,), -1.0),
        ],
        [("wqkv", (D, 3 * D), D ** (-0.5))],
        [("wo", (D, D), 3.0 * D ** (-0.5))],
        [("wf1", (D, FF), D ** (-0.5))],
        [("wf2", (FF, D), FF ** (-0.5))],
    ]


def rate_for(spread):
    return 2.0 * spread if spread > 0.0 else 0.5 if spread == 0.0 else 0.6


def decay_for(spread):
    return DECAY_RATE if spread > 0.0 else 0.0


def segment_lengths(layout, devices):
    lengths_out = []
    for segment in layout:
        used_len = sum((math.prod(entry[1]) for entry in segment))
        lengths_out.append(-(-used_len // devices) * devices)
    return lengths_out


def shard_rates(layout, devices, own_rank):
    rate_parts = []
    decay_parts = []
    for segment, seg_len in zip(layout, segment_lengths(layout, devices)):
        piece_len = seg_len // devices
        position = own_rank * piece_len + jnp.arange(piece_len, dtype=jnp.int32)
        seg_rates = jnp.zeros((piece_len,), F32)
        seg_decays = jnp.zeros((piece_len,), F32)
        offset = 0
        for entry_label, entry_dims, spread in segment:
            extent = math.prod(entry_dims)
            inside = (position >= offset) & (position < offset + extent)
            seg_rates = jnp.where(inside, rate_for(spread), seg_rates)
            seg_decays = jnp.where(inside, decay_for(spread), seg_decays)
            offset += extent
        rate_parts.append(seg_rates)
        decay_parts.append(seg_decays)
    return (jnp.concatenate(rate_parts), jnp.concatenate(decay_parts))


def mm(a, b):
    return jnp.dot(a, b, preferred_element_type=F32)


def mm_tn(a, b):
    return lax.dot_general(a, b, (((0,), (0,)), ((), ())), preferred_element_type=F32)


def mm_nt(a, b):
    return lax.dot_general(a, b, (((1,), (1,)), ((), ())), preferred_element_type=F32)


def low(v):
    return v.astype(BF16)


def split_three(v):
    hi = low(v)
    rest = v - hi.astype(F32)
    mid = low(rest)
    return hi, mid, low(rest - mid.astype(F32))


def mm_exact(a, b):
    hi, mid, lo = split_three(a)
    return mm(hi, b) + (mm(mid, b) + mm(lo, b))


LAM = (math.sqrt(2.0 / math.pi) * 0.044715) ** (-1.0 / 3.0)
ARG = math.sqrt(2.0 / math.pi) * LAM


def gelu_twice(y):
    square = y * y
    near = square + ARG
    t = jnp.tanh(y * near)
    up = 1.0 + t
    g = y * up
    return g, up + g * (1.0 - t) * (near + (square + square))


def gelu_pair(v):
    g, d = gelu_twice(v * (1.0 / LAM))
    return (0.5 * LAM) * g, 0.5 * d


def patch_ones():
    i = lax.broadcasted_iota(jnp.int32, (256, 256), 0) // GROUP
    j = lax.broadcasted_iota(jnp.int32, (256, 256), 1) // GROUP
    return (i == j).astype(F32).astype(BF16)


def token_ones():
    t = lax.broadcasted_iota(jnp.int32, (TOK, TILE), 0)
    p = lax.broadcasted_iota(jnp.int32, (TOK, TILE), 1) // GROUP
    return (t == p).astype(F32).astype(BF16)


def patch_sum(rows, ones):
    return mm_exact(rows, ones)


def rank_of(peer_dp, peer_core):
    return peer_dp * NC + peer_core


def me():
    return rank_of(lax.axis_index("dp"), lax.axis_index("fsdp"))


def all_peers(dp):
    n = dp * NC
    peers = []
    for k in range(1, n):
        p = lax.rem(me() + k, n)
        peers.append((p // NC, lax.rem(p, NC)))
    return peers


def greet(peers):
    barrier = pltpu.get_barrier_semaphore()
    for peer in peers:
        pl.semaphore_signal(barrier, inc=1, device_id=peer, device_id_type=MESH)


def greeted(peers):
    pl.semaphore_wait(pltpu.get_barrier_semaphore(), len(peers))


def send_to_all(dp, src, dst_of, send, recv):
    copies = []
    for k, peer in enumerate(all_peers(dp)):
        copy = pltpu.make_async_remote_copy(
            src_ref=src, dst_ref=dst_of(k), send_sem=send.at[k], recv_sem=recv.at[k],
            device_id=peer, device_id_type=MESH,
        )
        copy.start()
        copies.append(copy)
    return copies


def sum_start(dp, acc, slots, send, recv):
    return send_to_all(dp, acc, lambda k: slots.at[k], send, recv)


def sum_finish(acc, slots, copies):
    for copy in copies:
        copy.wait()
    return acc[...] + jnp.sum(slots[...], axis=0)


def sum_scratch(dp):
    n = dp * NC - 1
    return [
        pltpu.VMEM((8, 128), F32), pltpu.VMEM((n, 8, 128), F32),
        pltpu.SemaphoreType.DMA((n,)), pltpu.SemaphoreType.DMA((n,)),
    ]


def as_rows(*vectors):
    return jnp.concatenate(
        [v[:, 128 * k : 128 * k + 128] for v in vectors for k in range(v.shape[1] // 128)], axis=0
    )


def as_vector(rows, first, count):
    return jnp.concatenate([rows[k : k + 1, :] for k in range(first, first + count)], axis=1)


def vmem(count):
    return [pl.BlockSpec(memory_space=pltpu.VMEM)] * count


def shaped(*items):
    return [jax.ShapeDtypeStruct(s, t) for s, t in items]


def params(**more):
    return pltpu.CompilerParams(vmem_limit_bytes=VMEM_LIMIT, **more)


def where_am_i():
    at = lax.axis_index("dp")
    return at // (NY * NX), lax.rem(at // NX, NY), lax.rem(at, NX), lax.axis_index("fsdp")


def chip(z, y, x):
    return (z * NY + y) * NX + x


def spread_tokens(values):
    t = lax.broadcasted_iota(jnp.int32, (8, 256), 0)
    p = lax.broadcasted_iota(jnp.int32, (8, 256), 1) // GROUP
    return mm(low(values.astype(F32)), low((t == p).astype(F32)))


def geometry(points_ref, tokens_ref, rel_ref, counts_s, picked_s):
    pieces = points_ref.shape[1] // 256
    lane = lax.rem(lax.broadcasted_iota(jnp.int32, (1, 256), 1), GROUP).astype(F32)
    counts_s[...] = spread_tokens(tokens_ref[...])
    for i in range(pieces):
        at = slice(256 * i, 256 * i + 256)
        pick = (lane == counts_s[pieces + i : pieces + i + 1, :]).astype(F32)
        rows = points_ref[:, at] * pick
        picked_s[8 * i : 8 * i + 8, :] = jnp.concatenate([rows, jnp.zeros((5, 256), F32)], axis=0)
    picked_s[...] = patch_sum(picked_s[...], patch_ones())
    for i in range(pieces):
        at = slice(256 * i, 256 * i + 256)
        valid = (lane < counts_s[i : i + 1, :]).astype(F32)
        relative = (points_ref[:, at] - picked_s[8 * i : 8 * i + 3, :]) * valid
        rel_ref[:, at] = low(jnp.concatenate([relative, valid, relative, valid], axis=0))
    rel = rel_ref[...]
    return mm_nt(rel, rel)


def prepare_one(moments, small):
    n = moments[3:4, 3:4]
    w = [small[k : k + 1, :] for k in range(3)]
    gain, shift = small[3:4, :], small[4:5, :]
    mean = sum(w[k] * moments[k : k + 1, 3:4] for k in range(3)) / n
    square = jnp.zeros_like(mean)
    for j in range(3):
        for k in range(3):
            square = square + w[j] * w[k] * moments[j : j + 1, k : k + 1]
    inverse = lax.rsqrt(square / n - mean * mean + EPS_NORM)
    scale = inverse * gain
    scaled = [wk * scale for wk in w]
    parts = [v * (1.0 / LAM) for v in scaled + [shift - mean * scale]]
    high = [low(v) for v in parts]
    rest = [low(v - h.astype(F32)) for v, h in zip(parts, high)]
    forward = jnp.concatenate(high + rest, axis=0)
    high = [low(v) for v in scaled]
    rest = [low(v - h.astype(F32)) for v, h in zip(scaled, high)]
    zero = jnp.zeros((1, C1), BF16)
    backward = jnp.concatenate(high + [zero] + rest + [zero], axis=0)
    stats = jnp.concatenate(
        [mean, inverse, jnp.broadcast_to(n, (1, C1)), scale, jnp.zeros((4, C1), F32)], axis=0
    )
    return forward, backward, stats


def flat_rows(pieces, length, rows):
    lane = lax.broadcasted_iota(jnp.int32, (1, 128), 1)
    out = [jnp.zeros((1, 128), F32) for _ in range(rows)]
    for r in range(pieces.shape[0]):
        row = jnp.where(lane < length, pieces[r : r + 1, :], 0.0)
        at = length * r
        row = pltpu.roll(row, at % 128, 1) if at % 128 else row
        first = at // 128
        out[first] = out[first] + jnp.where(lane >= at % 128, row, 0.0)
        if at % 128 + length > 128:
            out[first + 1] = out[first + 1] + jnp.where(lane < at % 128, row, 0.0)
    return jnp.concatenate(out, axis=0)


def piece_of(rows, at, length):
    lane = lax.broadcasted_iota(jnp.int32, (1, 128), 1)
    first, shift = at // 128, at % 128
    row = rows[first : first + 1, :]
    if shift:
        row = pltpu.roll(row, 128 - shift, 1)
        if shift + length > 128:
            other = pltpu.roll(rows[first + 1 : first + 2, :], 128 - shift, 1)
            row = jnp.where(lane < 128 - shift, row, other)
    return jnp.where(lane < length, row, 0.0)


def segments_apart(flat, small):
    lane = lax.broadcasted_iota(jnp.int32, (1, 128), 1)
    turned = pltpu.roll(flat, 128 - small, 1)
    return jnp.where(lane < 128 - small, pltpu.roll(turned, 1, 0), turned)


def segments_joined(rows, first, small):
    lane = lax.broadcasted_iota(jnp.int32, (1, 128), 1)
    turned = pltpu.roll(rows, small, 1)
    row = lax.broadcasted_iota(jnp.int32, (rows.shape[0], 1), 0)
    joined = jnp.where(lane < small, turned, pltpu.roll(turned, rows.shape[0] - 1, 0))
    return jnp.where((lane < small) & (row == 0), first, joined)


def first_tile(rel, wn, ext_ref, gp_ref):
    valid = rel[3:4, :].astype(F32)
    for j in range(TILE // 256):
        at = slice(256 * j, 256 * j + 256)
        g, d = gelu_twice(mm_tn(wn, rel[:, at]))
        ext_ref[0:C1, at] = low(g * (valid[:, at] * (0.5 * LAM)))
        gp_ref[:, at] = low(d * (valid[:, at] * 0.5))
    ext_ref[C1:, :] = jnp.concatenate([rel[3:4], jnp.zeros((15, TILE), BF16)], axis=0)


def first_tokens(gext, ps_ref, w2e, w3_ref, pooled_o, gm_o, fw_o):
    lower = w3_ref[C2:, :]
    count = ps_ref[:, C1 : C1 + 1]
    fs = mm_exact(ps_ref[:, 0 : C1 + 16], w2e)
    pooled = low(fs / count)
    pooled_o[...] = pooled
    g = mm(pooled, w3_ref[0:C2, :])
    gm_o[...] = g
    fw = mm_exact(fs, lower)
    fw_o[...] = fw
    gram = sum(mm_tn(w2e, part) for part in split_three(mm_exact(gext, w2e)))
    one = jnp.sum(fw + count * g, axis=0, keepdims=True)
    two = jnp.sum(mm_exact(gram, lower) * lower.astype(F32), axis=0, keepdims=True)
    two = two + jnp.sum(g * (2.0 * fw + count * g), axis=0, keepdims=True)
    return as_rows(one, two)


def third_vectors(totals, n, psmall_ref):
    mean = as_vector(totals, 0, 4) / n
    inverse = lax.rsqrt(as_vector(totals, 4, 4) / n - mean * mean + EPS_NORM)
    gain, shift = as_vector(psmall_ref, 7, 4), as_vector(psmall_ref, 11, 4)
    return jnp.concatenate([inverse * gain, shift, mean, inverse, jnp.zeros((4, C3), F32)], axis=0)


def second_tile(act, mask, w23, gm, sv_ref, gp_o, pa_o, pg_o, pc_o, first):
    scale, shift = low(sv_ref[0:1, :] * (1.0 / LAM)), low(sv_ref[1:2, :] * (1.0 / LAM))
    turned = act.T
    c = mm(jnp.concatenate([turned, turned], axis=1), w23).reshape(TOK, GROUP, C3) + gm[:, None, :]
    c = low(c)
    g, gp = gelu_twice(c * scale[None] + shift[None])
    gc = (gp * c).reshape(TILE, C3)
    gp = gp.reshape(TILE, C3)
    gp_o[...] = gp
    g = g.reshape(TILE, C3)
    for q in range(TILE // 256):
        to = pl.ds(pl.multiple_of(first + 8 * q, 8), 8)
        at = slice(256 * q, 256 * q + 256)
        m = mask[8 * q : 8 * q + 8, at]
        pa_o[to, :] = mm(m, g[at]) * (0.5 * LAM)
        pg_o[to, :] = mm(m, gp[at]) * 0.5
        pc_o[to, :] = mm(m, gc[at]) * 0.5


class Gather:
    def __init__(self, blocks, send, recv, base):
        self.blocks, self.sems, self.base = blocks, (send, recv), base
        z, y, x, core = where_am_i()
        half = blocks.shape[-1] // 2
        one, two = pl.ds(0, half), pl.ds(half, half)
        every = slice(None)
        near = [(chip(lax.rem(z + k, NZ), y, x), core) for k in range(1, NZ)]
        over_y, over_x, twin = (chip(z, 1 - y, x), core), (chip(z, y, 1 - x), core), (chip(z, y, x), 1 - core)
        self.stages = [
            [((z, y, x, core), peer) for peer in near],
            [((every, y, x, core, every, one), over_y), ((every, y, x, core, every, two), over_x)],
            [((every, every, x, core, every, one), over_x), ((every, y, every, core, every, two), over_y)],
            [],
        ]
        self.inner = [
            [],
            [((every, y, x, core), twin)],
            [((every, 1 - y, x, core, every, one), twin), ((every, y, 1 - x, core, every, two), twin)],
            [((every, every, 1 - x, core, every, one), twin), ((every, 1 - y, every, core, every, two), twin)],
        ]

    def copies(self, stage, inner):
        table = self.inner if inner else self.stages
        k = self.base + (7 if inner else 0) + sum(len(s) for s in table[:stage])
        out = []
        for i, (index, peer) in enumerate(table[stage]):
            view = self.blocks.at[index]
            out.append(
                pltpu.make_async_remote_copy(
                    src_ref=view, dst_ref=view, send_sem=self.sems[0].at[k + i], recv_sem=self.sems[1].at[k + i],
                    device_id=peer, device_id_type=MESH,
                )
            )
        return out

    def advance(self, stage):
        if stage > 0:
            for copy in self.copies(stage - 1, False):
                copy.wait()
        if stage < 4:
            for copy in self.copies(stage, False) + self.copies(stage, True):
                copy.start()
        else:
            for inner_stage in range(4):
                for copy in self.copies(inner_stage, True):
                    copy.wait()


GATHER_SEMS = 12
W4_AT, QKV_AT, WO_AT, WF1_AT, WF2_AT, REST_WIDTH = 0, 384, 1536, 1920, 3456, 3840
UNDER = [("wqkv", QKV_AT, 3 * D), ("wo", WO_AT, D), ("wf1", WF1_AT, FF)]


def rest_wf2(d):
    out = [(48 * d, 16, 0, WF2_AT)]
    out += [(48 * d + 16 + 4 * j, 4, 12, QKV_AT + D * j) for j in range(8)]
    return out


def place(d):
    return d // 8, d // 4 % 2, d // 2 % 2, d % 2


def forward_kernel(known, dp, *refs):
    refs = list(refs)
    take = lambda count: [refs.pop(0) for _ in range(count)]
    points_ref, tokens_ref, pflat, bflat = take(4) if known else [None] * 4
    rel_o, moment_o, psmall_o, bsmall_o, w2_o, w3_o = take(6)
    w4_o, wqkv_o, wo_o, wf1_o, wf2_o = take(5) if known else [None] * 5
    ext_o, gp1_o, g_o, ps_o, gm_o, fw_o, pooled_o, sv_o, stats_o, wd_o, w23_o, gp_o, pa_o, pg_o, pc_o = take(15)
    ext_s, e_s, wn_s, w2_s, w23_s, acc3, sums3, ssend3, srecv3 = take(9)
    step = pl.program_id(0)
    tiles = pl.num_programs(0) // 2
    peers = all_peers(dp)
    if known:
        (
            tiny, rest, three, stage, wide, flat2, pal, bal, counts_s, picked_s,
            tsend, trecv, gsend, grecv,
        ) = take(14)
        z, y, x, core = where_am_i()
        gather_w3 = Gather(three, gsend, grecv, 0)
        gather_rest = Gather(rest, gsend, grecv, GATHER_SEMS)

    @pl.when(step == 0)
    def _():
        greet(peers)
        g_o[...] = jnp.zeros_like(g_o)
        e_s[...] = token_ones()
        if known:
            pal[...] = segments_apart(pflat[...], PSMALL)
            bal[...] = segments_apart(bflat[...], BSMALL)
            for j in range(C3 // 128):
                three[z, y, x, core, :, 128 * j : 128 * j + 128] = low(pal[pl.ds(9 + j, 16, stride=C3 // 128), :])
            for j in range(D // 128):
                stage[:, 128 * j : 128 * j + 128] = pal[pl.ds(73 + j, 16, stride=D // 128), :]
            start = 1
            for name, at, cols in UNDER:
                for j in range(cols // 128):
                    stage[0:12, at + 128 * j : at + 128 * j + 128] = bal[pl.ds(start + j, 12, stride=cols // 128), :]
                start += 12 * cols // 128
            for row, rows, under, at in rest_wf2(0):
                for j in range(D // 128):
                    stage[under : under + rows, at + 128 * j : at + 128 * j + 128] = bal[
                        pl.ds(start + 3 * row + j, rows, stride=3), :
                    ]
            rest[z, y, x, core] = low(stage[...])
            moments = geometry(points_ref, tokens_ref, rel_o, counts_s, picked_s)[0:4, :]
            moments = jnp.concatenate([moments, jnp.zeros((4, 120), F32)], axis=1)
            hi, mid, lo = [part.astype(F32) for part in split_three(moments)]
            packed = hi + pltpu.roll(mid, 8, 1) + pltpu.roll(lo, 16, 1)
            rows = [pal[1:9, :], pflat[0:1, :], bflat[0:1, :], packed, jnp.zeros((2, 128), F32)]
            own = tiny.at[me()]
            own[...] = low(jnp.concatenate(rows, axis=0))
            greeted(peers)
            for copy in send_to_all(dp, own, lambda k: own, tsend, trecv):
                copy.wait()
            gather_w3.advance(0)
            gather_rest.advance(0)
            psmall, bsmall = [], []
            packed = jnp.zeros((4, 128), F32)
            for d in range(dp * NC):
                rows = tiny[d].astype(F32)
                flat2[8 * d : 8 * d + 8, :] = rows[0:8, :]
                psmall.append(rows[8:9, :])
                bsmall.append(rows[9:10, :])
                packed = packed + rows[10:14, :]
            total = packed + pltpu.roll(packed, 120, 1) + pltpu.roll(packed, 112, 1)
            moment_o[...] = jnp.concatenate([total, jnp.zeros((4, 128), F32)], axis=0)
            psmall_o[0:18, :] = flat_rows(jnp.concatenate(psmall, axis=0), PSMALL, 18)
            bsmall_o[0:30, :] = flat_rows(jnp.concatenate(bsmall, axis=0), BSMALL, 30)
            for j in range(2):
                w2_o[:, 128 * j : 128 * j + 128] = low(flat2[pl.ds(j, C1, stride=2), :])
        else:
            greeted(peers)
        small = psmall_o[...]
        forward, backward, stats = prepare_one(moment_o[:, 0:8], small)
        wn_s[...] = forward
        wd_o[...] = backward
        stats_o[...] = stats
        w2_s[0:C1, :] = w2_o[...]
        b2 = as_vector(small, 5, 2)
        w2_s[C1:, :] = low(jnp.concatenate([b2, jnp.zeros((15, C2), F32)], axis=0))

    if known:
        for at_step, gather, number in (
            (2, gather_w3, 1), (3, gather_w3, 2), (5, gather_w3, 3), (6, gather_rest, 1), (7, gather_w3, 4),
            (8, gather_rest, 2), (12, gather_rest, 3),
        ):
            pl.when(step == at_step)(functools.partial(gather.advance, number))

    at = pl.ds(pl.multiple_of(lax.rem(step, tiles) * TILE, TILE), TILE)
    rel = rel_o[:, at]
    first = pl.multiple_of(lax.rem(step, tiles) * TOK, TOK)

    @pl.when(step < tiles)
    def _():
        first_tile(rel, wn_s[...], ext_o, gp1_o)
        ext = ext_o[...]
        ext_s[:, at] = ext[0:C1]
        both = mm_nt(jnp.concatenate([ext, e_s[...]], axis=0), ext)
        g_o[:, 0 : C1 + 16] += both[0 : C1 + 16]
        ps_o[pl.ds(first, TOK), 0 : C1 + 16] = both[C1 + 16 :]

    @pl.when(step == tiles)
    def _():
        if known:
            for d in range(dp * NC):
                w3_o[16 * d : 16 * d + 16, :] = three[place(d)]
        acc3[...] = first_tokens(g_o[:, 0 : C1 + 16], ps_o, w2_s[...], w3_o, pooled_o, gm_o, fw_o)
        copies = sum_start(dp, acc3, sums3, ssend3, srecv3)
        w23 = mm(w2_s[...], w3_o[C2:, :])
        w23_o[...] = w23
        high = low(w23[0:C1])
        w23_s[0:C1, :] = high
        w23_s[C1:, :] = low(w23[0:C1] - high.astype(F32))
        sv_o[...] = third_vectors(sum_finish(acc3, sums3, copies), stats_o[2:3, 0:1], psmall_o)
        mean = sv_o[2:3, :]
        gm = gm_o[...] - mean
        fw_o[...] = fw_o[...] + ps_o[:, C1 : C1 + 1] * gm
        gm_o[...] = gm + w23[C1 : C1 + 1, :]

    @pl.when(step >= tiles)
    def _():
        second_tile(
            ext_s[:, at], e_s[...] * rel[3:4, :], w23_s[...], gm_o[pl.ds(first, TOK), :], sv_o,
            gp_o, pa_o, pg_o, pc_o, first,
        )

    if known:

        @pl.when(step == 2 * tiles - 1)
        def _():
            gather_rest.advance(4)
            for d in range(dp * NC):
                block = rest.at[place(d)]
                w4_o[16 * d : 16 * d + 16, :] = block[:, W4_AT : W4_AT + D]
                wf2_o[48 * d : 48 * d + 16, :] = block[:, WF2_AT : WF2_AT + D]
                under = block[:, QKV_AT:WF2_AT].astype(F32)
                wide[12 * d : 12 * d + 12, :] = under[0:12, :]
                tail = [under[12:16, D * j : D * j + D] for j in range(8)]
                wf2_o[48 * d + 16 : 48 * d + 48, :] = low(jnp.concatenate(tail, axis=0))
            for (name, at_col, cols), out in zip(UNDER, (wqkv_o, wo_o, wf1_o)):
                out[...] = low(wide[:, at_col - QKV_AT : at_col - QKV_AT + cols])


def forward_call(known, dp, count, *args):
    tokens, tiles = count // GROUP, count // TILE
    single = dict(pipeline_mode=pl.Buffered(1))
    full = lambda *s: pl.BlockSpec(s, lambda i: (0, 0), **single)
    early = lambda r: pl.BlockSpec((r, TILE), lambda i: (0, jnp.minimum(i, tiles - 1)))
    given = [
        ((8, count), BF16), ((8, 128), F32), ((24, 128), F32), ((32, 128), F32), ((C1, C2), BF16), ((2 * C2, C3), BF16),
    ]
    gathered = [((C3, D), BF16), ((D, 3 * D), BF16), ((D, D), BF16), ((D, FF), BF16), ((FF, D), BF16)]
    outs = [(full(*s), s, t) for s, t in given + gathered] if known else []
    outs += [(early(C1 + 16), (C1 + 16, count), BF16), (early(C1), (C1, count), BF16)]
    outs += [
        (full(*s), s, t)
        for s, t in (
            ((C1 + 16, 256), F32), ((tokens, 256), F32), ((tokens, C3), F32), ((tokens, C3), F32),
            ((tokens, C2), BF16), ((8, C3), F32), ((8, C1), F32), ((8, C1), BF16), ((C1 + 16, C3), F32),
        )
    ]
    outs += [(pl.BlockSpec((TILE, C3), lambda i: (jnp.maximum(i - tiles, 0), 0)), (count, C3), BF16)]
    outs += [(full(tokens, C3), (tokens, C3), F32)] * 3
    scratch = [
        pltpu.VMEM((C1, count), BF16), pltpu.VMEM((TOK, TILE), BF16), pltpu.VMEM((8, C1), BF16),
        pltpu.VMEM((C1 + 16, C2), BF16), pltpu.VMEM((2 * C1, C3), BF16),
    ] + sum_scratch(dp)
    if known:
        n = dp * NC
        scratch += [
            pltpu.VMEM((n, 16, 128), BF16),
            pltpu.VMEM((NZ, NY, NX, NC, 16, REST_WIDTH), BF16),
            pltpu.VMEM((NZ, NY, NX, NC, 16, C3), BF16),
            pltpu.VMEM((16, REST_WIDTH), F32),
            pltpu.VMEM((D, WF2_AT - QKV_AT), F32),
            pltpu.VMEM((8 * n, 128), F32),
            pltpu.VMEM((PROWS, 128), F32), pltpu.VMEM((BROWS, 128), F32),
            pltpu.VMEM((count // 128, 256), F32), pltpu.VMEM((count // 32, 256), F32),
            pltpu.SemaphoreType.DMA((n - 1,)), pltpu.SemaphoreType.DMA((n - 1,)),
            pltpu.SemaphoreType.DMA((2 * GATHER_SEMS,)), pltpu.SemaphoreType.DMA((2 * GATHER_SEMS,)),
        ]
    return pl.pallas_call(
        functools.partial(forward_kernel, known, dp),
        grid=(2 * tiles,),
        in_specs=[full(*a.shape) for a in args],
        out_specs=[o[0] for o in outs],
        out_shape=shaped(*[o[1:] for o in outs]),
        scratch_shapes=scratch,
        compiler_params=params(collective_id=0, has_side_effects=True),
        name="forward",
    )(*args)


def wide_row(ref, first, rows):
    return jnp.concatenate([ref[k : k + 1, :] for k in range(first, first + rows)], axis=1)


def layer_norm(v, gain, shift):
    centred = v - jnp.mean(v, -1, keepdims=True)
    inverse = lax.rsqrt(jnp.mean(centred * centred, -1, keepdims=True) + EPS_NORM)
    unit = centred * inverse
    return unit, inverse, low(unit * gain + shift)


def norm_back(d_unit, unit, inverse):
    return inverse * (
        d_unit - jnp.mean(d_unit, -1, keepdims=True) - unit * jnp.mean(d_unit * unit, -1, keepdims=True)
    )


def col_sum(v):
    return jnp.sum(v, axis=0, keepdims=True)


def block_kernel(
    pa_ref, pg_ref, pc_ref, cnt_ref, len_ref, cot_ref, psmall_ref, bsmall_ref, sv_ref,
    w4_ref, wqkv_ref, wo_ref, wf1_ref, wf2_ref,
    out_o, gw4_o, gwqkv_o, gwo_o, gwf1_o, gwf2_o, small_o, tok_o, tg_o, back_o,
    qkv_s, mixed_s, soft_s, dmix_s, dqkv_s,
):
    step = pl.program_id(0)

    @pl.when(step == 0)
    def _():
        for ref in (gw4_o, gwqkv_o, gwo_o, gwf1_o, gwf2_o, small_o, back_o):
            ref[...] = jnp.zeros_like(ref)

    count = cnt_ref[:, C1 : C1 + 1]
    scale = HEAD_DIM ** (-0.5)
    b4 = wide_row(psmall_ref, 15, 3)
    ln1_gain, ln1_shift, bo = wide_row(bsmall_ref, 0, 3), wide_row(bsmall_ref, 3, 3), wide_row(bsmall_ref, 6, 3)
    ln2_gain, ln2_shift = wide_row(bsmall_ref, 9, 3), wide_row(bsmall_ref, 12, 3)
    bf1, bf2 = wide_row(bsmall_ref, 15, 12), wide_row(bsmall_ref, 27, 3)

    act = low(pa_ref[...] / count)
    x_zero = mm(act, w4_ref[...]) + b4
    unit_a, inv_a, normed_a = layer_norm(x_zero, ln1_gain, ln1_shift)
    qkv_s[...] = low(mm(normed_a, wqkv_ref[...]))

    row_cloud = lax.broadcasted_iota(jnp.int32, (PAIR, PAIR), 0) // PATCHES
    col = lax.broadcasted_iota(jnp.int32, (PAIR, PAIR), 1)
    left = lax.broadcasted_iota(jnp.int32, (1, 128), 1) < HEAD_DIM
    zero = jnp.zeros((1, 1), BF16)

    def halves(v):
        return jnp.where(left, v, zero), jnp.where(left, zero, v)

    tiles = TB // PAIR
    for s in range(tiles):
        first = (step * tiles + s) * 2
        visible = (row_cloud == col // PATCHES) & (
            lax.rem(col, PATCHES) < jnp.where(col < PATCHES, len_ref[first], len_ref[first + 1])
        )
        rows = slice(PAIR * s, PAIR * s + PAIR)
        for p in range(HEADS // 2):
            at = 128 * p
            q = qkv_s[rows, at : at + 128]
            k = qkv_s[rows, D + at : D + at + 128]
            v = qkv_s[rows, 2 * D + at : 2 * D + at + 128]
            mixed = []
            for a, q_half in enumerate(halves(q)):
                score = jnp.where(visible, mm_nt(q_half, k) * scale, NEG_FILL)
                raised = jnp.exp(score - jnp.max(score, -1, keepdims=True))
                soft = raised / jnp.sum(raised, -1, keepdims=True)
                soft_s[(s * (HEADS // 2) + p) * 2 + a] = soft
                mixed.append(mm(low(soft), v))
            mixed_s[rows, at : at + 128] = low(jnp.where(left, mixed[0], mixed[1]))

    mixed_low = mixed_s[...]
    x_one = x_zero + mm(mixed_low, wo_ref[...]) + bo
    unit_b, inv_b, normed_b = layer_norm(x_one, ln2_gain, ln2_shift)
    hidden, d_hidden = gelu_pair(mm(normed_b, wf1_ref[...]) + bf1)
    hidden = low(hidden)
    out_o[...] = x_one + mm(hidden, wf2_ref[...]) + bf2

    cot = cot_ref[...]
    grad = low(cot)
    gwf2_o[...] += mm_tn(hidden, grad)
    d_pre = mm_nt(grad, wf2_ref[...]) * d_hidden
    d_pre_low = low(d_pre)
    gwf1_o[...] += mm_tn(normed_b, d_pre_low)
    d_normed_b = mm_nt(d_pre_low, wf1_ref[...])
    d_x_one = cot + norm_back(d_normed_b * ln2_gain, unit_b, inv_b)
    d_x_low = low(d_x_one)
    gwo_o[...] += mm_tn(mixed_low, d_x_low)
    dmix_s[...] = low(mm_nt(d_x_low, wo_ref[...]))

    for s in range(tiles):
        rows = slice(PAIR * s, PAIR * s + PAIR)
        for p in range(HEADS // 2):
            at = 128 * p
            q = qkv_s[rows, at : at + 128]
            k = qkv_s[rows, D + at : D + at + 128]
            v = qkv_s[rows, 2 * D + at : 2 * D + at + 128]
            dm = dmix_s[rows, at : at + 128]
            d_q, d_k, d_v = [], [], []
            for a, dm_half in enumerate(halves(dm)):
                soft = soft_s[(s * (HEADS // 2) + p) * 2 + a]
                d_soft = mm_nt(dm_half, v)
                d_v.append(mm_tn(low(soft), dm))
                d_score = low(soft * (d_soft - jnp.sum(soft * d_soft, -1, keepdims=True)))
                d_q.append(mm(d_score, k))
                d_k.append(mm_tn(d_score, q))
            dqkv_s[rows, at : at + 128] = low(jnp.where(left, d_q[0], d_q[1]) * scale)
            dqkv_s[rows, D + at : D + at + 128] = low(jnp.where(left, d_k[0], d_k[1]) * scale)
            dqkv_s[rows, 2 * D + at : 2 * D + at + 128] = low(jnp.where(left, d_v[0], d_v[1]))

    d_qkv = dqkv_s[...]
    gwqkv_o[...] += mm_tn(normed_a, d_qkv)
    d_normed_a = mm_nt(d_qkv, wqkv_ref[...])
    d_x_zero = d_x_one + norm_back(d_normed_a * ln1_gain, unit_a, inv_a)
    d_x_low = low(d_x_zero)
    gw4_o[...] += mm_tn(act, d_x_low)
    token = mm_nt(d_x_low, w4_ref[...]) / count
    tok_o[...] = token
    grouped = token * pg_ref[...]
    tg_o[...] = grouped
    back_o[0:1, :] += col_sum(grouped)
    back_o[1:2, :] += col_sum(token * pc_ref[...]) * sv_ref[3:4, :]
    narrow = [
        col_sum(d_normed_a * unit_a), col_sum(d_normed_a), col_sum(d_x_one),
        col_sum(d_normed_b * unit_b), col_sum(d_normed_b), col_sum(cot), col_sum(d_x_zero),
    ]
    for k, row in enumerate(narrow):
        small_o[k : k + 1, 0:D] += row
    small_o[7:8, :] += col_sum(d_pre)


def third_back_tokens(
    totals, tg_ref, sc_ref, gm_ref, ps_ref, pooled_ref, gext_ref, w2_ref, w3_ref, w23_ref, sv_ref, stats_ref,
    kap_o, k_o, wb_o, top_o, corr_o, base_o,
):
    gain = sv_ref[0:1, :]
    n = stats_ref[2:3, 0:1]
    alpha = gain * as_vector(totals, 0, 4) / n
    beta = gain * as_vector(totals, 4, 4) * sv_ref[3:4, :] / n
    count = ps_ref[:, C1 : C1 + 1]
    w23 = w23_ref[...]
    act = low(w23[0:C1])
    per_token = low(gain * tg_ref[...] - (count * alpha + beta * sc_ref[...]))
    pooled = low(mm_nt(per_token, w3_ref[0:C2, :]) / count)
    shifted = low(alpha + beta * gm_ref[...])
    kap_o[...] = low(mm_nt(pooled, w2_ref[...]) - mm_nt(shifted, act))
    k_o[:, 0:C1] = low(-mm_nt(low(w23[0:C1] * beta), act))
    wb_o[...] = low(w23[0:C1] * gain)
    top_o[...] = mm_tn(pooled_ref[...], per_token)
    sums = low(ps_ref[:, 0 : C1 + 16])
    corr_o[...] = mm_tn(sums, shifted) + beta * mm(low(gext_ref[:, 0:C1]), act)
    base_o[...] = mm_tn(sums, pooled)


def last_tile(gp_ref, ext_ref, gp1_ref, rel, tok, kap, k_s, xe_s, wb_ref, wd_ref, h_o, q_o, d_at):
    dn = (gp_ref[...].reshape(TOK, GROUP, C3) * tok[:, None, :]).reshape(TILE, C3)
    xe_s[0:C1, :] = ext_ref[0:C1, :]
    k_s[:, C1 : C1 + TOK] = kap.T
    h_o[...] += mm(ext_ref[...], dn)
    d_act = mm_nt(wb_ref[...], dn) + mm(k_s[...], xe_s[...])
    d_one = low(d_act * gp1_ref[...].astype(F32))
    d_at(mm(wd_ref[...], d_one))
    q_o[...] += mm_nt(rel, d_one)


def last_weights(h, gain, corr, base, w2e, w3_ref):
    m = h * gain - corr
    parts = split_three(m)[0:2]
    grad_w3 = sum(mm_tn(w2e, part) for part in parts)
    return grad_w3, sum(mm_nt(part, w3_ref[C2:, :]) for part in parts) + base


def first_grads(q, moments, psmall, stats):
    mean, inverse, n, scale = stats[0:1], stats[1:2], stats[2:3], stats[3:4]
    w = [psmall[k : k + 1, :] for k in range(3)]
    one = q[3:4, :]
    two = inverse * (sum(w[k] * q[k : k + 1, :] for k in range(3)) - mean * one)
    grad_w = []
    for k in range(3):
        along = sum(w[j] * moments[k : k + 1, j : j + 1] for j in range(3)) - mean * moments[k : k + 1, 3:4]
        grad_w.append(scale * (q[k : k + 1, :] - (one * moments[k : k + 1, 3:4] + two * inverse * along) / n))
    flat = [
        jnp.sum(scale * w[k] * (one - two * inverse * mean) / n, axis=1, keepdims=True) for k in range(3)
    ]
    slope = [
        [jnp.sum(scale * w[k] * two * inverse * w[j] / n, axis=1, keepdims=True) for j in range(3)]
        for k in range(3)
    ]
    return grad_w, two, one, flat, slope


def point_gradient(d_ref, rel_ref, tokens_ref, flat, slope, out_ref, spread_s, sums_s):
    pieces = d_ref.shape[1] // 256
    lane = lax.rem(lax.broadcasted_iota(jnp.int32, (1, 256), 1), GROUP).astype(F32)
    base = jnp.concatenate(flat, axis=0)
    columns = [jnp.concatenate([slope[k][j] for k in range(3)], axis=0) for j in range(3)]
    spread_s[...] = spread_tokens(tokens_ref[pieces : 2 * pieces, :])
    for i in range(pieces):
        at = slice(256 * i, 256 * i + 256)
        rel = rel_ref[:, at].astype(F32)
        d = d_ref[:, at]
        out = d[0:3] + d[4:7] - rel[3:4] * base
        for j in range(3):
            out = out - columns[j] * rel[j : j + 1]
        out_ref[:, at] = out
        sums_s[8 * i : 8 * i + 8, :] = jnp.concatenate([out, jnp.zeros((5, 256), F32)], axis=0)
    sums_s[...] = patch_sum(sums_s[...], patch_ones())
    for i in range(pieces):
        at = slice(256 * i, 256 * i + 256)
        pick = (lane == spread_s[i : i + 1, :]).astype(F32)
        out_ref[:, at] = out_ref[:, at] - pick * sums_s[8 * i : 8 * i + 3, :]


def point_small_rows(grad_w, gain1, shift1, b2, tot, b4):
    rows = list(grad_w) + [gain1, shift1]
    rows += [b2[:, 128 * k : 128 * k + 128] for k in range(2)]
    rows += [tot[4:8, :], tot[0:4, :]]
    rows += [b4[:, 128 * k : 128 * k + 128] for k in range(3)]
    return jnp.concatenate(rows, axis=0)


def block_small_rows(small_ref):
    rows = [small_ref[k : k + 1, 128 * j : 128 * j + 128] for k in range(5) for j in range(3)]
    rows += [small_ref[7:8, 128 * j : 128 * j + 128] for j in range(12)]
    rows += [small_ref[5:6, 128 * j : 128 * j + 128] for j in range(3)]
    return jnp.concatenate(rows, axis=0)


class Scatter:
    def __init__(self, blocks, lands, send, recv, base):
        self.blocks, self.lands, self.sems, self.base = blocks, lands, (send, recv), base
        z, y, x, core = self.at = where_am_i()
        half = blocks.shape[-1] // 2
        self.one, self.two = pl.ds(0, half), pl.ds(half, half)
        every = slice(None)
        mine = blocks.at[core]
        near = [(chip(lax.rem(z + k, NZ), y, x), core) for k in range(1, NZ)]
        over_y, over_x, twin = (chip(z, 1 - y, x), core), (chip(z, y, 1 - x), core), (chip(z, y, x), 1 - core)
        land1, land2, land3, land4 = lands
        self.stages = [
            [(blocks.at[1 - core], land1, twin)],
            [
                (mine.at[:, :, 1 - x, :, self.one], land2.at[0], over_x),
                (mine.at[:, 1 - y, :, :, self.two], land2.at[1], over_y),
            ],
            [
                (mine.at[:, 1 - y, x, :, self.one], land3.at[0], over_y),
                (mine.at[:, y, 1 - x, :, self.two], land3.at[1], over_x),
            ],
            [(mine.at[lax.rem(z + k, NZ), y, x], land4.at[k - 1], near[k - 1]) for k in range(1, NZ)],
        ]

    def copies(self, stage):
        k = self.base + sum(len(s) for s in self.stages[:stage])
        return [
            pltpu.make_async_remote_copy(
                src_ref=src, dst_ref=dst, send_sem=self.sems[0].at[k + i], recv_sem=self.sems[1].at[k + i],
                device_id=peer, device_id_type=MESH,
            )
            for i, (src, dst, peer) in enumerate(self.stages[stage])
        ]

    def advance(self, stage):
        z, y, x, core = self.at
        mine = self.blocks.at[core]
        land1, land2, land3, land4 = self.lands
        if stage > 0:
            for copy in self.copies(stage - 1):
                copy.wait()
        if stage == 1:
            for cz in range(NZ):
                for cy in range(NY):
                    for cx in range(NX):
                        mine[cz, cy, cx] = mine[cz, cy, cx] + land1[cz, cy, cx]
        if stage == 2:
            for cz in range(NZ):
                for k in range(2):
                    mine[cz, k, x, :, self.one] = mine[cz, k, x, :, self.one] + land2[0, cz, k]
                    mine[cz, y, k, :, self.two] = mine[cz, y, k, :, self.two] + land2[1, cz, k]
        if stage == 3:
            for cz in range(NZ):
                mine[cz, y, x, :, self.one] = mine[cz, y, x, :, self.one] + land3[0, cz]
                mine[cz, y, x, :, self.two] = mine[cz, y, x, :, self.two] + land3[1, cz]
        if stage < 4:
            for copy in self.copies(stage):
                copy.start()
            return None
        total = mine[z, y, x].astype(F32)
        for k in range(NZ - 1):
            total = total + land4[k].astype(F32)
        return total


SCATTER_SEMS = 8
POINT_WIDTH = 768


def scatter_scratch(width):
    return [
        pltpu.VMEM((NC, NZ, NY, NX, 16, width), BF16),
        pltpu.VMEM((NZ, NY, NX, 16, width), BF16),
        pltpu.VMEM((2, NZ, 2, 16, width // 2), BF16),
        pltpu.VMEM((2, NZ, 16, width // 2), BF16),
        pltpu.VMEM((NZ - 1, 16, width), BF16),
    ]


def backward_kernel(known, dp, *refs):
    refs = list(refs)
    take = lambda count: [refs.pop(0) for _ in range(count)]
    pa_ref, pg_ref, pc_ref, ps_ref, len_ref, cot_ref, psmall_ref, bsmall_ref, sv_ref, stats_ref, moment_ref = take(11)
    w2_ref, w3_ref, w4_ref, wqkv_ref, wo_ref, wf1_ref, wf2_ref, w23_ref = take(8)
    sc_ref, gm_ref, pooled_ref, gext_ref, wd_ref, rel_ref, tokens_ref, gp_ref, ext_ref, gp1_ref = take(10)
    out_o, pg_o = take(2)
    if known:
        pflat_o, bflat_o = take(2)
        gw4_s, gwqkv_s, gwo_s, gwf1_s, gwf2_s = None, None, None, None, None
    else:
        prow_o, brow_o, gw2_o, gw3_o = take(4)
        gw4_s, gwqkv_s, gwo_s, gwf1_s, gwf2_s = take(5)
    small_s, tok_s, tg_s, back_s, qkv_s, mixed_s, soft_s, dmix_s, dqkv_s = take(9)
    tot_s, kap_s, k_s, wb_s, top_s, corr_s, base_s, h_s, q_s, d_s, xe_s, spread_s, sums_s = take(13)
    acc, slots, ssend, srecv, acc3, slots3, ssend3, srecv3 = take(8)
    step = pl.program_id(0)
    steps = pl.num_programs(0)
    peers = all_peers(dp)
    if known:
        gw4_s, gwqkv_s, gwo_s, gwf1_s, gwf2_s = take(5)
        rest0, rest1, rest2, rest3, rest4, point0, point1, point2, point3, point4 = take(10)
        stage, pstage, pal, bal, gsend, grecv = take(6)
        z, y, x, core = where_am_i()
        rest = Scatter(rest0, (rest1, rest2, rest3, rest4), gsend, grecv, 0)
        point = Scatter(point0, (point1, point2, point3, point4), gsend, grecv, SCATTER_SEMS)
    blocks = ps_ref.shape[0] // TB

    @pl.when(step == 0)
    def _():
        greet(peers)

    @pl.when(step < blocks)
    def _():
        rows = pl.ds(pl.multiple_of(step * TB, TB), TB)
        block_kernel(
            pa_ref, pg_ref, pc_ref, ps_ref.at[rows], len_ref, cot_ref, psmall_ref, bsmall_ref, sv_ref,
            w4_ref, wqkv_ref, wo_ref, wf1_ref, wf2_ref,
            out_o, gw4_s, gwqkv_s, gwo_s, gwf1_s, gwf2_s, small_s, tok_s.at[rows], tg_s.at[rows], back_s,
            qkv_s, mixed_s, soft_s, dmix_s, dqkv_s,
        )

    @pl.when(step == blocks - 1)
    def _():
        greeted(peers)
        acc3[...] = as_rows(back_s[0:1, :], back_s[1:2, :])
        copies = sum_start(dp, acc3, slots3, ssend3, srecv3)
        if known:
            for d in range(dp * NC):
                stage[:, W4_AT : W4_AT + D] = gw4_s[16 * d : 16 * d + 16, :]
                for (name, at, cols), ref in zip(UNDER, (gwqkv_s, gwo_s, gwf1_s)):
                    stage[0:12, at : at + cols] = ref[12 * d : 12 * d + 12, :]
                for row, rows, under, at in rest_wf2(d):
                    stage[under : under + rows, at : at + D] = gwf2_s[row : row + rows, :]
                cz, cy, cx, cc = place(d)
                rest0[cc, cz, cy, cx] = low(stage[...])
            rest.advance(0)
        for ref in (h_s, q_s):
            ref[...] = jnp.zeros_like(ref)
        xe_s[C1:, :] = token_ones()
        if known:
            rest.advance(1)
        tot_s[...] = sum_finish(acc3, slots3, copies)
        third_back_tokens(
            tot_s[...], tg_s, sc_ref, gm_ref, ps_ref, pooled_ref, gext_ref, w2_ref, w3_ref, w23_ref, sv_ref, stats_ref,
            kap_s, k_s, wb_s, top_s, corr_s, base_s,
        )

    if known:
        for at_step, number in ((5, 2), (7, 3)):
            pl.when(step == at_step)(functools.partial(rest.advance, number))

    @pl.when(step >= blocks)
    def _():
        tile = step - blocks
        at = pl.ds(pl.multiple_of(tile * TILE, TILE), TILE)
        ts = pl.ds(pl.multiple_of(tile * TOK, TOK), TOK)

        def put(d):
            d_s[:, at] = d

        last_tile(
            gp_ref, ext_ref, gp1_ref, rel_ref[:, at], low(tok_s[ts, :] * 0.5), kap_s[ts, :], k_s, xe_s, wb_s, wd_ref,
            h_s, q_s, put,
        )

    @pl.when(step == steps - 1)
    def _():
        acc[...] = q_s[...]
        copies = sum_start(dp, acc, slots, ssend, srecv)
        b2 = as_vector(psmall_ref, 5, 2)
        w2e = jnp.concatenate([w2_ref[...], low(jnp.concatenate([b2, jnp.zeros((15, C2), F32)], axis=0))], axis=0)
        gw3, gw2 = last_weights(h_s[...], sv_ref[0:1, :], corr_s[...], base_s[...], w2e, w3_ref)
        none = jnp.zeros((1, 128), F32)
        prow = point_small_rows([none] * 3, none, none, gw2[C1 : C1 + 1, :], jnp.zeros((8, 128), F32), small_s[6:7, 0:D])
        brow = block_small_rows(small_s)
        if known:
            pstage[...] = jnp.zeros_like(pstage)
            for d in range(dp * NC):
                if d < 16:
                    pstage[:, 0:C3] = top_s[16 * d : 16 * d + 16, :]
                else:
                    pstage[:, 0:C3] = gw3[16 * (d - 16) : 16 * (d - 16) + 16, :]
                pstage[0:4, C3 : C3 + C2] = gw2[4 * d : 4 * d + 4, :]
                pstage[4:5, C3 : C3 + 128] = piece_of(prow, PSMALL * d, PSMALL)
                pstage[5:6, C3 : C3 + 128] = piece_of(brow, BSMALL * d, BSMALL)
                cz, cy, cx, cc = place(d)
                point0[cc, cz, cy, cx] = low(pstage[...])
            point.advance(0)
            point.advance(1)
        totals = sum_finish(acc, slots, copies)
        grad_w, gain1, shift1, flat, slope = first_grads(totals, moment_ref[...], psmall_ref[...], stats_ref[...])
        full_rows = point_small_rows(grad_w, gain1, shift1, jnp.zeros((1, C2), F32), tot_s[...], jnp.zeros((1, D), F32))
        if known:
            point.advance(2)
            stage[...] = rest.advance(4)
            point.advance(3)
        point_gradient(d_s, rel_ref, tokens_ref, flat, slope, pg_o, spread_s, sums_s)
        if not known:
            prow_o[0:18, :] = prow + full_rows * (1.0 / (dp * NC))
            brow_o[0:30, :] = brow
            gw2_o[...] = gw2[0:C1]
            gw3_o[0:C2, :] = top_s[...]
            gw3_o[C2:, :] = gw3
            return
        own = jnp.zeros((1, 128), F32)
        for d in range(dp * NC):
            own = own + jnp.where(me() == d, piece_of(full_rows, PSMALL * d, PSMALL), 0.0)
        for j in range(D // 128):
            pal[pl.ds(73 + j, 16, stride=3), :] = stage[:, 128 * j : 128 * j + 128]
        start = 1
        for name, at, cols in UNDER:
            for j in range(cols // 128):
                bal[pl.ds(start + j, 12, stride=cols // 128), :] = stage[0:12, at + 128 * j : at + 128 * j + 128]
            start += 12 * cols // 128
        for row, rows, under, at in rest_wf2(0):
            for j in range(D // 128):
                bal[pl.ds(start + 3 * row + j, rows, stride=3), :] = stage[
                    under : under + rows, at + 128 * j : at + 128 * j + 128
                ]
        pstage[...] = point.advance(4)
        for j in range(C2 // 128):
            pal[pl.ds(1 + j, 4, stride=2), :] = pstage[0:4, C3 + 128 * j : C3 + 128 * j + 128]
        for j in range(C3 // 128):
            pal[pl.ds(9 + j, 16, stride=4), :] = pstage[:, 128 * j : 128 * j + 128]
        pflat_o[...] = segments_joined(pal[...], pstage[4:5, C3 : C3 + 128] + own, PSMALL)
        bflat_o[...] = segments_joined(bal[...], pstage[5:6, C3 : C3 + 128], BSMALL)


def backward_call(known, dp, *args):
    count = args[24].shape[1]
    tokens, blocks, tiles = count // GROUP, count // GROUP // TB, count // TILE
    single = dict(pipeline_mode=pl.Buffered(1))
    full = lambda *s: pl.BlockSpec(s, lambda i: (0, 0), **single)
    chunk = lambda c: pl.BlockSpec((TB, c), lambda i: (jnp.minimum(i, blocks - 1), 0))
    cols = lambda r: pl.BlockSpec((r, TILE), lambda i: (0, jnp.maximum(i - blocks, 0)))
    specs = [chunk(C3), chunk(C3), chunk(C3), full(tokens, 256), pl.BlockSpec(memory_space=pltpu.SMEM), chunk(D)]
    specs += [full(*a.shape) for a in args[6:26]]
    specs += [pl.BlockSpec((TILE, C3), lambda i: (jnp.maximum(i - blocks, 0), 0)), cols(C1 + 16), cols(C1)]
    grads = [((C3, D), F32), ((D, 3 * D), F32), ((D, D), F32), ((D, FF), F32), ((FF, D), F32)]
    outs = [(chunk(D), (tokens, D), F32), (full(3, count), (3, count), F32)]
    if known:
        outs += [(full(*s), s, t) for s, t in (((PROWS, 128), F32), ((BROWS, 128), F32))]
    else:
        more = [((24, 128), F32), ((32, 128), F32), ((C1, C2), F32), ((2 * C2, C3), F32)] + grads
        outs += [(full(*s), s, t) for s, t in more]
    pieces = count // 256
    scratch = [
        pltpu.VMEM((8, FF), F32), pltpu.VMEM((tokens, C3), F32), pltpu.VMEM((tokens, C3), F32), pltpu.VMEM((8, C3), F32),
        pltpu.VMEM((TB, 3 * D), BF16), pltpu.VMEM((TB, D), BF16),
        pltpu.VMEM((TB // PAIR * HEADS, PAIR, PAIR), F32), pltpu.VMEM((TB, D), BF16), pltpu.VMEM((TB, 3 * D), BF16),
        pltpu.VMEM((8, 128), F32), pltpu.VMEM((tokens, C1), BF16), pltpu.VMEM((C1, C1 + TOK), BF16),
        pltpu.VMEM((C1, C3), BF16), pltpu.VMEM((C2, C3), F32), pltpu.VMEM((C1 + 16, C3), F32),
        pltpu.VMEM((C1 + 16, C2), F32), pltpu.VMEM((C1 + 16, C3), F32), pltpu.VMEM((8, C1), F32),
        pltpu.VMEM((8, count), F32), pltpu.VMEM((C1 + TOK, TILE), BF16),
        pltpu.VMEM((pieces, 256), F32), pltpu.VMEM((8 * pieces, 256), F32),
    ]
    scratch += sum_scratch(dp) + sum_scratch(dp)
    if known:
        scratch += [pltpu.VMEM(s, t) for s, t in grads]
        scratch += scatter_scratch(REST_WIDTH) + scatter_scratch(POINT_WIDTH)
        scratch += [
            pltpu.VMEM((16, REST_WIDTH), F32), pltpu.VMEM((16, POINT_WIDTH), F32),
            pltpu.VMEM((PROWS, 128), F32), pltpu.VMEM((BROWS, 128), F32),
            pltpu.SemaphoreType.DMA((2 * SCATTER_SEMS,)), pltpu.SemaphoreType.DMA((2 * SCATTER_SEMS,)),
        ]
    return pl.pallas_call(
        functools.partial(backward_kernel, known, dp),
        grid=(blocks + tiles,),
        in_specs=specs,
        out_specs=[o[0] for o in outs],
        out_shape=shaped(*[o[1:] for o in outs]),
        scratch_shapes=scratch,
        compiler_params=params(collective_id=1, has_side_effects=True),
        name="backward",
    )(*args)


def geometry_kernel(points_ref, tokens_ref, rel_o, moment_o, counts_s, picked_s):
    moment_o[...] = jnp.concatenate(
        [geometry(points_ref, tokens_ref, rel_o, counts_s, picked_s), jnp.zeros((8, 120), F32)], axis=1
    )


def geometry_call(points, tokens):
    count = points.shape[1]
    return pl.pallas_call(
        geometry_kernel,
        out_shape=shaped(((8, count), BF16), ((8, 128), F32)),
        in_specs=vmem(2),
        out_specs=vmem(2),
        scratch_shapes=[pltpu.VMEM((count // 128, 256), F32), pltpu.VMEM((count // 32, 256), F32)],
        compiler_params=params(),
        name="geometry",
    )(points, tokens)


def gather_plain(points, tokens, point_master, block_master, devices):
    rel, moments = geometry_call(points, tokens)
    moments = lax.psum(moments, AXES)
    tables = []
    for master, layout in ((point_master, point_layout()), (block_master, block_layout())):
        offset = 0
        parts = []
        for seg_len in segment_lengths(layout, devices):
            piece = master[offset : offset + seg_len // devices].astype(BF16)
            offset += seg_len // devices
            parts.append(lax.all_gather(piece, AXES, axis=0, tiled=True))
        tables.append(parts)
    (ps, w2, w3, w4), (bs, wqkv, wo, wf1, wf2) = tables

    def rows_of(v, rows, used):
        v = v[:used].astype(F32).reshape(-1, 128)
        return jnp.concatenate([v, jnp.zeros((rows - v.shape[0], 128), F32)], axis=0)

    small = (rel, moments, rows_of(ps, 24, 18 * 128), rows_of(bs, 32, 30 * 128))
    point = (w2.reshape(C1, C2), w3.reshape(2 * C2, C3))
    block = (w4.reshape(C3, D), wqkv.reshape(D, 3 * D), wo.reshape(D, D), wf1.reshape(D, FF), wf2.reshape(FF, D))
    return small + point, block


def scatter_plain(devices, prow, brow, gw2, gw3, gw4, gwqkv, gwo, gwf1, gwf2):
    pieces = []
    for layout, tables in (
        (point_layout(), (prow[:18], gw2, gw3, gw4)),
        (block_layout(), (brow[:30], gwqkv, gwo, gwf1, gwf2)),
    ):
        parts = []
        for values, seg_len in zip(tables, segment_lengths(layout, devices)):
            values = values.reshape(-1)
            values = jnp.concatenate([values, jnp.zeros((seg_len - values.shape[0],), F32)])
            parts.append(lax.psum_scatter(values, AXES, scatter_dimension=0, tiled=True))
        pieces.append(parts)
    return pieces


def adam_update(master, moment_one, moment_two, gradient, step_rates, decays):
    one_new = BETA_ONE * moment_one + (1.0 - BETA_ONE) * gradient
    two_new = BETA_TWO * moment_two + (1.0 - BETA_TWO) * gradient * gradient
    fix_one = 1.0 - BETA_ONE**STEP
    fix_two = 1.0 - BETA_TWO**STEP
    direction = one_new / fix_one / (jnp.sqrt(two_new / fix_two) + ADAM_EPS)
    master_new = master - step_rates * (direction + decays * master)
    return (master_new, one_new, two_new)


def flat_of(vector, rows):
    return jnp.pad(vector, (0, rows * 128 - vector.shape[0])).reshape(rows, 128)


def on_device(
    points, point_count, centre_slot, cloud_length, cotangent, point_master, block_master,
    point_first, block_first, point_second, block_second,
):
    dp, fsdp = lax.axis_size("dp"), lax.axis_size("fsdp")
    devices = dp * fsdp
    own_rank = lax.axis_index(AXES)
    known = dp == NZ * NY * NX and fsdp == NC
    count = points.shape[1]
    tokens = jnp.concatenate([point_count, centre_slot]).reshape(-1, 8)
    if known:
        outs = forward_call(
            True, dp, count, points, tokens, flat_of(point_master, PROWS), flat_of(block_master, BROWS)
        )
        given, block, outs = outs[:6], outs[6:11], outs[11:]
    else:
        given, block = gather_plain(points, tokens, point_master, block_master, devices)
        outs = forward_call(False, dp, count, *given)
    rel, moments, psmall, bsmall, w2, w3 = given
    ext, gp1, gext, ps, gm, sc, pooled, sv, stats, wd, w23, gp, pa, pg, pc = outs
    outs = backward_call(
        known, dp, pa, pg, pc, ps, cloud_length, cotangent, psmall, bsmall, sv, stats, moments,
        w2, w3, *block, w23, sc, gm, pooled, gext, wd, rel, tokens, gp, ext, gp1,
    )
    tokens_out, point_grad = outs[:2]
    if known:
        point_gradient_vec = outs[2].reshape(-1)[: point_master.shape[0]]
        block_gradient = outs[3].reshape(-1)[: block_master.shape[0]]
        block_small = block_gradient[:BSMALL]
    else:
        point_parts, block_parts = scatter_plain(devices, *outs[2:])
        block_small = block_parts[0]
        point_gradient_vec = jnp.concatenate(point_parts)
        block_gradient = jnp.concatenate(block_parts)
    point_rates, point_decays = shard_rates(point_layout(), devices, own_rank)
    block_rates, block_decays = shard_rates(block_layout(), devices, own_rank)
    point_new, point_one, point_two = adam_update(
        point_master, point_first, point_second, point_gradient_vec, point_rates, point_decays
    )
    block_new, block_one, block_two = adam_update(
        block_master, block_first, block_second, block_gradient, block_rates, block_decays
    )
    return (
        tokens_out, point_grad, point_new, block_new, point_one, block_one, point_two, block_two,
        point_new.astype(BF16), block_new.astype(BF16), block_small,
    )


def solution(mesh):
    split = P(AXES)
    return jax.shard_map(
        on_device,
        mesh=mesh,
        in_specs=(P(None, AXES), split, split, split, P(AXES, None)) + (split,) * 6,
        out_specs=(P(AXES, None), P(None, AXES)) + (split,) * 9,
        check_vma=False,
    )
```

time: 202 us -> 173 us (0.86)
  Pallas kernels: 181 us -> 157 us
  local copies, waits for them, and re-layouts: 16.7 us -> 10.6 us
    pallas_call x2, Pallas kernels: 181 us -> 157 us  [the longest x1 85.3 us: backward_call(): pl.pallas_call(functools.partial(backward_kernel, known, dp), grid=(block...]
    slice x8 -> x1, local copies, waits for them, and re-layouts: 6.6 us -> 1.19 us  [on_device(): block_small = block_gradient[:BSMALL]]
    concatenate x2 -> x3, local copies, waits for them, and re-layouts: 4.17 us -> 1.53 us  [on_device(): tokens = jnp.concatenate([point_count, centre_slot]).reshape(-1, 8)]
    reshape x1 -> x2, local copies, waits for them, and re-layouts: 0.96 us -> 3.14 us  [flat_of(): return jnp.pad(vector, (0, rows * 128 - vector.shape[0])).reshape(rows, 128)]
where the time goes in v4:
time: 173 us
  Pallas kernels  157 us (91%)
  local copies, waits for them, and re-layouts  10.6 us (6%)
  other arithmetic  3.59 us (2%)
    pallas_call x1, Pallas kernels, backward_call(): pl.pallas_call(functools.partial(backward_kernel, known, dp), grid=(block...  85.3 us
    pallas_call x1, Pallas kernels, forward_call(): pl.pallas_call(functools.partial(forward_kernel, known, dp), grid=(2 * ti...  72.1 us

profile of v4, /device:TPU:0, one launch (start us, length us, event | category | flops | bytes accessed | tf_op | source)
XLA Modules:
  0.0 172.6 jit_solution(11106347870700811700)
XLA Ops:
  0.6 0.8 concatenate.20
  1.4 0.8 concatenate.21
  2.2 0.0 copy-start.2
  2.2 1.7 pad_bitcast_fusion.refs_3_
  3.9 1.5 pad_bitcast_fusion.1.refs_2_
  5.4 0.0 copy-done.2
  5.4 72.1 %forward.1 = (bf16[8,16384]{1,0:T(8,128)(2,1)}, f32[8,128]{1,0:T(8,128)}, f32[24,128]{1,0:T(8,128)}, f32[32,128]{1,0:T(8,128)}, bf16[128,256]{1,0:T(8,128)(2,1)}...) custom-call(f32[3,16384]{1,0:T(4,128)} %refs_0_.1, ...), custom_call_target="tpu_custom_call" | custom-call | tf_op jit(solution)/shard_map/forward/pallas_call | solution.py:653
  77.5 0.0 copy-start
  77.5 0.0 copy-start.5
  77.5 0.0 copy-start.6
  77.5 0.0 copy-start.3
  77.6 0.0 copy-start.7
  77.6 0.0 copy-start.8
  77.6 85.3 %backward.1 = (f32[512,384]{1,0:T(8,128)}, f32[3,16384]{1,0:T(4,128)}, f32[128,128]{1,0:T(8,128)}, f32[440,128]{1,0:T(8,128)}) custom-call(f32[512,512]{1,0:T(8,128)} %get-tuple-element.41.refs_0_, f32[512,512]{1,0:T(8,128)} %get-tuple-element.42.refs_1_, f32[512,512]{1,0:T(8,128)} %get-tuple-element.43.refs_2_, f32[512,256]{1,0:T(8,128)} %get-tuple-element.44.refs_3_, ...), custom_call_target="tpu_custom_call" | custom-call | tf_op jit(solution)/shard_map/backward/pallas_call | solution.py:1162
  162.9 0.0 copy-start.1
  162.9 0.0 copy-start.4
  163.1 1.4 concatenate.25
  164.5 1.4 concatenate.26
  166.0 0.0 copy-done
  166.0 0.0 copy-done.5
  166.0 0.0 copy-done.6
  166.0 1.9 %fusion.20 = (bf16[55416]{0:T(1024)(128)(2,1)}, f32[55416]{0:T(1024)}, f32[55416]{0:T(1024)}, f32[55416]{0:T(1024)}) fusion(f32[55416]{0:T(1024)S(1)} %copy-done, f32[55416]{0:T(1024)S(1)} %concatenate.25, f32[55416]{0:T(1024)S(1)} %concatenate.26, f32[56320]{0:T(1024)} %bitcast.6, f32[55416]{0:T(1024)S(1)} %copy-done.5, f32[55416]{0:T(1024)S(1)} %copy-done.6), kind=kLoop, calls=%fused_computation.66 | loop fusion | flops 886656 | bytes 2105808 | tf_op jit(solution)/shard_map/convert_element_type | solution.py:1290
  168.0 0.1 concatenate.23
  168.1 0.1 concatenate.24
  168.2 0.0 copy-done.3
  168.2 0.0 copy-done.7
  168.2 0.0 copy-done.8
  168.3 1.5 fusion.22
  169.8 1.2 slice.15
  171.0 0.0 copy-done.1
  171.0 0.9 copy.29
  171.9 0.0 copy-done.4
  171.9 0.7 copy.30
  (12 shorter events, 0.1 us)
Async XLA Ops:
  2.2 3.2 %copy-start.2 = (s32[128,8]{1,0:T(8,128)}, s32[128,8]{1,0:T(8,128)S(1)}, u32[]{:S(2)}) copy-start(s32[128,8]{1,0:T(8,128)S(1)} %constant_dynamic-update-slice_fusion.refs_1_.refs_25_) | copy-start | bytes 12292
  77.5 88.5 %copy-start = (f32[55416]{0:T(1024)S(1)}, f32[55416]{0:T(1024)}, u32[]{:S(2)}) copy-start(f32[55416]{0:T(1024)} %param.17) | copy-start | bytes 664996
  77.5 88.5 %copy-start.5 = (f32[55416]{0:T(1024)S(1)}, f32[55416]{0:T(1024)}, u32[]{:S(2)}) copy-start(f32[55416]{0:T(1024)} %param.19) | copy-start | bytes 664996
  77.5 88.5 %copy-start.6 = (f32[55416]{0:T(1024)S(1)}, f32[55416]{0:T(1024)}, u32[]{:S(2)}) copy-start(f32[55416]{0:T(1024)} %param.21) | copy-start | bytes 664996
  77.5 90.7 %copy-start.3 = (f32[15432]{0:T(1024)S(1)}, f32[15432]{0:T(1024)}, u32[]{:S(2)}) copy-start(f32[15432]{0:T(1024)} %param.16) | copy-start | bytes 185188
  77.6 90.7 %copy-start.7 = (f32[15432]{0:T(1024)S(1)}, f32[15432]{0:T(1024)}, u32[]{:S(2)}) copy-start(f32[15432]{0:T(1024)} %param.18) | copy-start | bytes 185188
  77.6 90.7 %copy-start.8 = (f32[15432]{0:T(1024)S(1)}, f32[15432]{0:T(1024)}, u32[]{:S(2)}) copy-start(f32[15432]{0:T(1024)} %param.20) | copy-start | bytes 185188
  162.9 8.1 %copy-start.1 = (f32[512,384]{1,0:T(8,128)S(1)}, f32[512,384]{1,0:T(8,128)}, u32[]{:S(2)}) copy-start(f32[512,384]{1,0:T(8,128)} %get-tuple-element.104) | copy-start | bytes 2359300
  162.9 8.9 %copy-start.4 = (f32[3,16384]{1,0:T(4,128)S(1)}, f32[3,16384]{1,0:T(4,128)}, u32[]{:S(2)}) copy-start(f32[3,16384]{1,0:T(4,128)} %get-tuple-element.105) | copy-start | bytes 589828

commit v5 on v4

--- a/solution.py
+++ b/solution.py
@@ -33,7 +33,6 @@
 VMEM_LIMIT = 60 * 2**20
 TILE = 2048
 TOK = TILE // GROUP
-TB = 256
 PAIR = 128
 
 NZ, NY, NX, NC = 4, 2, 2, 2
@@ -93,23 +92,24 @@
 
 
 def shard_rates(layout, devices, own_rank):
-    rate_parts = []
-    decay_parts = []
-    for segment, seg_len in zip(layout, segment_lengths(layout, devices)):
+    lengths = segment_lengths(layout, devices)
+    position = jnp.arange(sum(lengths) // devices, dtype=jnp.int32)
+    rates = jnp.zeros(position.shape, F32)
+    decays = jnp.zeros(position.shape, F32)
+    start = 0
+    for segment, seg_len in zip(layout, lengths):
         piece_len = seg_len // devices
-        position = own_rank * piece_len + jnp.arange(piece_len, dtype=jnp.int32)
-        seg_rates = jnp.zeros((piece_len,), F32)
-        seg_decays = jnp.zeros((piece_len,), F32)
+        here = (position >= start) & (position < start + piece_len)
+        inner = position + (own_rank * piece_len - start)
         offset = 0
         for entry_label, entry_dims, spread in segment:
             extent = math.prod(entry_dims)
-            inside = (position >= offset) & (position < offset + extent)
-            seg_rates = jnp.where(inside, rate_for(spread), seg_rates)
-            seg_decays = jnp.where(inside, decay_for(spread), seg_decays)
+            inside = here & (inner >= offset) & (inner < offset + extent)
+            rates = jnp.where(inside, rate_for(spread), rates)
+            decays = jnp.where(inside, decay_for(spread), decays)
             offset += extent
-        rate_parts.append(seg_rates)
-        decay_parts.append(seg_decays)
-    return (jnp.concatenate(rate_parts), jnp.concatenate(decay_parts))
+        start += piece_len
+    return rates, decays
 
 
 def mm(a, b):
@@ -201,15 +201,20 @@
     pl.semaphore_wait(pltpu.get_barrier_semaphore(), len(peers))
 
 
-def send_to_all(dp, src, dst_of, send, recv):
-    copies = []
-    for k, peer in enumerate(all_peers(dp)):
-        copy = pltpu.make_async_remote_copy(
+def sum_copies(dp, src, dst_of, send, recv):
+    return [
+        pltpu.make_async_remote_copy(
             src_ref=src, dst_ref=dst_of(k), send_sem=send.at[k], recv_sem=recv.at[k],
             device_id=peer, device_id_type=MESH,
         )
+        for k, peer in enumerate(all_peers(dp))
+    ]
+
+
+def send_to_all(dp, src, dst_of, send, recv):
+    copies = sum_copies(dp, src, dst_of, send, recv)
+    for copy in copies:
         copy.start()
-        copies.append(copy)
     return copies
 
 
@@ -387,7 +392,7 @@
     return jnp.concatenate([inverse * gain, shift, mean, inverse, jnp.zeros((4, C3), F32)], axis=0)
 
 
-def second_tile(act, mask, w23, gm, sv_ref, gp_o, pa_o, pg_o, pc_o, first):
+def second_tile(act, mask, w23, gm, count, sv_ref, gp_o, pa_o, pg_o, pc_o, first):
     scale, shift = low(sv_ref[0:1, :] * (1.0 / LAM)), low(sv_ref[1:2, :] * (1.0 / LAM))
     turned = act.T
     c = mm(jnp.concatenate([turned, turned], axis=1), w23).reshape(TOK, GROUP, C3) + gm[:, None, :]
@@ -397,13 +402,16 @@
     gp = gp.reshape(TILE, C3)
     gp_o[...] = gp
     g = g.reshape(TILE, C3)
+    means, gps, gcs = [], [], []
     for q in range(TILE // 256):
-        to = pl.ds(pl.multiple_of(first + 8 * q, 8), 8)
         at = slice(256 * q, 256 * q + 256)
         m = mask[8 * q : 8 * q + 8, at]
-        pa_o[to, :] = mm(m, g[at]) * (0.5 * LAM)
-        pg_o[to, :] = mm(m, gp[at]) * 0.5
-        pc_o[to, :] = mm(m, gc[at]) * 0.5
+        means.append(mm(m, g[at]) * (0.5 * LAM) / count[8 * q : 8 * q + 8, :])
+        gps.append(mm(m, gp[at]) * 0.5)
+        gcs.append(mm(m, gc[at]) * 0.5)
+    to = pl.ds(first, TOK)
+    for ref, parts in ((pa_o, means), (pg_o, gps), (pc_o, gcs)):
+        ref[to, :] = low(jnp.concatenate(parts, axis=0))
 
 
 class Gather:
@@ -456,14 +464,56 @@
 
 
 GATHER_SEMS = 12
-W4_AT, QKV_AT, WO_AT, WF1_AT, WF2_AT, REST_WIDTH = 0, 384, 1536, 1920, 3456, 3840
-UNDER = [("wqkv", QKV_AT, 3 * D), ("wo", WO_AT, D), ("wf1", WF1_AT, FF)]
-
-
-def rest_wf2(d):
-    out = [(48 * d, 16, 0, WF2_AT)]
-    out += [(48 * d + 16 + 4 * j, 4, 12, QKV_AT + D * j) for j in range(8)]
-    return out
+ATT_WIDTH, FFN_WIDTH = 4 * D, 6 * D
+
+
+def attention_rows(bal, pal, stage):
+    start = 1
+    for at, cols in ((0, 3 * D), (3 * D, D)):
+        for j in range(cols // 128):
+            stage[0:12, at + 128 * j : at + 128 * j + 128] = bal[pl.ds(start + j, 12, stride=cols // 128), :]
+        start += 12 * cols // 128
+    for k in range(4):
+        for j in range(D // 128):
+            to = D * k + 128 * j
+            stage[12:16, to : to + 128] = pal[pl.ds(73 + 12 * k + j, 4, stride=3), :]
+
+
+def attention_flat(stage, bal, pal):
+    start = 1
+    for at, cols in ((0, 3 * D), (3 * D, D)):
+        for j in range(cols // 128):
+            bal[pl.ds(start + j, 12, stride=cols // 128), :] = stage[0:12, at + 128 * j : at + 128 * j + 128]
+        start += 12 * cols // 128
+    for k in range(4):
+        for j in range(D // 128):
+            at = D * k + 128 * j
+            pal[pl.ds(73 + 12 * k + j, 4, stride=3), :] = stage[12:16, at : at + 128]
+
+
+FFN_PIECES = [(0, 16, 0, FF), (16, 16, 0, FF + D)] + [(32 + 4 * k, 4, 12, D * k) for k in range(4)]
+FFN_START = 1 + 12 * 4 * D // 128
+
+
+def ffn_rows(bal, stage):
+    for j in range(FF // 128):
+        stage[0:12, 128 * j : 128 * j + 128] = bal[pl.ds(FFN_START + j, 12, stride=FF // 128), :]
+    start = FFN_START + 12 * FF // 128
+    for row, rows, under, at in FFN_PIECES:
+        for j in range(D // 128):
+            to = at + 128 * j
+            stage[under : under + rows, to : to + 128] = bal[pl.ds(start + 3 * row + j, rows, stride=3), :]
+
+
+def ffn_flat(stage, bal):
+    for j in range(FF // 128):
+        bal[pl.ds(FFN_START + j, 12, stride=FF // 128), :] = stage[0:12, 128 * j : 128 * j + 128]
+    start = FFN_START + 12 * FF // 128
+    for row, rows, under, at in FFN_PIECES:
+        for j in range(D // 128):
+            bal[pl.ds(start + 3 * row + j, rows, stride=3), :] = stage[
+                under : under + rows, at + 128 * j : at + 128 * j + 128
+            ]
 
 
 def place(d):
@@ -477,18 +527,19 @@
     rel_o, moment_o, psmall_o, bsmall_o, w2_o, w3_o = take(6)
     w4_o, wqkv_o, wo_o, wf1_o, wf2_o = take(5) if known else [None] * 5
     ext_o, gp1_o, g_o, ps_o, gm_o, fw_o, pooled_o, sv_o, stats_o, wd_o, w23_o, gp_o, pa_o, pg_o, pc_o = take(15)
-    ext_s, e_s, wn_s, w2_s, w23_s, acc3, sums3, ssend3, srecv3 = take(9)
+    ext_s, gm_s, fw_s, e_s, wn_s, w2_s, w23_s, acc3, sums3, ssend3, srecv3 = take(11)
     step = pl.program_id(0)
     tiles = pl.num_programs(0) // 2
     peers = all_peers(dp)
     if known:
         (
-            tiny, rest, three, stage, wide, flat2, pal, bal, counts_s, picked_s,
+            tiny, att, ffn, three, stage, wide, flat2, pal, bal, counts_s, picked_s,
             tsend, trecv, gsend, grecv,
-        ) = take(14)
+        ) = take(15)
         z, y, x, core = where_am_i()
         gather_w3 = Gather(three, gsend, grecv, 0)
-        gather_rest = Gather(rest, gsend, grecv, GATHER_SEMS)
+        gather_att = Gather(att, gsend, grecv, GATHER_SEMS)
+        gather_ffn = Gather(ffn, gsend, grecv, 2 * GATHER_SEMS)
 
     @pl.when(step == 0)
     def _():
@@ -500,19 +551,10 @@
             bal[...] = segments_apart(bflat[...], BSMALL)
             for j in range(C3 // 128):
                 three[z, y, x, core, :, 128 * j : 128 * j + 128] = low(pal[pl.ds(9 + j, 16, stride=C3 // 128), :])
-            for j in range(D // 128):
-                stage[:, 128 * j : 128 * j + 128] = pal[pl.ds(73 + j, 16, stride=D // 128), :]
-            start = 1
-            for name, at, cols in UNDER:
-                for j in range(cols // 128):
-                    stage[0:12, at + 128 * j : at + 128 * j + 128] = bal[pl.ds(start + j, 12, stride=cols // 128), :]
-                start += 12 * cols // 128
-            for row, rows, under, at in rest_wf2(0):
-                for j in range(D // 128):
-                    stage[under : under + rows, at + 128 * j : at + 128 * j + 128] = bal[
-                        pl.ds(start + 3 * row + j, rows, stride=3), :
-                    ]
-            rest[z, y, x, core] = low(stage[...])
+            attention_rows(bal, pal, stage)
+            att[z, y, x, core] = low(stage[:, 0:ATT_WIDTH])
+            ffn_rows(bal, stage)
+            ffn[z, y, x, core] = low(stage[...])
             moments = geometry(points_ref, tokens_ref, rel_o, counts_s, picked_s)[0:4, :]
             moments = jnp.concatenate([moments, jnp.zeros((4, 120), F32)], axis=1)
             hi, mid, lo = [part.astype(F32) for part in split_three(moments)]
@@ -521,10 +563,14 @@
             own = tiny.at[me()]
             own[...] = low(jnp.concatenate(rows, axis=0))
             greeted(peers)
-            for copy in send_to_all(dp, own, lambda k: own, tsend, trecv):
+            copies = send_to_all(dp, own, lambda k: own, tsend, trecv)
+            gather_w3.advance(0)
+            gather_att.advance(0)
+            for copy in copies:
                 copy.wait()
-            gather_w3.advance(0)
-            gather_rest.advance(0)
+            gather_w3.advance(1)
+            gather_att.advance(1)
+            gather_ffn.advance(0)
             psmall, bsmall = [], []
             packed = jnp.zeros((4, 128), F32)
             for d in range(dp * NC):
@@ -552,8 +598,8 @@
 
     if known:
         for at_step, gather, number in (
-            (2, gather_w3, 1), (3, gather_w3, 2), (5, gather_w3, 3), (6, gather_rest, 1), (7, gather_w3, 4),
-            (8, gather_rest, 2), (12, gather_rest, 3),
+            (2, gather_w3, 2), (3, gather_att, 2), (4, gather_w3, 3), (5, gather_ffn, 1), (6, gather_att, 3),
+            (7, gather_w3, 4), (8, gather_ffn, 2), (9, gather_att, 4), (11, gather_ffn, 3),
         ):
             pl.when(step == at_step)(functools.partial(gather.advance, number))
 
@@ -575,7 +621,7 @@
         if known:
             for d in range(dp * NC):
                 w3_o[16 * d : 16 * d + 16, :] = three[place(d)]
-        acc3[...] = first_tokens(g_o[:, 0 : C1 + 16], ps_o, w2_s[...], w3_o, pooled_o, gm_o, fw_o)
+        acc3[...] = first_tokens(g_o[:, 0 : C1 + 16], ps_o, w2_s[...], w3_o, pooled_o, gm_s, fw_s)
         copies = sum_start(dp, acc3, sums3, ssend3, srecv3)
         w23 = mm(w2_s[...], w3_o[C2:, :])
         w23_o[...] = w23
@@ -584,32 +630,44 @@
         w23_s[C1:, :] = low(w23[0:C1] - high.astype(F32))
         sv_o[...] = third_vectors(sum_finish(acc3, sums3, copies), stats_o[2:3, 0:1], psmall_o)
         mean = sv_o[2:3, :]
-        gm = gm_o[...] - mean
-        fw_o[...] = fw_o[...] + ps_o[:, C1 : C1 + 1] * gm
-        gm_o[...] = gm + w23[C1 : C1 + 1, :]
+        gm = gm_s[...] - mean
+        fw_o[...] = low(fw_s[...] + ps_o[:, C1 : C1 + 1] * gm)
+        gm = gm + w23[C1 : C1 + 1, :]
+        gm_s[...] = gm
+        gm_o[...] = low(gm)
 
     @pl.when(step >= tiles)
     def _():
         second_tile(
-            ext_s[:, at], e_s[...] * rel[3:4, :], w23_s[...], gm_o[pl.ds(first, TOK), :], sv_o,
+            ext_s[:, at], e_s[...] * rel[3:4, :], w23_s[...], gm_s[pl.ds(first, TOK), :],
+            ps_o[pl.ds(first, TOK), C1 : C1 + 1], sv_o,
             gp_o, pa_o, pg_o, pc_o, first,
         )
 
     if known:
 
+        @pl.when(step == tiles + 2)
+        def _():
+            for d in range(dp * NC):
+                under = att[place(d)].astype(F32)
+                wide[12 * d : 12 * d + 12, :] = under[0:12, :]
+                tail = [under[12:16, D * k : D * k + D] for k in range(4)]
+                w4_o[16 * d : 16 * d + 16, :] = low(jnp.concatenate(tail, axis=0))
+            wqkv_o[...] = low(wide[:, 0 : 3 * D])
+            wo_o[...] = low(wide[:, 3 * D : 4 * D])
+
         @pl.when(step == 2 * tiles - 1)
         def _():
-            gather_rest.advance(4)
+            gather_ffn.advance(4)
             for d in range(dp * NC):
-                block = rest.at[place(d)]
-                w4_o[16 * d : 16 * d + 16, :] = block[:, W4_AT : W4_AT + D]
-                wf2_o[48 * d : 48 * d + 16, :] = block[:, WF2_AT : WF2_AT + D]
-                under = block[:, QKV_AT:WF2_AT].astype(F32)
+                block = ffn.at[place(d)]
+                under = block[:, 0:FF].astype(F32)
                 wide[12 * d : 12 * d + 12, :] = under[0:12, :]
-                tail = [under[12:16, D * j : D * j + D] for j in range(8)]
-                wf2_o[48 * d + 16 : 48 * d + 48, :] = low(jnp.concatenate(tail, axis=0))
-            for (name, at_col, cols), out in zip(UNDER, (wqkv_o, wo_o, wf1_o)):
-                out[...] = low(wide[:, at_col - QKV_AT : at_col - QKV_AT + cols])
+                wf2_o[48 * d : 48 * d + 16, :] = block[:, FF : FF + D]
+                wf2_o[48 * d + 16 : 48 * d + 32, :] = block[:, FF + D : FF + 2 * D]
+                tail = [under[12:16, D * k : D * k + D] for k in range(4)]
+                wf2_o[48 * d + 32 : 48 * d + 48, :] = low(jnp.concatenate(tail, axis=0))
+            wf1_o[...] = low(wide[...])
 
 
 def forward_call(known, dp, count, *args):
@@ -626,29 +684,31 @@
     outs += [
         (full(*s), s, t)
         for s, t in (
-            ((C1 + 16, 256), F32), ((tokens, 256), F32), ((tokens, C3), F32), ((tokens, C3), F32),
+            ((C1 + 16, 256), F32), ((tokens, 256), F32), ((tokens, C3), BF16), ((tokens, C3), BF16),
             ((tokens, C2), BF16), ((8, C3), F32), ((8, C1), F32), ((8, C1), BF16), ((C1 + 16, C3), F32),
         )
     ]
     outs += [(pl.BlockSpec((TILE, C3), lambda i: (jnp.maximum(i - tiles, 0), 0)), (count, C3), BF16)]
-    outs += [(full(tokens, C3), (tokens, C3), F32)] * 3
+    outs += [(full(tokens, C3), (tokens, C3), BF16)] * 3
     scratch = [
-        pltpu.VMEM((C1, count), BF16), pltpu.VMEM((TOK, TILE), BF16), pltpu.VMEM((8, C1), BF16),
+        pltpu.VMEM((C1, count), BF16), pltpu.VMEM((tokens, C3), F32), pltpu.VMEM((tokens, C3), F32),
+        pltpu.VMEM((TOK, TILE), BF16), pltpu.VMEM((8, C1), BF16),
         pltpu.VMEM((C1 + 16, C2), BF16), pltpu.VMEM((2 * C1, C3), BF16),
     ] + sum_scratch(dp)
     if known:
         n = dp * NC
         scratch += [
             pltpu.VMEM((n, 16, 128), BF16),
-            pltpu.VMEM((NZ, NY, NX, NC, 16, REST_WIDTH), BF16),
+            pltpu.VMEM((NZ, NY, NX, NC, 16, ATT_WIDTH), BF16),
+            pltpu.VMEM((NZ, NY, NX, NC, 16, FFN_WIDTH), BF16),
             pltpu.VMEM((NZ, NY, NX, NC, 16, C3), BF16),
-            pltpu.VMEM((16, REST_WIDTH), F32),
-            pltpu.VMEM((D, WF2_AT - QKV_AT), F32),
+            pltpu.VMEM((16, FFN_WIDTH), F32),
+            pltpu.VMEM((D, FF), F32),
             pltpu.VMEM((8 * n, 128), F32),
             pltpu.VMEM((PROWS, 128), F32), pltpu.VMEM((BROWS, 128), F32),
             pltpu.VMEM((count // 128, 256), F32), pltpu.VMEM((count // 32, 256), F32),
             pltpu.SemaphoreType.DMA((n - 1,)), pltpu.SemaphoreType.DMA((n - 1,)),
-            pltpu.SemaphoreType.DMA((2 * GATHER_SEMS,)), pltpu.SemaphoreType.DMA((2 * GATHER_SEMS,)),
+            pltpu.SemaphoreType.DMA((3 * GATHER_SEMS,)), pltpu.SemaphoreType.DMA((3 * GATHER_SEMS,)),
         ]
     return pl.pallas_call(
         functools.partial(forward_kernel, known, dp),
@@ -683,19 +743,12 @@
     return jnp.sum(v, axis=0, keepdims=True)
 
 
-def block_kernel(
+def block_step(
     pa_ref, pg_ref, pc_ref, cnt_ref, len_ref, cot_ref, psmall_ref, bsmall_ref, sv_ref,
     w4_ref, wqkv_ref, wo_ref, wf1_ref, wf2_ref,
-    out_o, gw4_o, gwqkv_o, gwo_o, gwf1_o, gwf2_o, small_o, tok_o, tg_o, back_o,
-    qkv_s, mixed_s, soft_s, dmix_s, dqkv_s,
+    out_o, small_o, tok_o, tg_o, back_o, qkv_s, mixed_s, soft_s, dmix_s, dqkv_s, dhid_s,
+    ffn_grads, between, token_grads, attention_grads,
 ):
-    step = pl.program_id(0)
-
-    @pl.when(step == 0)
-    def _():
-        for ref in (gw4_o, gwqkv_o, gwo_o, gwf1_o, gwf2_o, small_o, back_o):
-            ref[...] = jnp.zeros_like(ref)
-
     count = cnt_ref[:, C1 : C1 + 1]
     scale = HEAD_DIM ** (-0.5)
     b4 = wide_row(psmall_ref, 15, 3)
@@ -703,7 +756,7 @@
     ln2_gain, ln2_shift = wide_row(bsmall_ref, 9, 3), wide_row(bsmall_ref, 12, 3)
     bf1, bf2 = wide_row(bsmall_ref, 15, 12), wide_row(bsmall_ref, 27, 3)
 
-    act = low(pa_ref[...] / count)
+    act = pa_ref[...]
     x_zero = mm(act, w4_ref[...]) + b4
     unit_a, inv_a, normed_a = layer_norm(x_zero, ln1_gain, ln1_shift)
     qkv_s[...] = low(mm(normed_a, wqkv_ref[...]))
@@ -716,9 +769,9 @@
     def halves(v):
         return jnp.where(left, v, zero), jnp.where(left, zero, v)
 
-    tiles = TB // PAIR
+    tiles = pa_ref.shape[0] // PAIR
     for s in range(tiles):
-        first = (step * tiles + s) * 2
+        first = 2 * s
         visible = (row_cloud == col // PATCHES) & (
             lax.rem(col, PATCHES) < jnp.where(col < PATCHES, len_ref[first], len_ref[first + 1])
         )
@@ -741,19 +794,20 @@
     x_one = x_zero + mm(mixed_low, wo_ref[...]) + bo
     unit_b, inv_b, normed_b = layer_norm(x_one, ln2_gain, ln2_shift)
     hidden, d_hidden = gelu_pair(mm(normed_b, wf1_ref[...]) + bf1)
+    dhid_s[...] = low(d_hidden)
     hidden = low(hidden)
     out_o[...] = x_one + mm(hidden, wf2_ref[...]) + bf2
 
     cot = cot_ref[...]
     grad = low(cot)
-    gwf2_o[...] += mm_tn(hidden, grad)
-    d_pre = mm_nt(grad, wf2_ref[...]) * d_hidden
+    d_pre = mm_nt(grad, wf2_ref[...]) * dhid_s[...].astype(F32)
     d_pre_low = low(d_pre)
-    gwf1_o[...] += mm_tn(normed_b, d_pre_low)
+    small_o[7:8, :] = col_sum(d_pre)
+    ffn_grads(mm_tn(normed_b, d_pre_low), mm_tn(hidden, grad))
     d_normed_b = mm_nt(d_pre_low, wf1_ref[...])
     d_x_one = cot + norm_back(d_normed_b * ln2_gain, unit_b, inv_b)
     d_x_low = low(d_x_one)
-    gwo_o[...] += mm_tn(mixed_low, d_x_low)
+    d_x_one_low = d_x_low
     dmix_s[...] = low(mm_nt(d_x_low, wo_ref[...]))
 
     for s in range(tiles):
@@ -776,25 +830,24 @@
             dqkv_s[rows, D + at : D + at + 128] = low(jnp.where(left, d_k[0], d_k[1]) * scale)
             dqkv_s[rows, 2 * D + at : 2 * D + at + 128] = low(jnp.where(left, d_v[0], d_v[1]))
 
+    between()
     d_qkv = dqkv_s[...]
-    gwqkv_o[...] += mm_tn(normed_a, d_qkv)
     d_normed_a = mm_nt(d_qkv, wqkv_ref[...])
     d_x_zero = d_x_one + norm_back(d_normed_a * ln1_gain, unit_a, inv_a)
     d_x_low = low(d_x_zero)
-    gw4_o[...] += mm_tn(act, d_x_low)
     token = mm_nt(d_x_low, w4_ref[...]) / count
     tok_o[...] = token
-    grouped = token * pg_ref[...]
+    grouped = token * pg_ref[...].astype(F32)
     tg_o[...] = grouped
-    back_o[0:1, :] += col_sum(grouped)
-    back_o[1:2, :] += col_sum(token * pc_ref[...]) * sv_ref[3:4, :]
+    back_o[...] = as_rows(col_sum(grouped), col_sum(token * pc_ref[...].astype(F32)) * sv_ref[3:4, :])
+    token_grads()
     narrow = [
         col_sum(d_normed_a * unit_a), col_sum(d_normed_a), col_sum(d_x_one),
         col_sum(d_normed_b * unit_b), col_sum(d_normed_b), col_sum(cot), col_sum(d_x_zero),
     ]
     for k, row in enumerate(narrow):
-        small_o[k : k + 1, 0:D] += row
-    small_o[7:8, :] += col_sum(d_pre)
+        small_o[k : k + 1, 0:D] = row
+    attention_grads(mm_tn(normed_a, d_qkv), mm_tn(mixed_low, d_x_one_low), mm_tn(act, d_x_low))
 
 
 def third_back_tokens(
@@ -808,9 +861,9 @@
     count = ps_ref[:, C1 : C1 + 1]
     w23 = w23_ref[...]
     act = low(w23[0:C1])
-    per_token = low(gain * tg_ref[...] - (count * alpha + beta * sc_ref[...]))
+    per_token = low(gain * tg_ref[...] - (count * alpha + beta * sc_ref[...].astype(F32)))
     pooled = low(mm_nt(per_token, w3_ref[0:C2, :]) / count)
-    shifted = low(alpha + beta * gm_ref[...])
+    shifted = low(alpha + beta * gm_ref[...].astype(F32))
     kap_o[...] = low(mm_nt(pooled, w2_ref[...]) - mm_nt(shifted, act))
     k_o[:, 0:C1] = low(-mm_nt(low(w23[0:C1] * beta), act))
     wb_o[...] = low(w23[0:C1] * gain)
@@ -982,72 +1035,88 @@
     out_o, pg_o = take(2)
     if known:
         pflat_o, bflat_o = take(2)
-        gw4_s, gwqkv_s, gwo_s, gwf1_s, gwf2_s = None, None, None, None, None
     else:
-        prow_o, brow_o, gw2_o, gw3_o = take(4)
-        gw4_s, gwqkv_s, gwo_s, gwf1_s, gwf2_s = take(5)
-    small_s, tok_s, tg_s, back_s, qkv_s, mixed_s, soft_s, dmix_s, dqkv_s = take(9)
+        prow_o, brow_o, gw2_o, gw3_o, gw4_o, gwqkv_o, gwo_o, gwf1_o, gwf2_o = take(9)
+    small_s, tok_s, tg_s, acc3, qkv_s, mixed_s, soft_s, dmix_s, dqkv_s, dhid_s = take(10)
     tot_s, kap_s, k_s, wb_s, top_s, corr_s, base_s, h_s, q_s, d_s, xe_s, spread_s, sums_s = take(13)
-    acc, slots, ssend, srecv, acc3, slots3, ssend3, srecv3 = take(8)
+    acc, slots, ssend, srecv, unused, slots3, ssend3, srecv3 = take(8)
     step = pl.program_id(0)
     steps = pl.num_programs(0)
     peers = all_peers(dp)
     if known:
-        gw4_s, gwqkv_s, gwo_s, gwf1_s, gwf2_s = take(5)
-        rest0, rest1, rest2, rest3, rest4, point0, point1, point2, point3, point4 = take(10)
-        stage, pstage, pal, bal, gsend, grecv = take(6)
+        ffn0, ffn1, ffn2, ffn3, ffn4, att0, att1, att2, att3, att4, point0, point1, point2, point3, point4 = take(15)
+        wide, tall, stage, pstage, pal, bal, gsend, grecv = take(8)
         z, y, x, core = where_am_i()
-        rest = Scatter(rest0, (rest1, rest2, rest3, rest4), gsend, grecv, 0)
-        point = Scatter(point0, (point1, point2, point3, point4), gsend, grecv, SCATTER_SEMS)
-    blocks = ps_ref.shape[0] // TB
+        ffn = Scatter(ffn0, (ffn1, ffn2, ffn3, ffn4), gsend, grecv, 0)
+        att = Scatter(att0, (att1, att2, att3, att4), gsend, grecv, SCATTER_SEMS)
+        point = Scatter(point0, (point1, point2, point3, point4), gsend, grecv, 2 * SCATTER_SEMS)
+
+    def ffn_grads(gwf1, gwf2):
+        if not known:
+            gwf1_o[...], gwf2_o[...] = gwf1, gwf2
+            return
+        wide[...] = gwf1
+        tall[...] = gwf2
+        for d in range(dp * NC):
+            stage[0:12, 0:FF] = wide[12 * d : 12 * d + 12, :]
+            for row, rows, under, at in FFN_PIECES:
+                stage[under : under + rows, at : at + D] = tall[48 * d + row : 48 * d + row + rows, :]
+            cz, cy, cx, cc = place(d)
+            ffn0[cc, cz, cy, cx] = low(stage[...])
+        greeted(peers)
+        ffn.advance(0)
+
+    def between():
+        if known:
+            ffn.advance(1)
+
+    def token_grads():
+        if not known:
+            greeted(peers)
+        sum_start(dp, acc3, slots3, ssend3, srecv3)
+
+    def attention_grads(gwqkv, gwo, gw4):
+        if not known:
+            gwqkv_o[...], gwo_o[...], gw4_o[...] = gwqkv, gwo, gw4
+            return
+        wide[:, 0 : 3 * D] = gwqkv
+        wide[:, 3 * D :] = gwo
+        tall[0:C3, :] = gw4
+        for d in range(dp * NC):
+            stage[0:12, 0:ATT_WIDTH] = wide[12 * d : 12 * d + 12, :]
+            for k in range(4):
+                stage[12:16, D * k : D * k + D] = tall[16 * d + 4 * k : 16 * d + 4 * k + 4, :]
+            cz, cy, cx, cc = place(d)
+            att0[cc, cz, cy, cx] = low(stage[:, 0:ATT_WIDTH])
+        att.advance(0)
+        ffn.advance(2)
+        att.advance(1)
 
     @pl.when(step == 0)
     def _():
         greet(peers)
-
-    @pl.when(step < blocks)
-    def _():
-        rows = pl.ds(pl.multiple_of(step * TB, TB), TB)
-        block_kernel(
-            pa_ref, pg_ref, pc_ref, ps_ref.at[rows], len_ref, cot_ref, psmall_ref, bsmall_ref, sv_ref,
+        block_step(
+            pa_ref, pg_ref, pc_ref, ps_ref, len_ref, cot_ref, psmall_ref, bsmall_ref, sv_ref,
             w4_ref, wqkv_ref, wo_ref, wf1_ref, wf2_ref,
-            out_o, gw4_s, gwqkv_s, gwo_s, gwf1_s, gwf2_s, small_s, tok_s.at[rows], tg_s.at[rows], back_s,
-            qkv_s, mixed_s, soft_s, dmix_s, dqkv_s,
+            out_o, small_s, tok_s, tg_s, acc3, qkv_s, mixed_s, soft_s, dmix_s, dqkv_s, dhid_s,
+            ffn_grads, between, token_grads, attention_grads,
         )
-
-    @pl.when(step == blocks - 1)
-    def _():
-        greeted(peers)
-        acc3[...] = as_rows(back_s[0:1, :], back_s[1:2, :])
-        copies = sum_start(dp, acc3, slots3, ssend3, srecv3)
-        if known:
-            for d in range(dp * NC):
-                stage[:, W4_AT : W4_AT + D] = gw4_s[16 * d : 16 * d + 16, :]
-                for (name, at, cols), ref in zip(UNDER, (gwqkv_s, gwo_s, gwf1_s)):
-                    stage[0:12, at : at + cols] = ref[12 * d : 12 * d + 12, :]
-                for row, rows, under, at in rest_wf2(d):
-                    stage[under : under + rows, at : at + D] = gwf2_s[row : row + rows, :]
-                cz, cy, cx, cc = place(d)
-                rest0[cc, cz, cy, cx] = low(stage[...])
-            rest.advance(0)
         for ref in (h_s, q_s):
             ref[...] = jnp.zeros_like(ref)
         xe_s[C1:, :] = token_ones()
-        if known:
-            rest.advance(1)
-        tot_s[...] = sum_finish(acc3, slots3, copies)
+        tot_s[...] = sum_finish(acc3, slots3, sum_copies(dp, acc3, lambda k: slots3.at[k], ssend3, srecv3))
         third_back_tokens(
             tot_s[...], tg_s, sc_ref, gm_ref, ps_ref, pooled_ref, gext_ref, w2_ref, w3_ref, w23_ref, sv_ref, stats_ref,
             kap_s, k_s, wb_s, top_s, corr_s, base_s,
         )
 
     if known:
-        for at_step, number in ((5, 2), (7, 3)):
-            pl.when(step == at_step)(functools.partial(rest.advance, number))
-
-    @pl.when(step >= blocks)
+        for at_step, group, number in ((3, ffn, 3), (4, att, 2), (6, att, 3)):
+            pl.when(step == at_step)(functools.partial(group.advance, number))
+
+    @pl.when(step >= 1)
     def _():
-        tile = step - blocks
+        tile = step - 1
         at = pl.ds(pl.multiple_of(tile * TILE, TILE), TILE)
         ts = pl.ds(pl.multiple_of(tile * TOK, TOK), TOK)
 
@@ -1088,7 +1157,10 @@
         full_rows = point_small_rows(grad_w, gain1, shift1, jnp.zeros((1, C2), F32), tot_s[...], jnp.zeros((1, D), F32))
         if known:
             point.advance(2)
-            stage[...] = rest.advance(4)
+            stage[...] = ffn.advance(4)
+            ffn_flat(stage, bal)
+            stage[:, 0:ATT_WIDTH] = att.advance(4)
+            attention_flat(stage, bal, pal)
             point.advance(3)
         point_gradient(d_s, rel_ref, tokens_ref, flat, slope, pg_o, spread_s, sums_s)
         if not known:
@@ -1101,18 +1173,6 @@
         own = jnp.zeros((1, 128), F32)
         for d in range(dp * NC):
             own = own + jnp.where(me() == d, piece_of(full_rows, PSMALL * d, PSMALL), 0.0)
-        for j in range(D // 128):
-            pal[pl.ds(73 + j, 16, stride=3), :] = stage[:, 128 * j : 128 * j + 128]
-        start = 1
-        for name, at, cols in UNDER:
-            for j in range(cols // 128):
-                bal[pl.ds(start + j, 12, stride=cols // 128), :] = stage[0:12, at + 128 * j : at + 128 * j + 128]
-            start += 12 * cols // 128
-        for row, rows, under, at in rest_wf2(0):
-            for j in range(D // 128):
-                bal[pl.ds(start + 3 * row + j, rows, stride=3), :] = stage[
-                    under : under + rows, at + 128 * j : at + 128 * j + 128
-                ]
         pstage[...] = point.advance(4)
         for j in range(C2 // 128):
             pal[pl.ds(1 + j, 4, stride=2), :] = pstage[0:4, C3 + 128 * j : C3 + 128 * j + 128]
@@ -1124,26 +1184,25 @@
 
 def backward_call(known, dp, *args):
     count = args[24].shape[1]
-    tokens, blocks, tiles = count // GROUP, count // GROUP // TB, count // TILE
+    tokens, tiles = count // GROUP, count // TILE
     single = dict(pipeline_mode=pl.Buffered(1))
     full = lambda *s: pl.BlockSpec(s, lambda i: (0, 0), **single)
-    chunk = lambda c: pl.BlockSpec((TB, c), lambda i: (jnp.minimum(i, blocks - 1), 0))
-    cols = lambda r: pl.BlockSpec((r, TILE), lambda i: (0, jnp.maximum(i - blocks, 0)))
-    specs = [chunk(C3), chunk(C3), chunk(C3), full(tokens, 256), pl.BlockSpec(memory_space=pltpu.SMEM), chunk(D)]
-    specs += [full(*a.shape) for a in args[6:26]]
-    specs += [pl.BlockSpec((TILE, C3), lambda i: (jnp.maximum(i - blocks, 0), 0)), cols(C1 + 16), cols(C1)]
-    grads = [((C3, D), F32), ((D, 3 * D), F32), ((D, D), F32), ((D, FF), F32), ((FF, D), F32)]
-    outs = [(chunk(D), (tokens, D), F32), (full(3, count), (3, count), F32)]
+    cols = lambda r: pl.BlockSpec((r, TILE), lambda i: (0, jnp.maximum(i - 1, 0)))
+    specs = [full(*a.shape) for a in args[:26]]
+    specs[4] = pl.BlockSpec(memory_space=pltpu.SMEM)
+    specs += [pl.BlockSpec((TILE, C3), lambda i: (jnp.maximum(i - 1, 0), 0)), cols(C1 + 16), cols(C1)]
+    outs = [((tokens, D), F32), ((3, count), F32)]
     if known:
-        outs += [(full(*s), s, t) for s, t in (((PROWS, 128), F32), ((BROWS, 128), F32))]
+        outs += [((PROWS, 128), F32), ((BROWS, 128), F32)]
     else:
-        more = [((24, 128), F32), ((32, 128), F32), ((C1, C2), F32), ((2 * C2, C3), F32)] + grads
-        outs += [(full(*s), s, t) for s, t in more]
+        outs += [((24, 128), F32), ((32, 128), F32), ((C1, C2), F32), ((2 * C2, C3), F32), ((C3, D), F32)]
+        outs += [((D, 3 * D), F32), ((D, D), F32), ((D, FF), F32), ((FF, D), F32)]
     pieces = count // 256
     scratch = [
-        pltpu.VMEM((8, FF), F32), pltpu.VMEM((tokens, C3), F32), pltpu.VMEM((tokens, C3), F32), pltpu.VMEM((8, C3), F32),
-        pltpu.VMEM((TB, 3 * D), BF16), pltpu.VMEM((TB, D), BF16),
-        pltpu.VMEM((TB // PAIR * HEADS, PAIR, PAIR), F32), pltpu.VMEM((TB, D), BF16), pltpu.VMEM((TB, 3 * D), BF16),
+        pltpu.VMEM((8, FF), F32), pltpu.VMEM((tokens, C3), F32), pltpu.VMEM((tokens, C3), F32), pltpu.VMEM((8, 128), F32),
+        pltpu.VMEM((tokens, 3 * D), BF16), pltpu.VMEM((tokens, D), BF16),
+        pltpu.VMEM((tokens // PAIR * HEADS, PAIR, PAIR), F32), pltpu.VMEM((tokens, D), BF16),
+        pltpu.VMEM((tokens, 3 * D), BF16), pltpu.VMEM((tokens, FF), BF16),
         pltpu.VMEM((8, 128), F32), pltpu.VMEM((tokens, C1), BF16), pltpu.VMEM((C1, C1 + TOK), BF16),
         pltpu.VMEM((C1, C3), BF16), pltpu.VMEM((C2, C3), F32), pltpu.VMEM((C1 + 16, C3), F32),
         pltpu.VMEM((C1 + 16, C2), F32), pltpu.VMEM((C1 + 16, C3), F32), pltpu.VMEM((8, C1), F32),
@@ -1152,19 +1211,19 @@
     ]
     scratch += sum_scratch(dp) + sum_scratch(dp)
     if known:
-        scratch += [pltpu.VMEM(s, t) for s, t in grads]
-        scratch += scatter_scratch(REST_WIDTH) + scatter_scratch(POINT_WIDTH)
+        scratch += scatter_scratch(FFN_WIDTH) + scatter_scratch(ATT_WIDTH) + scatter_scratch(POINT_WIDTH)
         scratch += [
-            pltpu.VMEM((16, REST_WIDTH), F32), pltpu.VMEM((16, POINT_WIDTH), F32),
+            pltpu.VMEM((D, FF), F32), pltpu.VMEM((FF, D), F32),
+            pltpu.VMEM((16, FFN_WIDTH), F32), pltpu.VMEM((16, POINT_WIDTH), F32),
             pltpu.VMEM((PROWS, 128), F32), pltpu.VMEM((BROWS, 128), F32),
-            pltpu.SemaphoreType.DMA((2 * SCATTER_SEMS,)), pltpu.SemaphoreType.DMA((2 * SCATTER_SEMS,)),
+            pltpu.SemaphoreType.DMA((3 * SCATTER_SEMS,)), pltpu.SemaphoreType.DMA((3 * SCATTER_SEMS,)),
         ]
     return pl.pallas_call(
         functools.partial(backward_kernel, known, dp),
-        grid=(blocks + tiles,),
+        grid=(1 + tiles,),
         in_specs=specs,
-        out_specs=[o[0] for o in outs],
-        out_shape=shaped(*[o[1:] for o in outs]),
+        out_specs=[full(*s) for s, t in outs],
+        out_shape=shaped(*outs),
         scratch_shapes=scratch,
         compiler_params=params(collective_id=1, has_side_effects=True),
         name="backward",

time: 173 us -> 157 us (0.908)
  Pallas kernels: 157 us -> 142 us
    pallas_call x1, Pallas kernels: 85.3 us -> 73.7 us  [backward_call(): pl.pallas_call(functools.partial(backward_kernel, known, dp), grid=(1 + t...]
    pallas_call x1, Pallas kernels: 72.1 us -> 68.7 us  [forward_call(): pl.pallas_call(functools.partial(forward_kernel, known, dp), grid=(2 * ti...]
    concatenate x4 -> x0, local copies, waits for them, and re-layouts: 3.08 us -> none  [shard_rates(): return (jnp.concatenate(rate_parts), jnp.concatenate(decay_parts))]
    unnamed x21 -> x17, local copies, waits for them, and re-layouts: 1.64 us -> 3.81 us
where the time goes in v5:
time: 157 us; the launch traced here: 156 us
  Pallas kernels  142 us (90%)
  local copies, waits for them, and re-layouts  9.66 us (6%)
  other arithmetic  3.6 us (2%)
    pallas_call x1, Pallas kernels, backward_call(): pl.pallas_call(functools.partial(backward_kernel, known, dp), grid=(1 + t...  73.7 us
    pallas_call x1, Pallas kernels, forward_call(): pl.pallas_call(functools.partial(forward_kernel, known, dp), grid=(2 * ti...  68.7 us
    unnamed x17, local copies, waits for them, and re-layouts  3.81 us

profile of v5, /device:TPU:0, one launch (start us, length us, event | category | flops | bytes accessed | tf_op | source)
XLA Modules:
  0.0 156.5 jit_solution(7648401777098851768)
XLA Ops:
  0.6 0.8 concatenate.8
  1.4 0.8 concatenate.9
  2.2 0.0 copy-start.1
  2.2 1.7 %pad_bitcast_fusion.refs_3_ = f32[440,128]{1,0:T(8,128)} fusion(f32[55416]{0:T(1024)} %param.17), kind=kLoop, calls=%fused_computation.47 | loop fusion | bytes 446944 | tf_op jit(solution)/shard_map/reshape | solution.py:1302
  3.9 1.5 pad_bitcast_fusion.1.refs_2_
  5.4 0.0 copy-done.1
  5.4 68.7 %forward.1 = (bf16[8,16384]{1,0:T(8,128)(2,1)}, f32[8,128]{1,0:T(8,128)}, f32[24,128]{1,0:T(8,128)}, f32[32,128]{1,0:T(8,128)}, bf16[128,256]{1,0:T(8,128)(2,1)}...) custom-call(f32[3,16384]{1,0:T(4,128)} %refs_0_.1, ...), custom_call_target="tpu_custom_call" | custom-call | tf_op jit(solution)/shard_map/forward/pallas_call | solution.py:713
  74.1 0.0 copy-start
  74.1 0.0 copy-start.3
  74.1 0.0 copy-start.4
  74.1 0.0 copy-start.2
  74.1 0.0 copy-start.5
  74.1 0.0 copy-start.6
  74.1 73.7 %backward.1 = (f32[512,384]{1,0:T(8,128)}, f32[3,16384]{1,0:T(4,128)}, f32[128,128]{1,0:T(8,128)}, f32[440,128]{1,0:T(8,128)}) custom-call(bf16[512,512]{1,0:T(8,128)(2,1)} %get-tuple-element.41.refs_0_, bf16[512,512]{1,0:T(8,128)(2,1)} %get-tuple-element.42.refs_1_, bf16[512,512]{1,0:T(8,128)(2,1)} %get-tuple-element.43.refs_2_, ...), custom_call_target="tpu_custom_call" | custom-call | tf_op jit(solution)/shard_map/backward/pallas_call | solution.py:1221
  147.9 0.0 copy-done
  147.9 0.0 copy-done.3
  147.9 0.0 copy-done.4
  147.9 2.0 %fusion.93 = (bf16[55416]{0:T(1024)(128)(2,1)}, f32[55416]{0:T(1024)}, f32[55416]{0:T(1024)}, f32[55416]{0:T(1024)}) fusion(f32[55416]{0:T(1024)S(1)} %copy-done, s32[]{:T(128)S(6)} %mul.113, s32[]{:T(128)S(6)} %sub.34, s32[]{:T(128)S(6)} %sub.33, s32[]{:T(128)S(6)} %sub.32, s32[]{:T(128)S(6)} %sub.31, f32[56320]{0:T(1024)} %bitcast.6, ...), kind=kLoop, calls=%fused_computation.128 | loop fusion | flops 5153688 | bytes 1662500 | tf_op jit(solution)/shard_map/convert_element_type | solution.py:1349
  149.9 0.0 copy-done.2
  149.9 0.0 copy-done.5
  149.9 0.0 copy-done.6
  149.9 1.6 %fusion.95 = (bf16[15432]{0:T(1024)(128)(2,1)}, f32[15432]{0:T(1024)}, f32[15432]{0:T(1024)}, f32[15432]{0:T(1024)}) fusion(f32[15432]{0:T(1024)S(1)} %copy-done.2, s32[]{:T(128)S(6)} %mul.98, s32[]{:T(128)S(6)} %sub.29, s32[]{:T(128)S(6)} %sub.28, s32[]{:T(128)S(6)} %sub.27, f32[16384]{0:T(1024)} %bitcast.8, f32[15432]{0:T(1024)S(1)} %copy-done.5, ...), kind=kLoop, calls=%fused_computation.129 | loop fusion | flops 1388880 | bytes 462976 | tf_op jit(solution)/shard_map/convert_element_type | solution.py:1349
  151.5 1.2 slice.15
  152.7 2.1 %copy.29 = f32[512,384]{1,0:T(8,128)} copy(f32[512,384]{1,0:T(8,128)} %get-tuple-element.90) | data formatting | bytes 1572864
  154.8 1.7 %copy.30 = f32[3,16384]{1,0:T(4,128)} copy(f32[3,16384]{1,0:T(4,128)} %get-tuple-element.91) | data formatting | bytes 393216
  (2 shorter events, 0.0 us)
Async XLA Ops:
  2.2 3.2 %copy-start.1 = (s32[128,8]{1,0:T(8,128)}, s32[128,8]{1,0:T(8,128)S(1)}, u32[]{:S(2)}) copy-start(s32[128,8]{1,0:T(8,128)S(1)} %constant_dynamic-update-slice_fusion.refs_1_.refs_25_) | copy-start | bytes 12292
  74.1 73.8 %copy-start = (f32[55416]{0:T(1024)S(1)}, f32[55416]{0:T(1024)}, u32[]{:S(2)}) copy-start(f32[55416]{0:T(1024)} %param.17) | copy-start | bytes 664996
  74.1 73.8 %copy-start.3 = (f32[55416]{0:T(1024)S(1)}, f32[55416]{0:T(1024)}, u32[]{:S(2)}) copy-start(f32[55416]{0:T(1024)} %param.19) | copy-start | bytes 664996
  74.1 73.8 %copy-start.4 = (f32[55416]{0:T(1024)S(1)}, f32[55416]{0:T(1024)}, u32[]{:S(2)}) copy-start(f32[55416]{0:T(1024)} %param.21) | copy-start | bytes 664996
  74.1 75.8 %copy-start.2 = (f32[15432]{0:T(1024)S(1)}, f32[15432]{0:T(1024)}, u32[]{:S(2)}) copy-start(f32[15432]{0:T(1024)} %param.16) | copy-start | bytes 185188
  74.1 75.8 %copy-start.5 = (f32[15432]{0:T(1024)S(1)}, f32[15432]{0:T(1024)}, u32[]{:S(2)}) copy-start(f32[15432]{0:T(1024)} %param.18) | copy-start | bytes 185188
  74.1 75.8 %copy-start.6 = (f32[15432]{0:T(1024)S(1)}, f32[15432]{0:T(1024)}, u32[]{:S(2)}) copy-start(f32[15432]{0:T(1024)} %param.20) | copy-start | bytes 185188

commit v6 on v5

--- a/solution.py
+++ b/solution.py
@@ -33,7 +33,10 @@
 VMEM_LIMIT = 60 * 2**20
 TILE = 2048
 TOK = TILE // GROUP
-PAIR = 128
+STEP_TILES = 2
+AHEAD = 4
+WIDE = TILE * STEP_TILES
+PAIR = 256
 
 NZ, NY, NX, NC = 4, 2, 2, 2
 PROWS, BROWS = 128, 440
@@ -154,8 +157,8 @@
 
 
 def gelu_pair(v):
-    g, d = gelu_twice(v * (1.0 / LAM))
-    return (0.5 * LAM) * g, 0.5 * d
+    g, d = gelu_twice(low(v * (1.0 / LAM)))
+    return low(g.astype(F32) * (0.5 * LAM)), d * 0.5
 
 
 def patch_ones():
@@ -358,14 +361,15 @@
     return jnp.where((lane < small) & (row == 0), first, joined)
 
 
-def first_tile(rel, wn, ext_ref, gp_ref):
+def first_tile(rel, wn, ext_ref, gp_ref, start):
     valid = rel[3:4, :].astype(F32)
     for j in range(TILE // 256):
         at = slice(256 * j, 256 * j + 256)
+        to = slice(start + 256 * j, start + 256 * j + 256)
         g, d = gelu_twice(mm_tn(wn, rel[:, at]))
-        ext_ref[0:C1, at] = low(g * (valid[:, at] * (0.5 * LAM)))
-        gp_ref[:, at] = low(d * (valid[:, at] * 0.5))
-    ext_ref[C1:, :] = jnp.concatenate([rel[3:4], jnp.zeros((15, TILE), BF16)], axis=0)
+        ext_ref[0:C1, to] = low(g * (valid[:, at] * (0.5 * LAM)))
+        gp_ref[:, to] = low(d * (valid[:, at] * 0.5))
+    ext_ref[C1:, start : start + TILE] = jnp.concatenate([rel[3:4], jnp.zeros((15, TILE), BF16)], axis=0)
 
 
 def first_tokens(gext, ps_ref, w2e, w3_ref, pooled_o, gm_o, fw_o):
@@ -392,7 +396,7 @@
     return jnp.concatenate([inverse * gain, shift, mean, inverse, jnp.zeros((4, C3), F32)], axis=0)
 
 
-def second_tile(act, mask, w23, gm, count, sv_ref, gp_o, pa_o, pg_o, pc_o, first):
+def second_tile(act, mask, w23, gm, count, sv_ref, gp_o, start, pa_o, pg_o, pc_o, first):
     scale, shift = low(sv_ref[0:1, :] * (1.0 / LAM)), low(sv_ref[1:2, :] * (1.0 / LAM))
     turned = act.T
     c = mm(jnp.concatenate([turned, turned], axis=1), w23).reshape(TOK, GROUP, C3) + gm[:, None, :]
@@ -400,7 +404,7 @@
     g, gp = gelu_twice(c * scale[None] + shift[None])
     gc = (gp * c).reshape(TILE, C3)
     gp = gp.reshape(TILE, C3)
-    gp_o[...] = gp
+    gp_o[start : start + TILE, :] = gp
     g = g.reshape(TILE, C3)
     means, gps, gcs = [], [], []
     for q in range(TILE // 256):
@@ -409,9 +413,8 @@
         means.append(mm(m, g[at]) * (0.5 * LAM) / count[8 * q : 8 * q + 8, :])
         gps.append(mm(m, gp[at]) * 0.5)
         gcs.append(mm(m, gc[at]) * 0.5)
-    to = pl.ds(first, TOK)
     for ref, parts in ((pa_o, means), (pg_o, gps), (pc_o, gcs)):
-        ref[to, :] = low(jnp.concatenate(parts, axis=0))
+        ref[first, :] = low(jnp.concatenate(parts, axis=0))
 
 
 class Gather:
@@ -549,12 +552,6 @@
         if known:
             pal[...] = segments_apart(pflat[...], PSMALL)
             bal[...] = segments_apart(bflat[...], BSMALL)
-            for j in range(C3 // 128):
-                three[z, y, x, core, :, 128 * j : 128 * j + 128] = low(pal[pl.ds(9 + j, 16, stride=C3 // 128), :])
-            attention_rows(bal, pal, stage)
-            att[z, y, x, core] = low(stage[:, 0:ATT_WIDTH])
-            ffn_rows(bal, stage)
-            ffn[z, y, x, core] = low(stage[...])
             moments = geometry(points_ref, tokens_ref, rel_o, counts_s, picked_s)[0:4, :]
             moments = jnp.concatenate([moments, jnp.zeros((4, 120), F32)], axis=1)
             hi, mid, lo = [part.astype(F32) for part in split_three(moments)]
@@ -564,8 +561,14 @@
             own[...] = low(jnp.concatenate(rows, axis=0))
             greeted(peers)
             copies = send_to_all(dp, own, lambda k: own, tsend, trecv)
+            for j in range(C3 // 128):
+                three[z, y, x, core, :, 128 * j : 128 * j + 128] = low(pal[pl.ds(9 + j, 16, stride=C3 // 128), :])
             gather_w3.advance(0)
+            attention_rows(bal, pal, stage)
+            att[z, y, x, core] = low(stage[:, 0:ATT_WIDTH])
             gather_att.advance(0)
+            ffn_rows(bal, stage)
+            ffn[z, y, x, core] = low(stage[...])
             for copy in copies:
                 copy.wait()
             gather_w3.advance(1)
@@ -598,23 +601,25 @@
 
     if known:
         for at_step, gather, number in (
-            (2, gather_w3, 2), (3, gather_att, 2), (4, gather_w3, 3), (5, gather_ffn, 1), (6, gather_att, 3),
-            (7, gather_w3, 4), (8, gather_ffn, 2), (9, gather_att, 4), (11, gather_ffn, 3),
+            (1, gather_w3, 2), (1, gather_att, 2), (2, gather_w3, 3), (2, gather_ffn, 1), (3, gather_att, 3),
+            (4, gather_w3, 4), (4, gather_ffn, 2), (5, gather_att, 4), (5, gather_ffn, 3),
         ):
             pl.when(step == at_step)(functools.partial(gather.advance, number))
 
-    at = pl.ds(pl.multiple_of(lax.rem(step, tiles) * TILE, TILE), TILE)
-    rel = rel_o[:, at]
-    first = pl.multiple_of(lax.rem(step, tiles) * TOK, TOK)
+    def tile_at(half):
+        tile = lax.rem(step, tiles) * STEP_TILES + half
+        return pl.ds(pl.multiple_of(tile * TILE, TILE), TILE), pl.ds(pl.multiple_of(tile * TOK, TOK), TOK)
 
     @pl.when(step < tiles)
     def _():
-        first_tile(rel, wn_s[...], ext_o, gp1_o)
-        ext = ext_o[...]
-        ext_s[:, at] = ext[0:C1]
-        both = mm_nt(jnp.concatenate([ext, e_s[...]], axis=0), ext)
-        g_o[:, 0 : C1 + 16] += both[0 : C1 + 16]
-        ps_o[pl.ds(first, TOK), 0 : C1 + 16] = both[C1 + 16 :]
+        for half in range(STEP_TILES):
+            at, ts = tile_at(half)
+            first_tile(rel_o[:, at], wn_s[...], ext_o, gp1_o, half * TILE)
+            ext = ext_o[:, half * TILE : half * TILE + TILE]
+            ext_s[:, at] = ext[0:C1]
+            both = mm_nt(jnp.concatenate([ext, e_s[...]], axis=0), ext)
+            g_o[:, 0 : C1 + 16] += both[0 : C1 + 16]
+            ps_o[ts, 0 : C1 + 16] = both[C1 + 16 :]
 
     @pl.when(step == tiles)
     def _():
@@ -638,15 +643,16 @@
 
     @pl.when(step >= tiles)
     def _():
-        second_tile(
-            ext_s[:, at], e_s[...] * rel[3:4, :], w23_s[...], gm_s[pl.ds(first, TOK), :],
-            ps_o[pl.ds(first, TOK), C1 : C1 + 1], sv_o,
-            gp_o, pa_o, pg_o, pc_o, first,
-        )
+        for half in range(STEP_TILES):
+            at, ts = tile_at(half)
+            second_tile(
+                ext_s[:, at], e_s[...] * rel_o[3:4, at], w23_s[...], gm_s[ts, :], ps_o[ts, C1 : C1 + 1], sv_o,
+                gp_o, half * TILE, pa_o, pg_o, pc_o, ts,
+            )
 
     if known:
 
-        @pl.when(step == tiles + 2)
+        @pl.when(step == tiles + 1)
         def _():
             for d in range(dp * NC):
                 under = att[place(d)].astype(F32)
@@ -671,10 +677,10 @@
 
 
 def forward_call(known, dp, count, *args):
-    tokens, tiles = count // GROUP, count // TILE
+    tokens, tiles = count // GROUP, count // WIDE
     single = dict(pipeline_mode=pl.Buffered(1))
     full = lambda *s: pl.BlockSpec(s, lambda i: (0, 0), **single)
-    early = lambda r: pl.BlockSpec((r, TILE), lambda i: (0, jnp.minimum(i, tiles - 1)))
+    early = lambda r: pl.BlockSpec((r, WIDE), lambda i: (0, jnp.minimum(i, tiles - 1)))
     given = [
         ((8, count), BF16), ((8, 128), F32), ((24, 128), F32), ((32, 128), F32), ((C1, C2), BF16), ((2 * C2, C3), BF16),
     ]
@@ -688,7 +694,7 @@
             ((tokens, C2), BF16), ((8, C3), F32), ((8, C1), F32), ((8, C1), BF16), ((C1 + 16, C3), F32),
         )
     ]
-    outs += [(pl.BlockSpec((TILE, C3), lambda i: (jnp.maximum(i - tiles, 0), 0)), (count, C3), BF16)]
+    outs += [(pl.BlockSpec((WIDE, C3), lambda i: (jnp.maximum(i - tiles, 0), 0)), (count, C3), BF16)]
     outs += [(full(tokens, C3), (tokens, C3), BF16)] * 3
     scratch = [
         pltpu.VMEM((C1, count), BF16), pltpu.VMEM((tokens, C3), F32), pltpu.VMEM((tokens, C3), F32),
@@ -771,10 +777,10 @@
 
     tiles = pa_ref.shape[0] // PAIR
     for s in range(tiles):
-        first = 2 * s
-        visible = (row_cloud == col // PATCHES) & (
-            lax.rem(col, PATCHES) < jnp.where(col < PATCHES, len_ref[first], len_ref[first + 1])
-        )
+        seen = jnp.zeros((1, PAIR), jnp.int32)
+        for c in range(PAIR // PATCHES):
+            seen = jnp.where(col[0:1, :] // PATCHES == c, len_ref[s * (PAIR // PATCHES) + c], seen)
+        visible = (row_cloud == col // PATCHES) & (lax.rem(col, PATCHES) < seen)
         rows = slice(PAIR * s, PAIR * s + PAIR)
         for p in range(HEADS // 2):
             at = 128 * p
@@ -794,8 +800,7 @@
     x_one = x_zero + mm(mixed_low, wo_ref[...]) + bo
     unit_b, inv_b, normed_b = layer_norm(x_one, ln2_gain, ln2_shift)
     hidden, d_hidden = gelu_pair(mm(normed_b, wf1_ref[...]) + bf1)
-    dhid_s[...] = low(d_hidden)
-    hidden = low(hidden)
+    dhid_s[...] = d_hidden
     out_o[...] = x_one + mm(hidden, wf2_ref[...]) + bf2
 
     cot = cot_ref[...]
@@ -873,13 +878,13 @@
     base_o[...] = mm_tn(sums, pooled)
 
 
-def last_tile(gp_ref, ext_ref, gp1_ref, rel, tok, kap, k_s, xe_s, wb_ref, wd_ref, h_o, q_o, d_at):
-    dn = (gp_ref[...].reshape(TOK, GROUP, C3) * tok[:, None, :]).reshape(TILE, C3)
-    xe_s[0:C1, :] = ext_ref[0:C1, :]
+def last_tile(gp, ext, gp1, rel, tok, kap, k_s, xe_s, wb_ref, wd_ref, h_o, q_o, d_at):
+    dn = (gp.reshape(TOK, GROUP, C3) * tok[:, None, :]).reshape(TILE, C3)
+    xe_s[0:C1, :] = ext[0:C1, :]
     k_s[:, C1 : C1 + TOK] = kap.T
-    h_o[...] += mm(ext_ref[...], dn)
+    h_o[...] += mm(ext, dn)
     d_act = mm_nt(wb_ref[...], dn) + mm(k_s[...], xe_s[...])
-    d_one = low(d_act * gp1_ref[...].astype(F32))
+    d_one = low(d_act * gp1.astype(F32))
     d_at(mm(wd_ref[...], d_one))
     q_o[...] += mm_nt(rel, d_one)
 
@@ -1040,6 +1045,7 @@
     small_s, tok_s, tg_s, acc3, qkv_s, mixed_s, soft_s, dmix_s, dqkv_s, dhid_s = take(10)
     tot_s, kap_s, k_s, wb_s, top_s, corr_s, base_s, h_s, q_s, d_s, xe_s, spread_s, sums_s = take(13)
     acc, slots, ssend, srecv, unused, slots3, ssend3, srecv3 = take(8)
+    gp_r, ext_r, gp1_r, read_sem = take(4)
     step = pl.program_id(0)
     steps = pl.num_programs(0)
     peers = all_peers(dp)
@@ -1092,9 +1098,19 @@
         ffn.advance(2)
         att.advance(1)
 
+    def reads(tile, slot):
+        at = pl.ds(pl.multiple_of(tile * TILE, TILE), TILE)
+        pairs = ((gp_ref.at[at, :], gp_r), (ext_ref.at[:, at], ext_r), (gp1_ref.at[:, at], gp1_r))
+        return [
+            pltpu.make_async_copy(src, ring.at[slot], read_sem.at[slot, k]) for k, (src, ring) in enumerate(pairs)
+        ]
+
     @pl.when(step == 0)
     def _():
         greet(peers)
+        for tile in range(AHEAD):
+            for copy in reads(tile, tile):
+                copy.start()
         block_step(
             pa_ref, pg_ref, pc_ref, ps_ref, len_ref, cot_ref, psmall_ref, bsmall_ref, sv_ref,
             w4_ref, wqkv_ref, wo_ref, wf1_ref, wf2_ref,
@@ -1119,19 +1135,26 @@
         tile = step - 1
         at = pl.ds(pl.multiple_of(tile * TILE, TILE), TILE)
         ts = pl.ds(pl.multiple_of(tile * TOK, TOK), TOK)
+        slot = lax.rem(tile, AHEAD)
 
         def put(d):
             d_s[:, at] = d
 
+        for copy in reads(tile, slot):
+            copy.wait()
         last_tile(
-            gp_ref, ext_ref, gp1_ref, rel_ref[:, at], low(tok_s[ts, :] * 0.5), kap_s[ts, :], k_s, xe_s, wb_s, wd_ref,
-            h_s, q_s, put,
+            gp_r[slot], ext_r[slot], gp1_r[slot], rel_ref[:, at], low(tok_s[ts, :] * 0.5), kap_s[ts, :],
+            k_s, xe_s, wb_s, wd_ref, h_s, q_s, put,
         )
+
+        @pl.when(tile + AHEAD < steps - 1)
+        def _():
+            for copy in reads(tile + AHEAD, slot):
+                copy.start()
 
     @pl.when(step == steps - 1)
     def _():
         acc[...] = q_s[...]
-        copies = sum_start(dp, acc, slots, ssend, srecv)
         b2 = as_vector(psmall_ref, 5, 2)
         w2e = jnp.concatenate([w2_ref[...], low(jnp.concatenate([b2, jnp.zeros((15, C2), F32)], axis=0))], axis=0)
         gw3, gw2 = last_weights(h_s[...], sv_ref[0:1, :], corr_s[...], base_s[...], w2e, w3_ref)
@@ -1151,6 +1174,8 @@
                 cz, cy, cx, cc = place(d)
                 point0[cc, cz, cy, cx] = low(pstage[...])
             point.advance(0)
+        copies = sum_start(dp, acc, slots, ssend, srecv)
+        if known:
             point.advance(1)
         totals = sum_finish(acc, slots, copies)
         grad_w, gain1, shift1, flat, slope = first_grads(totals, moment_ref[...], psmall_ref[...], stats_ref[...])
@@ -1187,10 +1212,9 @@
     tokens, tiles = count // GROUP, count // TILE
     single = dict(pipeline_mode=pl.Buffered(1))
     full = lambda *s: pl.BlockSpec(s, lambda i: (0, 0), **single)
-    cols = lambda r: pl.BlockSpec((r, TILE), lambda i: (0, jnp.maximum(i - 1, 0)))
     specs = [full(*a.shape) for a in args[:26]]
     specs[4] = pl.BlockSpec(memory_space=pltpu.SMEM)
-    specs += [pl.BlockSpec((TILE, C3), lambda i: (jnp.maximum(i - 1, 0), 0)), cols(C1 + 16), cols(C1)]
+    specs += [pl.BlockSpec(memory_space=pl.ANY)] * 3
     outs = [((tokens, D), F32), ((3, count), F32)]
     if known:
         outs += [((PROWS, 128), F32), ((BROWS, 128), F32)]
@@ -1210,6 +1234,10 @@
         pltpu.VMEM((pieces, 256), F32), pltpu.VMEM((8 * pieces, 256), F32),
     ]
     scratch += sum_scratch(dp) + sum_scratch(dp)
+    scratch += [
+        pltpu.VMEM((AHEAD, TILE, C3), BF16), pltpu.VMEM((AHEAD, C1 + 16, TILE), BF16), pltpu.VMEM((AHEAD, C1, TILE), BF16),
+        pltpu.SemaphoreType.DMA((AHEAD, 3)),
+    ]
     if known:
         scratch += scatter_scratch(FFN_WIDTH) + scatter_scratch(ATT_WIDTH) + scatter_scratch(POINT_WIDTH)
         scratch += [

time: 157 us -> 144 us (0.917)
  Pallas kernels: 142 us -> 129 us
    pallas_call x1, Pallas kernels: 73.7 us -> 64.1 us  [backward_call(): pl.pallas_call(functools.partial(backward_kernel, known, dp), grid=(1 + t...]
    pallas_call x1, Pallas kernels: 68.7 us -> 64.9 us  [forward_call(): pl.pallas_call(functools.partial(forward_kernel, known, dp), grid=(2 * ti...]
where the time goes in v6:
time: 144 us; the launch traced here: 143 us
  Pallas kernels  129 us (90%)
  local copies, waits for them, and re-layouts  9.66 us (7%)
  other arithmetic  3.6 us (2%)
    pallas_call x1, Pallas kernels, forward_call(): pl.pallas_call(functools.partial(forward_kernel, known, dp), grid=(2 * ti...  64.9 us
    pallas_call x1, Pallas kernels, backward_call(): pl.pallas_call(functools.partial(backward_kernel, known, dp), grid=(1 + t...  64.1 us
    unnamed x17, local copies, waits for them, and re-layouts  3.81 us
    reshape x2, local copies, waits for them, and re-layouts, flat_of(): return jnp.pad(vector, (0, rows * 128 - vector.shape[0])).reshape(rows, 128)  3.14 us

profile of v6, /device:TPU:0, one launch (start us, length us, event | category | flops | bytes accessed | tf_op | source)
XLA Modules:
  0.0 143.1 jit_solution(532233749239657291)
XLA Ops:
  0.6 0.8 concatenate.8
  1.4 0.8 concatenate.9
  2.2 0.0 copy-start.1
  2.2 1.7 %pad_bitcast_fusion.refs_3_ = f32[440,128]{1,0:T(8,128)} fusion(f32[55416]{0:T(1024)} %param.17), kind=kLoop, calls=%fused_computation.47 | loop fusion | bytes 446944 | tf_op jit(solution)/shard_map/reshape | solution.py:1330
  3.9 1.5 %pad_bitcast_fusion.1.refs_2_ = f32[128,128]{1,0:T(8,128)} fusion(f32[15432]{0:T(1024)} %param.16), kind=kLoop, calls=%fused_computation.109 | loop fusion | bytes 127264 | tf_op jit(solution)/shard_map/reshape | solution.py:1330
  5.4 0.0 copy-done.1
  5.4 64.9 %forward.1 = (bf16[8,16384]{1,0:T(8,128)(2,1)}, f32[8,128]{1,0:T(8,128)}, f32[24,128]{1,0:T(8,128)}, f32[32,128]{1,0:T(8,128)}, bf16[128,256]{1,0:T(8,128)(2,1)}...) custom-call(f32[3,16384]{1,0:T(4,128)} %refs_0_.1, ...), custom_call_target="tpu_custom_call" | custom-call | tf_op jit(solution)/shard_map/forward/pallas_call | solution.py:719
  70.3 0.0 copy-start
  70.3 0.0 copy-start.3
  70.3 0.0 copy-start.4
  70.3 0.0 copy-start.2
  70.3 0.0 copy-start.5
  70.3 0.0 copy-start.6
  70.4 64.1 %backward.1 = (f32[512,384]{1,0:T(8,128)}, f32[3,16384]{1,0:T(4,128)}, f32[128,128]{1,0:T(8,128)}, f32[440,128]{1,0:T(8,128)}) custom-call(bf16[512,512]{1,0:T(8,128)(2,1)} %get-tuple-element.41.refs_0_, bf16[512,512]{1,0:T(8,128)(2,1)} %get-tuple-element.42.refs_1_, bf16[512,512]{1,0:T(8,128)(2,1)} %get-tuple-element.43.refs_2_, ...), custom_call_target="tpu_custom_call" | custom-call | tf_op jit(solution)/shard_map/backward/pallas_call | solution.py:1249
  134.5 0.0 copy-done
  134.5 0.0 copy-done.3
  134.5 0.0 copy-done.4
  134.5 2.0 %fusion.93 = (bf16[55416]{0:T(1024)(128)(2,1)}, f32[55416]{0:T(1024)}, f32[55416]{0:T(1024)}, f32[55416]{0:T(1024)}) fusion(f32[55416]{0:T(1024)S(1)} %copy-done, s32[]{:T(128)S(6)} %mul.113, s32[]{:T(128)S(6)} %sub.34, s32[]{:T(128)S(6)} %sub.33, s32[]{:T(128)S(6)} %sub.32, s32[]{:T(128)S(6)} %sub.31, f32[56320]{0:T(1024)} %bitcast.6, ...), kind=kLoop, calls=%fused_computation.128 | loop fusion | flops 5153688 | bytes 1662500 | tf_op jit(solution)/shard_map/convert_element_type | solution.py:1377
  136.5 0.0 copy-done.2
  136.5 0.0 copy-done.5
  136.5 0.0 copy-done.6
  136.5 1.6 %fusion.95 = (bf16[15432]{0:T(1024)(128)(2,1)}, f32[15432]{0:T(1024)}, f32[15432]{0:T(1024)}, f32[15432]{0:T(1024)}) fusion(f32[15432]{0:T(1024)S(1)} %copy-done.2, s32[]{:T(128)S(6)} %mul.98, s32[]{:T(128)S(6)} %sub.29, s32[]{:T(128)S(6)} %sub.28, s32[]{:T(128)S(6)} %sub.27, f32[16384]{0:T(1024)} %bitcast.8, f32[15432]{0:T(1024)S(1)} %copy-done.5, ...), kind=kLoop, calls=%fused_computation.129 | loop fusion | flops 1388880 | bytes 462976 | tf_op jit(solution)/shard_map/convert_element_type | solution.py:1377
  138.1 1.2 slice.15
  139.3 2.1 %copy.29 = f32[512,384]{1,0:T(8,128)} copy(f32[512,384]{1,0:T(8,128)} %get-tuple-element.90) | data formatting | bytes 1572864
  141.4 1.7 %copy.30 = f32[3,16384]{1,0:T(4,128)} copy(f32[3,16384]{1,0:T(4,128)} %get-tuple-element.91) | data formatting | bytes 393216
  (2 shorter events, 0.0 us)
Async XLA Ops:
  2.2 3.2 %copy-start.1 = (s32[128,8]{1,0:T(8,128)}, s32[128,8]{1,0:T(8,128)S(1)}, u32[]{:S(2)}) copy-start(s32[128,8]{1,0:T(8,128)S(1)} %constant_dynamic-update-slice_fusion.refs_1_.refs_25_) | copy-start | bytes 12292
  70.3 64.2 %copy-start = (f32[55416]{0:T(1024)S(1)}, f32[55416]{0:T(1024)}, u32[]{:S(2)}) copy-start(f32[55416]{0:T(1024)} %param.17) | copy-start | bytes 664996
  70.3 64.2 %copy-start.3 = (f32[55416]{0:T(1024)S(1)}, f32[55416]{0:T(1024)}, u32[]{:S(2)}) copy-start(f32[55416]{0:T(1024)} %param.19) | copy-start | bytes 664996
  70.3 64.2 %copy-start.4 = (f32[55416]{0:T(1024)S(1)}, f32[55416]{0:T(1024)}, u32[]{:S(2)}) copy-start(f32[55416]{0:T(1024)} %param.21) | copy-start | bytes 664996
  70.3 66.2 %copy-start.2 = (f32[15432]{0:T(1024)S(1)}, f32[15432]{0:T(1024)}, u32[]{:S(2)}) copy-start(f32[15432]{0:T(1024)} %param.16) | copy-start | bytes 185188
  70.3 66.2 %copy-start.5 = (f32[15432]{0:T(1024)S(1)}, f32[15432]{0:T(1024)}, u32[]{:S(2)}) copy-start(f32[15432]{0:T(1024)} %param.18) | copy-start | bytes 185188
  70.3 66.2 %copy-start.6 = (f32[15432]{0:T(1024)S(1)}, f32[15432]{0:T(1024)}, u32[]{:S(2)}) copy-start(f32[15432]{0:T(1024)} %param.20) | copy-start | bytes 185188

commit v7 on v6

--- a/solution.py
+++ b/solution.py
@@ -271,15 +271,20 @@
 
 
 def spread_tokens(values):
-    t = lax.broadcasted_iota(jnp.int32, (8, 256), 0)
-    p = lax.broadcasted_iota(jnp.int32, (8, 256), 1) // GROUP
-    return mm(low(values.astype(F32)), low((t == p).astype(F32)))
-
-
-def geometry(points_ref, tokens_ref, rel_ref, counts_s, picked_s):
+    tokens = values.shape[1]
+    piece = lax.broadcasted_iota(jnp.int32, (tokens // 8, tokens), 0)
+    token = lax.broadcasted_iota(jnp.int32, (tokens // 8, tokens), 1)
+    apart = jnp.where(piece == token // 8, values.astype(F32), 0.0)
+    token = lax.rem(lax.broadcasted_iota(jnp.int32, (tokens, 256), 0), 8)
+    patch = lax.broadcasted_iota(jnp.int32, (tokens, 256), 1) // GROUP
+    return mm(low(apart), low((token == patch).astype(F32)))
+
+
+def geometry(points_ref, counts_ref, centres_ref, rel_ref, counts_s, picked_s):
     pieces = points_ref.shape[1] // 256
     lane = lax.rem(lax.broadcasted_iota(jnp.int32, (1, 256), 1), GROUP).astype(F32)
-    counts_s[...] = spread_tokens(tokens_ref[...])
+    counts_s[0:pieces, :] = spread_tokens(counts_ref[...])
+    counts_s[pieces:, :] = spread_tokens(centres_ref[...])
     for i in range(pieces):
         at = slice(256 * i, 256 * i + 256)
         pick = (lane == counts_s[pieces + i : pieces + i + 1, :]).astype(F32)
@@ -526,7 +531,7 @@
 def forward_kernel(known, dp, *refs):
     refs = list(refs)
     take = lambda count: [refs.pop(0) for _ in range(count)]
-    points_ref, tokens_ref, pflat, bflat = take(4) if known else [None] * 4
+    points_ref, counts_ref, centres_ref, pflat, bflat = take(5) if known else [None] * 5
     rel_o, moment_o, psmall_o, bsmall_o, w2_o, w3_o = take(6)
     w4_o, wqkv_o, wo_o, wf1_o, wf2_o = take(5) if known else [None] * 5
     ext_o, gp1_o, g_o, ps_o, gm_o, fw_o, pooled_o, sv_o, stats_o, wd_o, w23_o, gp_o, pa_o, pg_o, pc_o = take(15)
@@ -552,7 +557,7 @@
         if known:
             pal[...] = segments_apart(pflat[...], PSMALL)
             bal[...] = segments_apart(bflat[...], BSMALL)
-            moments = geometry(points_ref, tokens_ref, rel_o, counts_s, picked_s)[0:4, :]
+            moments = geometry(points_ref, counts_ref, centres_ref, rel_o, counts_s, picked_s)[0:4, :]
             moments = jnp.concatenate([moments, jnp.zeros((4, 120), F32)], axis=1)
             hi, mid, lo = [part.astype(F32) for part in split_three(moments)]
             packed = hi + pltpu.roll(mid, 8, 1) + pltpu.roll(lo, 16, 1)
@@ -569,9 +574,9 @@
             gather_att.advance(0)
             ffn_rows(bal, stage)
             ffn[z, y, x, core] = low(stage[...])
+            gather_w3.advance(1)
             for copy in copies:
                 copy.wait()
-            gather_w3.advance(1)
             gather_att.advance(1)
             gather_ffn.advance(0)
             psmall, bsmall = [], []
@@ -601,8 +606,8 @@
 
     if known:
         for at_step, gather, number in (
-            (1, gather_w3, 2), (1, gather_att, 2), (2, gather_w3, 3), (2, gather_ffn, 1), (3, gather_att, 3),
-            (4, gather_w3, 4), (4, gather_ffn, 2), (5, gather_att, 4), (5, gather_ffn, 3),
+            (1, gather_w3, 2), (2, gather_w3, 3), (2, gather_att, 2), (3, gather_ffn, 1), (4, gather_w3, 4),
+            (5, gather_att, 3), (5, gather_ffn, 2), (6, gather_att, 4), (7, gather_ffn, 3),
         ):
             pl.when(step == at_step)(functools.partial(gather.advance, number))
 
@@ -652,7 +657,7 @@
 
     if known:
 
-        @pl.when(step == tiles + 1)
+        @pl.when(step == tiles + 2)
         def _():
             for d in range(dp * NC):
                 under = att[place(d)].astype(F32)
@@ -915,12 +920,12 @@
     return grad_w, two, one, flat, slope
 
 
-def point_gradient(d_ref, rel_ref, tokens_ref, flat, slope, out_ref, spread_s, sums_s):
+def point_gradient(d_ref, rel_ref, centres_ref, flat, slope, out_ref, spread_s, sums_s):
     pieces = d_ref.shape[1] // 256
     lane = lax.rem(lax.broadcasted_iota(jnp.int32, (1, 256), 1), GROUP).astype(F32)
     base = jnp.concatenate(flat, axis=0)
     columns = [jnp.concatenate([slope[k][j] for k in range(3)], axis=0) for j in range(3)]
-    spread_s[...] = spread_tokens(tokens_ref[pieces : 2 * pieces, :])
+    spread_s[...] = spread_tokens(centres_ref[...])
     for i in range(pieces):
         at = slice(256 * i, 256 * i + 256)
         rel = rel_ref[:, at].astype(F32)
@@ -1036,7 +1041,7 @@
     take = lambda count: [refs.pop(0) for _ in range(count)]
     pa_ref, pg_ref, pc_ref, ps_ref, len_ref, cot_ref, psmall_ref, bsmall_ref, sv_ref, stats_ref, moment_ref = take(11)
     w2_ref, w3_ref, w4_ref, wqkv_ref, wo_ref, wf1_ref, wf2_ref, w23_ref = take(8)
-    sc_ref, gm_ref, pooled_ref, gext_ref, wd_ref, rel_ref, tokens_ref, gp_ref, ext_ref, gp1_ref = take(10)
+    sc_ref, gm_ref, pooled_ref, gext_ref, wd_ref, rel_ref, centres_ref, gp_ref, ext_ref, gp1_ref = take(10)
     out_o, pg_o = take(2)
     if known:
         pflat_o, bflat_o = take(2)
@@ -1127,7 +1132,7 @@
         )
 
     if known:
-        for at_step, group, number in ((3, ffn, 3), (4, att, 2), (6, att, 3)):
+        for at_step, group, number in ((4, ffn, 3), (5, att, 2), (7, att, 3)):
             pl.when(step == at_step)(functools.partial(group.advance, number))
 
     @pl.when(step >= 1)
@@ -1187,7 +1192,7 @@
             stage[:, 0:ATT_WIDTH] = att.advance(4)
             attention_flat(stage, bal, pal)
             point.advance(3)
-        point_gradient(d_s, rel_ref, tokens_ref, flat, slope, pg_o, spread_s, sums_s)
+        point_gradient(d_s, rel_ref, centres_ref, flat, slope, pg_o, spread_s, sums_s)
         if not known:
             prow_o[0:18, :] = prow + full_rows * (1.0 / (dp * NC))
             brow_o[0:30, :] = brow
@@ -1258,27 +1263,26 @@
     )(*args)
 
 
-def geometry_kernel(points_ref, tokens_ref, rel_o, moment_o, counts_s, picked_s):
-    moment_o[...] = jnp.concatenate(
-        [geometry(points_ref, tokens_ref, rel_o, counts_s, picked_s), jnp.zeros((8, 120), F32)], axis=1
-    )
-
-
-def geometry_call(points, tokens):
+def geometry_kernel(points_ref, counts_ref, centres_ref, rel_o, moment_o, counts_s, picked_s):
+    moments = geometry(points_ref, counts_ref, centres_ref, rel_o, counts_s, picked_s)
+    moment_o[...] = jnp.concatenate([moments, jnp.zeros((8, 120), F32)], axis=1)
+
+
+def geometry_call(points, counts, centres):
     count = points.shape[1]
     return pl.pallas_call(
         geometry_kernel,
         out_shape=shaped(((8, count), BF16), ((8, 128), F32)),
-        in_specs=vmem(2),
+        in_specs=vmem(3),
         out_specs=vmem(2),
         scratch_shapes=[pltpu.VMEM((count // 128, 256), F32), pltpu.VMEM((count // 32, 256), F32)],
         compiler_params=params(),
         name="geometry",
-    )(points, tokens)
-
-
-def gather_plain(points, tokens, point_master, block_master, devices):
-    rel, moments = geometry_call(points, tokens)
+    )(points, counts, centres)
+
+
+def gather_plain(points, counts, centres, point_master, block_master, devices):
+    rel, moments = geometry_call(points, counts, centres)
     moments = lax.psum(moments, AXES)
     tables = []
     for master, layout in ((point_master, point_layout()), (block_master, block_layout())):
@@ -1339,20 +1343,20 @@
     own_rank = lax.axis_index(AXES)
     known = dp == NZ * NY * NX and fsdp == NC
     count = points.shape[1]
-    tokens = jnp.concatenate([point_count, centre_slot]).reshape(-1, 8)
+    counts, centres = point_count.reshape(1, -1), centre_slot.reshape(1, -1)
     if known:
         outs = forward_call(
-            True, dp, count, points, tokens, flat_of(point_master, PROWS), flat_of(block_master, BROWS)
+            True, dp, count, points, counts, centres, flat_of(point_master, PROWS), flat_of(block_master, BROWS)
         )
         given, block, outs = outs[:6], outs[6:11], outs[11:]
     else:
-        given, block = gather_plain(points, tokens, point_master, block_master, devices)
+        given, block = gather_plain(points, counts, centres, point_master, block_master, devices)
         outs = forward_call(False, dp, count, *given)
     rel, moments, psmall, bsmall, w2, w3 = given
     ext, gp1, gext, ps, gm, sc, pooled, sv, stats, wd, w23, gp, pa, pg, pc = outs
     outs = backward_call(
         known, dp, pa, pg, pc, ps, cloud_length, cotangent, psmall, bsmall, sv, stats, moments,
-        w2, w3, *block, w23, sc, gm, pooled, gext, wd, rel, tokens, gp, ext, gp1,
+        w2, w3, *block, w23, sc, gm, pooled, gext, wd, rel, centres, gp, ext, gp1,
     )
     tokens_out, point_grad = outs[:2]
     if known:

time: 144 us -> 136 us (0.944)
  Pallas kernels: 129 us -> 124 us
  local copies, waits for them, and re-layouts: 9.66 us -> 8.09 us
    pallas_call x1, Pallas kernels: 64.9 us -> 60.9 us  [forward_call(): pl.pallas_call(functools.partial(forward_kernel, known, dp), grid=(2 * ti...]
    concatenate x3 -> x0, local copies, waits for them, and re-layouts: 1.53 us -> none  [on_device(): tokens = jnp.concatenate([point_count, centre_slot]).reshape(-1, 8)]
    pallas_call x1, Pallas kernels: 64.1 us -> 62.6 us  [backward_call(): pl.pallas_call(functools.partial(backward_kernel, known, dp), grid=(1 + t...]
    unnamed x17 -> x14, local copies, waits for them, and re-layouts: 3.81 us -> 3.8 us
where the time goes in v7:
time: 136 us
  Pallas kernels  124 us (91%)
  local copies, waits for them, and re-layouts  8.09 us (6%)
  other arithmetic  3.6 us (3%)
    pallas_call x1, Pallas kernels, backward_call(): pl.pallas_call(functools.partial(backward_kernel, known, dp), grid=(1 + t...  62.6 us
    pallas_call x1, Pallas kernels, forward_call(): pl.pallas_call(functools.partial(forward_kernel, known, dp), grid=(2 * ti...  60.9 us
    unnamed x14, local copies, waits for them, and re-layouts  3.8 us
    reshape x2, local copies, waits for them, and re-layouts, flat_of(): return jnp.pad(vector, (0, rows * 128 - vector.shape[0])).reshape(rows, 128)  3.11 us

profile of v7, /device:TPU:0, one launch (start us, length us, event | category | flops | bytes accessed | tf_op | source)
XLA Modules:
  0.0 136.0 jit_solution(16535802033783325389)
XLA Ops:
  0.6 1.6 %pad_bitcast_fusion.refs_4_ = f32[440,128]{1,0:T(8,128)} fusion(f32[55416]{0:T(1024)} %param.17), kind=kLoop, calls=%fused_computation.47 | loop fusion | bytes 446944 | tf_op jit(solution)/shard_map/reshape | solution.py:1334
  2.3 1.5 %pad_bitcast_fusion.1.refs_3_ = f32[128,128]{1,0:T(8,128)} fusion(f32[15432]{0:T(1024)} %param.16), kind=kLoop, calls=%fused_computation.109 | loop fusion | bytes 127264 | tf_op jit(solution)/shard_map/reshape | solution.py:1334
  3.8 60.9 %forward.1 = (bf16[8,16384]{1,0:T(8,128)(2,1)}, f32[8,128]{1,0:T(8,128)}, f32[24,128]{1,0:T(8,128)}, f32[32,128]{1,0:T(8,128)}, bf16[128,256]{1,0:T(8,128)(2,1)}...) custom-call(f32[3,16384]{1,0:T(4,128)} %refs_0_.1, ...), custom_call_target="tpu_custom_call" | custom-call | tf_op jit(solution)/shard_map/forward/pallas_call | solution.py:724
  64.7 0.0 copy-start
  64.7 0.0 copy-start.2
  64.7 0.0 copy-start.3
  64.7 0.0 copy-start.1
  64.7 0.0 copy-start.4
  64.8 0.0 copy-start.5
  64.8 62.6 %backward.1 = (f32[512,384]{1,0:T(8,128)}, f32[3,16384]{1,0:T(4,128)}, f32[128,128]{1,0:T(8,128)}, f32[440,128]{1,0:T(8,128)}) custom-call(bf16[512,512]{1,0:T(8,128)(2,1)} %get-tuple-element.41.refs_0_, bf16[512,512]{1,0:T(8,128)(2,1)} %get-tuple-element.42.refs_1_, bf16[512,512]{1,0:T(8,128)(2,1)} %get-tuple-element.43.refs_2_, ...), custom_call_target="tpu_custom_call" | custom-call | tf_op jit(solution)/shard_map/backward/pallas_call | solution.py:1254
  127.4 0.0 copy-done
  127.4 0.0 copy-done.2
  127.4 0.0 copy-done.3
  127.4 2.0 %fusion.93 = (bf16[55416]{0:T(1024)(128)(2,1)}, f32[55416]{0:T(1024)}, f32[55416]{0:T(1024)}, f32[55416]{0:T(1024)}) fusion(f32[55416]{0:T(1024)S(1)} %copy-done, s32[]{:T(128)S(6)} %mul.113, s32[]{:T(128)S(6)} %sub.34, s32[]{:T(128)S(6)} %sub.33, s32[]{:T(128)S(6)} %sub.32, s32[]{:T(128)S(6)} %sub.31, f32[56320]{0:T(1024)} %bitcast.8, ...), kind=kLoop, calls=%fused_computation.126 | loop fusion | flops 5153688 | bytes 1662500 | tf_op jit(solution)/shard_map/convert_element_type | solution.py:1381
  129.4 0.0 copy-done.1
  129.4 0.0 copy-done.4
  129.4 0.0 copy-done.5
  129.4 1.6 %fusion.95 = (bf16[15432]{0:T(1024)(128)(2,1)}, f32[15432]{0:T(1024)}, f32[15432]{0:T(1024)}, f32[15432]{0:T(1024)}) fusion(f32[15432]{0:T(1024)S(1)} %copy-done.1, s32[]{:T(128)S(6)} %mul.98, s32[]{:T(128)S(6)} %sub.29, s32[]{:T(128)S(6)} %sub.28, s32[]{:T(128)S(6)} %sub.27, f32[16384]{0:T(1024)} %bitcast.10, f32[15432]{0:T(1024)S(1)} %copy-done.4, ...), kind=kLoop, calls=%fused_computation.127 | loop fusion | flops 1388880 | bytes 462976 | tf_op jit(solution)/shard_map/convert_element_type | solution.py:1381
  131.0 1.2 slice.15
  132.2 2.1 %copy.24 = f32[512,384]{1,0:T(8,128)} copy(f32[512,384]{1,0:T(8,128)} %get-tuple-element.90) | data formatting | bytes 1572864
  134.3 1.7 %copy.25 = f32[3,16384]{1,0:T(4,128)} copy(f32[3,16384]{1,0:T(4,128)} %get-tuple-element.91) | data formatting | bytes 393216
Async XLA Ops:
  64.7 62.7 %copy-start = (f32[55416]{0:T(1024)S(1)}, f32[55416]{0:T(1024)}, u32[]{:S(2)}) copy-start(f32[55416]{0:T(1024)} %param.17) | copy-start | bytes 664996
  64.7 62.7 %copy-start.2 = (f32[55416]{0:T(1024)S(1)}, f32[55416]{0:T(1024)}, u32[]{:S(2)}) copy-start(f32[55416]{0:T(1024)} %param.19) | copy-start | bytes 664996
  64.7 62.7 %copy-start.3 = (f32[55416]{0:T(1024)S(1)}, f32[55416]{0:T(1024)}, u32[]{:S(2)}) copy-start(f32[55416]{0:T(1024)} %param.21) | copy-start | bytes 664996
  64.7 64.7 %copy-start.1 = (f32[15432]{0:T(1024)S(1)}, f32[15432]{0:T(1024)}, u32[]{:S(2)}) copy-start(f32[15432]{0:T(1024)} %param.16) | copy-start | bytes 185188
  64.7 64.7 %copy-start.4 = (f32[15432]{0:T(1024)S(1)}, f32[15432]{0:T(1024)}, u32[]{:S(2)}) copy-start(f32[15432]{0:T(1024)} %param.18) | copy-start | bytes 185188
  64.8 64.7 %copy-start.5 = (f32[15432]{0:T(1024)S(1)}, f32[15432]{0:T(1024)}, u32[]{:S(2)}) copy-start(f32[15432]{0:T(1024)} %param.20) | copy-start | bytes 185188

commit v8 on v7

--- a/solution.py
+++ b/solution.py
@@ -555,13 +555,21 @@
         g_o[...] = jnp.zeros_like(g_o)
         e_s[...] = token_ones()
         if known:
-            pal[...] = segments_apart(pflat[...], PSMALL)
-            bal[...] = segments_apart(bflat[...], BSMALL)
+            for vector, rows, small in ((pflat, pal, PSMALL), (bflat, bal, BSMALL)):
+                rows[...] = jnp.zeros_like(rows)
+                length = vector.shape[0]
+                for k in range(-(-length // 128)):
+                    width = min(128, length - 128 * k)
+                    rows[k, 0:width] = vector[128 * k : 128 * k + width]
+                first = rows[0:1, :]
+                rows[...] = segments_apart(rows[...], small)
+                rows[0:1, :] = first
             moments = geometry(points_ref, counts_ref, centres_ref, rel_o, counts_s, picked_s)[0:4, :]
             moments = jnp.concatenate([moments, jnp.zeros((4, 120), F32)], axis=1)
             hi, mid, lo = [part.astype(F32) for part in split_three(moments)]
             packed = hi + pltpu.roll(mid, 8, 1) + pltpu.roll(lo, 16, 1)
-            rows = [pal[1:9, :], pflat[0:1, :], bflat[0:1, :], packed, jnp.zeros((2, 128), F32)]
+            firsts = [pal[0:1, :], bal[0:1, :]]
+            rows = [pal[1:9, :], *firsts, packed, jnp.zeros((2, 128), F32)]
             own = tiny.at[me()]
             own[...] = low(jnp.concatenate(rows, axis=0))
             greeted(peers)
@@ -724,7 +732,7 @@
     return pl.pallas_call(
         functools.partial(forward_kernel, known, dp),
         grid=(2 * tiles,),
-        in_specs=[full(*a.shape) for a in args],
+        in_specs=[full(*a.shape) if a.ndim == 2 else pl.BlockSpec(memory_space=pltpu.VMEM) for a in args],
         out_specs=[o[0] for o in outs],
         out_shape=shaped(*[o[1:] for o in outs]),
         scratch_shapes=scratch,
@@ -1330,10 +1338,6 @@
     return (master_new, one_new, two_new)
 
 
-def flat_of(vector, rows):
-    return jnp.pad(vector, (0, rows * 128 - vector.shape[0])).reshape(rows, 128)
-
-
 def on_device(
     points, point_count, centre_slot, cloud_length, cotangent, point_master, block_master,
     point_first, block_first, point_second, block_second,
@@ -1346,7 +1350,7 @@
     counts, centres = point_count.reshape(1, -1), centre_slot.reshape(1, -1)
     if known:
         outs = forward_call(
-            True, dp, count, points, counts, centres, flat_of(point_master, PROWS), flat_of(block_master, BROWS)
+            True, dp, count, points, counts, centres, point_master, block_master
         )
         given, block, outs = outs[:6], outs[6:11], outs[11:]
     else:

time: 136 us -> 133 us (0.978)
  local copies, waits for them, and re-layouts: 8.09 us -> 4.98 us
    reshape x2 -> x0, local copies, waits for them, and re-layouts: 3.11 us -> none  [flat_of(): return jnp.pad(vector, (0, rows * 128 - vector.shape[0])).reshape(rows, 128)]
where the time goes in v8:
time: 133 us
  Pallas kernels  124 us (93%)
  local copies, waits for them, and re-layouts  4.98 us (4%)
  other arithmetic  3.6 us (3%)
    pallas_call x1, Pallas kernels, backward_call(): pl.pallas_call(functools.partial(backward_kernel, known, dp), grid=(1 + t...  62.6 us
    pallas_call x1, Pallas kernels, forward_call(): pl.pallas_call(functools.partial(forward_kernel, known, dp), grid=(2 * ti...  60.9 us
    unnamed x14, local copies, waits for them, and re-layouts  3.8 us

profile of v8, /device:TPU:0, one launch (start us, length us, event | category | flops | bytes accessed | tf_op | source)
XLA Modules:
  0.0 132.8 jit_solution(2095908109961193050)
XLA Ops:
  0.6 60.9 %forward.1 = (bf16[8,16384]{1,0:T(8,128)(2,1)}, f32[8,128]{1,0:T(8,128)}, f32[24,128]{1,0:T(8,128)}, f32[32,128]{1,0:T(8,128)}, bf16[128,256]{1,0:T(8,128)(2,1)}...) custom-call(f32[3,16384]{1,0:T(4,128)} %refs_0_.1, ...), custom_call_target="tpu_custom_call" | custom-call | tf_op jit(solution)/shard_map/forward/pallas_call | solution.py:732
  61.6 0.0 copy-start
  61.6 0.0 copy-start.2
  61.6 0.0 copy-start.3
  61.6 0.0 copy-start.1
  61.6 0.0 copy-start.4
  61.6 0.0 copy-start.5
  61.6 62.6 %backward.1 = (f32[512,384]{1,0:T(8,128)}, f32[3,16384]{1,0:T(4,128)}, f32[128,128]{1,0:T(8,128)}, f32[440,128]{1,0:T(8,128)}) custom-call(bf16[512,512]{1,0:T(8,128)(2,1)} %get-tuple-element.41.refs_0_, bf16[512,512]{1,0:T(8,128)(2,1)} %get-tuple-element.42.refs_1_, bf16[512,512]{1,0:T(8,128)(2,1)} %get-tuple-element.43.refs_2_, ...), custom_call_target="tpu_custom_call" | custom-call | tf_op jit(solution)/shard_map/backward/pallas_call | solution.py:1262
  124.2 0.0 copy-done
  124.3 0.0 copy-done.2
  124.3 0.0 copy-done.3
  124.3 2.0 %fusion.93 = (bf16[55416]{0:T(1024)(128)(2,1)}, f32[55416]{0:T(1024)}, f32[55416]{0:T(1024)}, f32[55416]{0:T(1024)}) fusion(f32[55416]{0:T(1024)S(1)} %copy-done, s32[]{:T(128)S(6)} %mul.113, s32[]{:T(128)S(6)} %sub.34, s32[]{:T(128)S(6)} %sub.33, s32[]{:T(128)S(6)} %sub.32, s32[]{:T(128)S(6)} %sub.31, f32[56320]{0:T(1024)} %bitcast.4, ...), kind=kLoop, calls=%fused_computation.124 | loop fusion | flops 5153688 | bytes 1662500 | tf_op jit(solution)/shard_map/convert_element_type | solution.py:1385
  126.3 0.0 copy-done.1
  126.3 0.0 copy-done.4
  126.3 0.0 copy-done.5
  126.3 1.6 %fusion.95 = (bf16[15432]{0:T(1024)(128)(2,1)}, f32[15432]{0:T(1024)}, f32[15432]{0:T(1024)}, f32[15432]{0:T(1024)}) fusion(f32[15432]{0:T(1024)S(1)} %copy-done.1, s32[]{:T(128)S(6)} %mul.98, s32[]{:T(128)S(6)} %sub.29, s32[]{:T(128)S(6)} %sub.28, s32[]{:T(128)S(6)} %sub.27, f32[16384]{0:T(1024)} %bitcast.6, f32[15432]{0:T(1024)S(1)} %copy-done.4, ...), kind=kLoop, calls=%fused_computation.125 | loop fusion | flops 1388880 | bytes 462976 | tf_op jit(solution)/shard_map/convert_element_type | solution.py:1385
  127.9 1.2 slice.15
  129.1 2.1 %copy.24 = f32[512,384]{1,0:T(8,128)} copy(f32[512,384]{1,0:T(8,128)} %get-tuple-element.90) | data formatting | bytes 1572864
  131.1 1.7 %copy.25 = f32[3,16384]{1,0:T(4,128)} copy(f32[3,16384]{1,0:T(4,128)} %get-tuple-element.91) | data formatting | bytes 393216
Async XLA Ops:
  61.6 62.7 %copy-start = (f32[55416]{0:T(1024)S(1)}, f32[55416]{0:T(1024)}, u32[]{:S(2)}) copy-start(f32[55416]{0:T(1024)} %refs_4_.2) | copy-start | bytes 664996
  61.6 62.7 %copy-start.2 = (f32[55416]{0:T(1024)S(1)}, f32[55416]{0:T(1024)}, u32[]{:S(2)}) copy-start(f32[55416]{0:T(1024)} %param.19) | copy-start | bytes 664996
  61.6 62.7 %copy-start.3 = (f32[55416]{0:T(1024)S(1)}, f32[55416]{0:T(1024)}, u32[]{:S(2)}) copy-start(f32[55416]{0:T(1024)} %param.21) | copy-start | bytes 664996
  61.6 64.7 %copy-start.1 = (f32[15432]{0:T(1024)S(1)}, f32[15432]{0:T(1024)}, u32[]{:S(2)}) copy-start(f32[15432]{0:T(1024)} %refs_3_.1) | copy-start | bytes 185188
  61.6 64.7 %copy-start.4 = (f32[15432]{0:T(1024)S(1)}, f32[15432]{0:T(1024)}, u32[]{:S(2)}) copy-start(f32[15432]{0:T(1024)} %param.18) | copy-start | bytes 185188
  61.6 64.7 %copy-start.5 = (f32[15432]{0:T(1024)S(1)}, f32[15432]{0:T(1024)}, u32[]{:S(2)}) copy-start(f32[15432]{0:T(1024)} %param.20) | copy-start | bytes 185188
